TPU v7x, 32 devices: a whole 2x2x4 slice. The times are simulated.
32 devices in a mesh: groups: 2 (over y), attn: 4 (over z), ffn: 4 (over x, core).
Axes of the slice: x: 2, y: 2, z: 4, core: 2. Of those that a mesh axis runs over, the one named last changes fastest.
Arguments:
- query: bfloat16 [128, 16384], P(('groups', 'attn', 'ffn')), parts along dimension 0, may hold values from -64.7 to 64.7
- cache: bfloat16 [128, 1024, 512], P(('groups', 'attn', 'ffn')), parts along dimension 0, may hold values from -4.04 to 4.04
- lengths: int32 [128], P(('groups', 'attn', 'ffn')), parts along dimension 0, may hold values from 2 to 1024, as said below
- resid: bfloat16 [128, 7168], P(('groups', 'attn'), 'ffn'), parts along dimension 0, may hold values from -3 to 3
- out_weight: bfloat16 [16384, 7168], P('attn', 'ffn'), may hold values from -0.1875 to 0.1875
- norm_gain: float32 [7168], P('ffn'), may hold values from 0.1 to 1.9
- w_gate: bfloat16 [7168, 18432], P('ffn', 'attn'), may hold values from -0.0625 to 0.0625
- w_up: bfloat16 [7168, 18432], P('ffn', 'attn'), may hold values from -0.0625 to 0.0625
- w_down: bfloat16 [18432, 7168], P('attn', 'ffn'), may hold values from -0.046875 to 0.046875
Outputs:
- mixed: bfloat16 [128, 7168], P(('groups', 'attn'), 'ffn'), parts along dimension 0
There are 2 independent parts, one for each index of `groups`. A program takes and returns all parts, laid end to end along the dimension named above; an argument that names none is the same for every part. Nothing has to cross between parts.
Inputs may be any that keep to these rules, and one draw needn't show every extreme that they name: `lengths`: one request has all 1024 positions in use.
All inputs are finite; a program needn't handle non-finite values.
Results may differ from a plain program's by a relative error of at most 0.0062.
Values may be sent and summed in bfloat16 or wider, within the bound.
No kernel may reach another device: no remote copies, remote signals or barrier semaphores. Data moves between devices by JAX's collectives and lax.ppermute only.
A program may use at most 192 MiB of HBM per device.

v0:
```python
import jax
import jax.numpy as jnp
from jax import lax
from jax.sharding import PartitionSpec as P

D = 7168


def local(query, cache, lengths, resid, out_weight, norm_gain, w_gate, w_up, w_down):
    rows_dev, feature_width = query.shape
    head_dim = cache.shape[2] // 2
    head_count = feature_width // head_dim
    positions_count = cache.shape[1]
    query_heads = query.reshape(rows_dev, head_count, head_dim)
    keys = cache[:, :, :head_dim]
    values = cache[:, :, head_dim:]
    scores = jnp.einsum(
        "rhd,rtd->rht", query_heads, keys, preferred_element_type=jnp.float32
    ) * head_dim ** (-0.5)
    positions = lax.broadcasted_iota(jnp.int32, (1, 1, positions_count), 2)
    valid = positions < lengths[:, None, None]
    scores = jnp.where(valid, scores, -jnp.inf)
    top = jnp.max(scores, axis=-1, keepdims=True)
    weights = jnp.exp(scores - top)
    probs = (weights / jnp.sum(weights, axis=-1, keepdims=True)).astype(jnp.bfloat16)
    attended = jnp.einsum("rht,rtd->rhd", probs, values, preferred_element_type=jnp.float32)
    attended = attended.astype(jnp.bfloat16).reshape(rows_dev, feature_width)
    attn_count = lax.axis_size("attn")
    grouped = lax.all_gather(attended, "ffn", axis=0, tiled=True)
    heads_rows = lax.all_to_all(grouped, "attn", split_axis=1, concat_axis=0, tiled=True)
    total_rows = heads_rows.shape[0]
    own_count = total_rows // attn_count
    own_start = lax.axis_index("attn") * own_count
    partial_value = jnp.dot(heads_rows, out_weight, preferred_element_type=jnp.float32)
    own_part = lax.dynamic_slice_in_dim(partial_value, own_start, own_count, 0) + resid.astype(
        jnp.float32
    )
    partial_value = lax.dynamic_update_slice_in_dim(partial_value, own_part, own_start, 0)
    state_all = lax.psum(partial_value, "attn")
    squares = lax.psum(jnp.sum(state_all * state_all, axis=1), "ffn")
    normed_all = (state_all * lax.rsqrt(squares / D + 1e-06)[:, None] * norm_gain).astype(
        jnp.bfloat16
    )
    gate_part = jnp.dot(normed_all, w_gate, preferred_element_type=jnp.float32)
    up_part = jnp.dot(normed_all, w_up, preferred_element_type=jnp.float32)
    both_parts = jnp.concatenate([gate_part, up_part], axis=1)
    state_own = lax.dynamic_slice_in_dim(state_all, own_start, own_count, 0)
    half_width = w_gate.shape[1]
    shares = lax.psum_scatter(both_parts, "ffn", scatter_dimension=0, tiled=True)
    active_share = (jax.nn.silu(shares[:, :half_width]) * shares[:, half_width:]).astype(
        jnp.bfloat16
    )
    active = lax.all_gather(active_share, "ffn", axis=0, tiled=True)
    returned = lax.psum_scatter(
        jnp.dot(active, w_down, preferred_element_type=jnp.float32),
        "attn",
        scatter_dimension=0,
        tiled=True,
    )
    return (state_own + returned).astype(jnp.bfloat16)


def solution(mesh):
    placed = (
        P(("groups", "attn", "ffn"), None),
        P(("groups", "attn", "ffn"), None, None),
        P(("groups", "attn", "ffn")),
        P(("groups", "attn"), "ffn"),
        P("attn", "ffn"),
        P("ffn"),
        P("ffn", "attn"),
        P("ffn", "attn"),
        P("attn", "ffn"),
    )
    return jax.shard_map(
        local, mesh=mesh, in_specs=placed, out_specs=P(("groups", "attn"), "ffn"), check_vma=False
    )
```

profile of v0, /device:TPU:0, one launch (start us, length us, event | category | flops | bytes accessed | tf_op | source)
XLA Modules:
  0.0 194.1 jit_solution(5858100768478625286)
XLA Ops:
  6.5 0.7 iota_compare_fusion
  7.3 2.4 %fusion.10 = f32[4,64,1024]{2,1,0:T(8,128)S(1)} fusion(bf16[4,1024,512]{2,1,0:T(8,128)(2,1)} %param.10, pred[4,1024]{1,0:T(4,128)(4,1)S(1)} %iota_compare_fusion, bf16[1,4,64,256]{3,1,2,0:T(4,128)(2,1)} %bitcast.16), kind=kOutput, calls=%fused_computation.9 | convolution fusion | flops 134742016 | bytes 3280896 | tf_op jit(solution)/shard_map/rhd,rtd->rht/dot_general | solution.py:17
  9.7 0.3 fusion.23
  10.0 2.2 %fusion.13 = bf16[4,64,256]{2,1,0:T(8,128)(2,1)S(1)} fusion(bf16[4,1024,512]{2,1,0:T(8,128)(2,1)} %param.10, f32[4,64]{1,0:T(4,128)S(1)} %fusion.23, f32[4,64,1024]{2,1,0:T(8,128)S(1)} %fusion.10), kind=kOutput, calls=%fused_computation.10 | convolution fusion | flops 135070976 | bytes 4327424 | tf_op jit(solution)/shard_map/rht,rtd->rhd/dot_general | solution.py:26
  12.2 0.1 reshape.36
  12.3 8.6 %all-gather = bf16[4,4,16384]{2,1,0:T(4,128)(2,1)S(1)} all-gather(bf16[1,4,16384]{2,1,0:T(4,128)(2,1)S(1)} %reshape.36), channel_id=1, replica_groups=mesh['groups'=2,'attn'=4,'ffn'=4] {'ffn'}, dimensions={0}, use_global_device_ids=true | all-gather | bytes 655360 | tf_op jit(solution)/shard_map/all_gather | solution.py:29
  20.9 0.4 all_to_all.14
  21.3 1.1 copy.11
  22.4 4.9 %all-to-all-start = ((bf16[16,4,4096]{2,0,1:T(8,128)(2,1)}), bf16[16,4,4096]{2,0,1:T(8,128)(2,1)S(1)}, u32[]{:S(2)}, u32[]{:S(2)}) async-start(bf16[16,4,4096]{2,0,1:T(8,128)(2,1)} %copy.11), calls=%async_computation | async-start | bytes 1048576 | tf_op jit(solution)/shard_map/all_to_all | solution.py:30
  27.3 15.0 %all-to-all-done = bf16[16,4,4096]{2,0,1:T(8,128)(2,1)S(1)} async-done(((bf16[16,4,4096]{2,0,1:T(8,128)(2,1)}), bf16[16,4,4096]{2,0,1:T(8,128)(2,1)S(1)}, u32[]{:S(2)}, u32[]{:S(2)}) %all-to-all-start) | async-done | bytes 524320 | tf_op jit(solution)/shard_map/all_to_all | solution.py:30
  42.3 7.8 %fusion.24 = f32[64,1792]{1,0:T(8,128)S(1)} fusion(bf16[64,4096]{1,0:T(8,128)(2,1)S(1)} %bitcast.15, bf16[4096,1792]{1,0:T(8,128)(2,1)} %param.13), kind=kOutput, calls=%fused_computation.27 | convolution fusion | flops 939524096 | bytes 15663104 | tf_op jit(solution)/shard_map/dot_general | solution.py:34
  50.1 0.8 copy-done.1
  51.0 36.3 %all-reduce.2.cloned.1.call-done = f32[64,1792]{1,0:T(8,128)} async-done(((f32[64,1792]{1,0:T(8,128)}), f32[64,1792]{1,0:T(8,128)}) %all-reduce.2.cloned.1.call-update) | async-done | bytes 458768 | tf_op jit(solution)/shard_map/psum | solution.py:39
  87.3 1.1 multiply_reduce_fusion
  88.4 5.7 %psum.15 = f32[64]{0:T(128)S(1)} all-reduce(f32[64]{0:T(128)S(1)} %multiply_reduce_fusion), channel_id=1, replica_groups=mesh['groups'=2,'attn'=4,'ffn'=4] {'ffn'}, use_global_device_ids=true, to_apply=%region_4.5 | all-reduce | flops 64 | bytes 512 | tf_op jit(solution)/shard_map/psum | solution.py:40
  94.1 8.9 %fusion.21 = f32[64,4608]{1,0:T(8,128)S(1)} fusion(bf16[1792,4608]{1,0:T(8,128)(2,1)} %param.16, f32[64,1792]{1,0:T(8,128)} %all-reduce.2.cloned.1.call-done, f32[1792]{0:T(1024)S(1)} %copy-done.2, f32[64]{0:T(128)S(1)} %add_rsqrt_fusion), kind=kOutput, calls=%fused_computation.24 | convolution fusion | flops 1057308672 | bytes 18160896 | tf_op jit(solution)/shard_map/dot_general | solution.py:45
  103.1 8.7 %fusion.22 = f32[64,4608]{1,0:T(8,128)S(1)} fusion(bf16[1792,4608]{1,0:T(8,128)(2,1)} %param.15, f32[64,1792]{1,0:T(8,128)S(1)} %copy-done, f32[1792]{0:T(1024)S(1)} %copy-done.2, f32[64]{0:T(128)S(1)} %add_rsqrt_fusion), kind=kOutput, calls=%fused_computation.25 | convolution fusion | flops 1057308672 | bytes 18160896 | tf_op jit(solution)/shard_map/dot_general | solution.py:44
  111.8 1.6 pad_maximum_fusion
  113.5 33.3 %reduce-scatter.3.cloned.1.call-done = f32[16,9216]{1,0:T(8,128)} async-done(((f32[64,9216]{1,0:T(8,128)}), f32[16,9216]{1,0:T(8,128)}) %reduce-scatter.3.cloned.1.call-update) | async-done | bytes 589840 | tf_op jit(solution)/shard_map/reduce_scatter | solution.py:49
  146.7 1.1 fusion.17
  147.9 7.1 %all_gather.7 = bf16[64,4608]{1,0:T(8,128)(2,1)S(1)} all-gather(bf16[16,4608]{1,0:T(8,128)(2,1)S(1)} %fusion.17), channel_id=1, replica_groups=mesh['groups'=2,'attn'=4,'ffn'=4] {'ffn'}, dimensions={0}, use_global_device_ids=true | all-gather | bytes 737280 | tf_op jit(solution)/shard_map/all_gather | solution.py:53
  155.0 9.4 %fusion.25 = f32[64,1792]{1,0:T(8,128)} fusion(bf16[64,4608]{1,0:T(8,128)(2,1)S(1)} %all_gather.7, bf16[4608,1792]{1,0:T(8,128)(2,1)} %param.17), kind=kOutput, calls=%fused_computation.28 | convolution fusion | flops 1056964608 | bytes 17563648 | tf_op jit(solution)/shard_map/dot_general | solution.py:55
  164.5 21.6 %reduce-scatter.5.cloned.1.call-done = f32[16,1792]{1,0:T(8,128)} async-done(((f32[64,1792]{1,0:T(8,128)}), f32[16,1792]{1,0:T(8,128)}) %reduce-scatter.5.cloned.1.call-update) | async-done | bytes 114704 | tf_op jit(solution)/shard_map/reduce_scatter | solution.py:54
  186.0 1.5 add_convert_fusion
  (15 shorter events, 0.2 us)
Async XLA Ops:
  22.4 19.9 %all-to-all-start = ((bf16[16,4,4096]{2,0,1:T(8,128)(2,1)}), bf16[16,4,4096]{2,0,1:T(8,128)(2,1)S(1)}, u32[]{:S(2)}, u32[]{:S(2)}) async-start(bf16[16,4,4096]{2,0,1:T(8,128)(2,1)} %copy.11), calls=%async_computation | async-start | bytes 1048576 | tf_op jit(solution)/shard_map/all_to_all | solution.py:30
  27.3 60.0 %all-reduce.2.cloned.1.call-start = ((), (), s32[]{:S(2)}) async-start(), calls=%async_computation.3 | async-start | bytes 917504 | tf_op jit(solution)/shard_map/psum | solution.py:39
  42.3 7.8 %copy-start.3 = (bf16[16,1792]{1,0:T(8,128)(2,1)S(1)}, bf16[16,1792]{1,0:T(8,128)(2,1)}, u32[]{:S(2)}) copy-start(bf16[16,1792]{1,0:T(8,128)(2,1)} %param.12) | copy-start | bytes 172036
  42.3 51.9 %copy-start.2 = (f32[1792]{0:T(1024)S(1)}, f32[1792]{0:T(1024)}, u32[]{:S(2)}) copy-start(f32[1792]{0:T(1024)} %param.14) | copy-start | bytes 21508
  50.1 0.8 copy-start.1
  50.9 95.8 %reduce-scatter.3.cloned.1.call-start = ((), (), s32[]{:S(2)}) async-start(), calls=%async_computation.4 | async-start | bytes 2949120 | tf_op jit(solution)/shard_map/reduce_scatter | solution.py:49
  94.1 9.0 %copy-start = (f32[64,1792]{1,0:T(8,128)S(1)}, f32[64,1792]{1,0:T(8,128)}, u32[]{:S(2)}) copy-start(f32[64,1792]{1,0:T(8,128)} %all-reduce.2.cloned.1.call-done) | copy-start | bytes 1376260
  113.4 72.6 %reduce-scatter.5.cloned.1.call-start = ((), (), s32[]{:S(2)}) async-start(), calls=%async_computation.5 | async-start | bytes 573440 | tf_op jit(solution)/shard_map/reduce_scatter | solution.py:54
Sparse Core Ops, SparseCore 0:
  51.0 36.2 all-reduce.1
  113.5 33.1 reduce-scatter.2
  164.6 21.3 reduce-scatter.4
where the time goes:
time: 195 us; the launch traced here: 194 us
  waiting for transfers between devices  106 us (54%)
  matrix products  39.5 us (20%)
  blocking collectives  21.4 us (11%)
  between operations  13.2 us (7%)
  other arithmetic  6.47 us (3%)
  starting transfers between devices  4.96 us (3%)
  local copies, waits for them, and re-layouts  2.34 us (1%)
    psum x1, waiting for transfers between devices, local(): state_all = lax.psum(partial_value, 'attn')  36.3 us
    reduce_scatter x1, waiting for transfers between devices, local(): lax.psum_scatter(both_parts, 'ffn', scatter_dimension=0, tiled=True)  33.3 us
    reduce_scatter x1, waiting for transfers between devices, local(): lax.psum_scatter(jnp.dot(active, w_down, preferred_element_type=jnp.float...  21.6 us
    all_to_all x1, waiting for transfers between devices, local(): lax.all_to_all(grouped, 'attn', split_axis=1, concat_axis=0, tiled=True)  15 us
    dot_general x1, matrix products, local(): jnp.dot(active, w_down, preferred_element_type=jnp.float32)  9.43 us
    dot_general x1, matrix products, local(): up_part = jnp.dot(normed_all, w_up, preferred_element_type=jnp.float32)  8.94 us
    dot_general x1, matrix products, local(): gate_part = jnp.dot(normed_all, w_gate, preferred_element_type=jnp.float32)  8.74 us
    all_gather x1, blocking collectives, local(): grouped = lax.all_gather(attended, 'ffn', axis=0, tiled=True)  8.62 us
  transfers between devices with their start and end apart: 4, of which 4 were waited for; matrix products, arithmetic and copies ran while one was open for 0% of the time, Pallas kernels for 0%

commit v1 on v0

--- a/solution.py
+++ b/solution.py
@@ -1,12 +1,19 @@
+import functools
+
 import jax
 import jax.numpy as jnp
 from jax import lax
+from jax.experimental import pallas as pl
+from jax.experimental.pallas import tpu as pltpu
 from jax.sharding import PartitionSpec as P
 
 D = 7168
-
-
-def local(query, cache, lengths, resid, out_weight, norm_gain, w_gate, w_up, w_down):
+F32 = jnp.float32
+BF16 = jnp.bfloat16
+MIB = 1 << 20
+
+
+def plain(query, cache, lengths, resid, out_weight, norm_gain, w_gate, w_up, w_down):
     rows_dev, feature_width = query.shape
     head_dim = cache.shape[2] // 2
     head_count = feature_width // head_dim
@@ -60,6 +67,346 @@
     return (state_own + returned).astype(jnp.bfloat16)
 
 
+VM = pl.BlockSpec(memory_space=pltpu.VMEM)
+
+
+def call(kernel, name, outs, ins, scratch=(), weights=(), specs=None, flops=0, moved=0, limit=8):
+    weights = [pltpu.with_memory_space_constraint(w, pltpu.VMEM) for w in weights]
+    return pl.pallas_call(
+        kernel,
+        out_shape=[jax.ShapeDtypeStruct(s, t) for s, t in outs],
+        in_specs=(specs or [VM] * len(ins)) + [VM] * len(weights),
+        out_specs=[VM] * len(outs),
+        scratch_shapes=list(scratch),
+        compiler_params=pltpu.CompilerParams(vmem_limit_bytes=limit * MIB),
+        cost_estimate=pl.CostEstimate(flops=flops, bytes_accessed=moved, transcendentals=0),
+        name=name,
+    )(*ins, *weights)
+
+
+def swap(x, axis, step):
+    count = lax.axis_size(axis)
+    return lax.ppermute(x, axis, [(i, i ^ step) for i in range(count)])
+
+
+def tiles(width, tile=256):
+    return [(s, min(tile, width - s)) for s in range(0, width, tile)]
+
+
+def split3(value):
+    high = value.astype(BF16).astype(F32)
+    middle = (value - high).astype(BF16).astype(F32)
+    low = value - high - middle
+    lane = lax.broadcasted_iota(jnp.int32, (value.shape[0], 128), 1)
+    zero = jnp.zeros((value.shape[0], 128), F32)
+    block = jnp.where(lane == 0, high, jnp.where(lane == 1, middle, jnp.where(lane == 2, low, zero)))
+    return block.astype(BF16)
+
+
+def join3(block):
+    return jnp.sum(block.astype(F32), axis=1, keepdims=True)
+
+
+def attend(attn, rows, heads, hd, length, lens, q, cache, *refs):
+    outs, (kv, sems, att) = refs[:attn], refs[attn:]
+    copies = [pltpu.make_async_copy(cache.at[r], kv.at[r], sems.at[r]) for r in range(rows)]
+    for c in copies:
+        c.start()
+    position = lax.broadcasted_iota(jnp.int32, (1, length), 1)
+    per = heads // attn
+    for r in range(rows):
+        copies[r].wait()
+        s = lax.dot_general(
+            q[r], kv[r, :, :hd], (((1,), (1,)), ((), ())), preferred_element_type=F32
+        ) * hd ** (-0.5)
+        s = jnp.where(position < lens[r], s, -jnp.inf)
+        p = jnp.exp(s - jnp.max(s, axis=1, keepdims=True))
+        p = (p / jnp.sum(p, axis=1, keepdims=True)).astype(BF16)
+        o = jnp.dot(p, kv[r, :, hd:], preferred_element_type=F32).astype(BF16)
+        att[r] = o.reshape(attn, per, hd)
+    me = lax.axis_index("attn")
+    for k in range(attn):
+        outs[k][...] = att[:, me ^ k]
+
+
+def pack(attn, *refs):
+    out = refs[attn]
+    me = lax.axis_index("attn")
+    for k in range(attn):
+        out[me ^ k] = refs[k][...]
+
+
+def project(attn, ffn, rows, per, hd, *refs):
+    blocks, (resid, w) = refs[:ffn], refs[ffn : ffn + 2]
+    sends, (own, xs, x, res) = refs[ffn + 2 : ffn + 1 + attn], refs[ffn + 1 + attn :]
+    f, a = lax.axis_index("ffn"), lax.axis_index("attn")
+    total = attn * ffn * rows
+    for j in range(ffn):
+        for i in range(attn):
+            start = pl.multiple_of((i * ffn + (f ^ j)) * rows * per, rows * per)
+            value = blocks[j][i].reshape(rows * per, hd).astype(F32)
+            for c in range(hd // 128):
+                xs[c, pl.ds(start, rows * per), :] = value[:, c * 128 : (c + 1) * 128]
+    for h in range(per):
+        for c in range(hd // 128):
+            s = h * hd + c * 128
+            x[:, s : s + 128] = xs[c, pl.ds(h, total, stride=per), :].astype(BF16)
+    for s, n in tiles(w.shape[1]):
+        y = jnp.dot(x[...], w[:, s : s + n], preferred_element_type=F32)
+        res[:, :, s : s + n] = y.reshape(attn, ffn * rows, n)
+    for k in range(1, attn):
+        sends[k - 1][...] = res[a ^ k].astype(BF16)
+    own[...] = res[a] + resid[...].astype(F32)
+
+
+def settle(attn, *refs):
+    own, gain = refs[0], refs[attn]
+    state, xg = refs[attn + 1 :]
+    width = own.shape[1]
+    total = own[...]
+    for k in range(1, attn):
+        total = total + refs[k][...].astype(F32)
+    state[...] = total
+    xg[:, :width] = (total * gain[...]).astype(BF16)
+    xg[:, width:] = split3(jnp.sum(total * total, axis=1, keepdims=True))
+
+
+def gather_rows(attn, *refs):
+    x = refs[attn]
+    a = lax.axis_index("attn")
+    for k in range(attn):
+        x[a ^ k] = refs[k][...]
+
+
+def hidden(j, ffn, chunk, x, wg, wu, out):
+    start = (lax.axis_index("ffn") ^ j) * chunk
+    rows, width = x.shape[0] * x.shape[1], wg.shape[0]
+    lhs = x[:, :, :width].reshape(rows, width)
+    whole = chunk // 256 * 256
+
+    def columns(w, s, n):
+        return w[:, pl.ds(pl.multiple_of(start + s, 128), n)]
+
+    for base, w in ((0, wg), (chunk, wu)):
+        for s, n in tiles(whole):
+            y = jnp.dot(lhs, columns(w, s, n), preferred_element_type=F32)
+            out[:, base + s : base + s + n] = y.astype(out.dtype)
+    rest = chunk - whole
+    if rest:
+        w = jnp.concatenate([columns(wg, whole, rest), columns(wu, whole, rest)], axis=1)
+        y = jnp.dot(lhs, w, preferred_element_type=F32).astype(out.dtype)
+        out[:, whole:chunk] = y[:, :rest]
+        out[:, chunk + whole : 2 * chunk] = y[:, rest:]
+    if out.dtype == BF16:
+        out[:, 2 * chunk :] = x[:, :, width:].reshape(rows, 128)
+
+
+def relay(chunk, mine, x, theirs, out):
+    rows = mine.shape[0]
+    width = x.shape[2] - 128
+    out[:, : 2 * chunk] = (mine[...] + theirs[:, : 2 * chunk].astype(F32)).astype(BF16)
+    squares = join3(x[:, :, width:].reshape(rows, 128)) + join3(theirs[:, 2 * chunk :])
+    out[:, 2 * chunk :] = split3(squares)
+
+
+def activate(chunk, mine, x, near, far, out):
+    rows = mine.shape[0]
+    width = x.shape[2] - 128
+    squares = (
+        join3(x[:, :, width:].reshape(rows, 128))
+        + join3(near[:, 2 * chunk :])
+        + join3(far[:, 2 * chunk :])
+    )
+    scale = lax.rsqrt(squares / D + 1e-06)
+    for s, n in tiles(chunk, 384):
+        gate, up = (
+            (
+                mine[:, b : b + n] + near[:, b : b + n].astype(F32) + far[:, b : b + n].astype(F32)
+            )
+            * scale
+            for b in (s, chunk + s)
+        )
+        out[:, s : s + n] = (gate / (1.0 + jnp.exp(-gate)) * up).astype(BF16)
+
+
+def down(j, first, last, attn, chunk, *refs):
+    refs = list(refs)
+    active = refs.pop(0)
+    acc = None if first else refs.pop(0)
+    w = refs.pop(0)
+    start = pl.multiple_of((lax.axis_index("ffn") ^ j) * chunk, chunk)
+    rows = active.shape[0]
+    a = lax.axis_index("attn")
+    res = refs[-1]
+    for s, n in tiles(w.shape[1]):
+        y = jnp.dot(active[...], w[pl.ds(start, chunk), s : s + n], preferred_element_type=F32)
+        if acc is not None:
+            y = y + acc[:, s : s + n]
+        if last:
+            res[:, :, s : s + n] = y.reshape(attn, rows // attn, n)
+        else:
+            res[:, s : s + n] = y
+    if last:
+        for k in range(1, attn):
+            refs[k - 1][...] = res[a ^ k].astype(BF16)
+        refs[attn - 1][...] = res[a]
+
+
+def finish(attn, *refs):
+    total = refs[0][...] + refs[1][...]
+    for k in range(1, attn):
+        total = total + refs[1 + k][...].astype(F32)
+    refs[-1][...] = total.astype(BF16)
+
+
+def fast(query, cache, lengths, resid, out_weight, norm_gain, w_gate, w_up, w_down):
+    attn, ffn = lax.axis_size("attn"), lax.axis_size("ffn")
+    rows, features = query.shape
+    length, hd = cache.shape[1], cache.shape[2] // 2
+    heads = features // hd
+    per = heads // attn
+    own_rows, width = resid.shape
+    total = own_rows * attn
+    chunk = w_gate.shape[1] // ffn
+    block = (rows, per, hd)
+
+    parts = call(
+        functools.partial(attend, attn, rows, heads, hd, length),
+        "attend",
+        [(block, BF16)] * attn,
+        [lengths, query.reshape(rows, heads, hd), cache],
+        [
+            pltpu.VMEM(cache.shape, BF16),
+            pltpu.SemaphoreType.DMA((rows,)),
+            pltpu.VMEM((rows, attn, per, hd), BF16),
+        ],
+        specs=[
+            pl.BlockSpec(memory_space=pltpu.SMEM),
+            VM,
+            pl.BlockSpec(memory_space=pltpu.HBM),
+        ],
+        flops=4 * rows * heads * length * hd,
+        moved=cache.size * 2,
+        limit=16,
+    )
+    parts = [parts[0]] + [swap(parts[k], "attn", k) for k in range(1, attn)]
+    (mine,) = call(functools.partial(pack, attn), "pack", [((attn, *block), BF16)], parts)
+    across = swap(mine, "ffn", 2)
+    beside = swap(mine, "ffn", 1)
+    diagonal = swap(across, "ffn", 1)
+
+    *sends, own = call(
+        functools.partial(project, attn, ffn, rows, per, hd),
+        "project",
+        [((own_rows, width), BF16)] * (attn - 1) + [((own_rows, width), F32)],
+        [mine, beside, across, diagonal, resid],
+        [
+            pltpu.VMEM((hd // 128, total * per, 128), F32),
+            pltpu.VMEM((total, per * hd), BF16),
+            pltpu.VMEM((attn, own_rows, width), F32),
+        ],
+        [out_weight],
+        flops=2 * total * out_weight.size,
+        moved=out_weight.size * 2,
+    )
+    came = [swap(sends[k - 1], "attn", k) for k in range(1, attn)]
+    state, xg = call(
+        functools.partial(settle, attn),
+        "settle",
+        [((own_rows, width), F32), ((own_rows, width + 128), BF16)],
+        [own, *came, norm_gain.reshape(1, width)],
+    )
+    xs = [xg] + [swap(xg, "attn", k) for k in range(1, attn)]
+    (x,) = call(
+        functools.partial(gather_rows, attn),
+        "gather_rows",
+        [((attn, own_rows, width + 128), BF16)],
+        xs,
+    )
+
+    def part(j, name, wide):
+        shape = ((total, 2 * chunk), F32) if wide else ((total, 2 * chunk + 128), BF16)
+        return call(
+            functools.partial(hidden, j, ffn, chunk),
+            name,
+            [shape],
+            [x],
+            weights=[w_gate, w_up],
+            flops=4 * total * width * chunk,
+            moved=4 * width * chunk,
+        )[0]
+
+    far_beside = swap(part(3, "hidden_diagonal", False), "ffn", 1)
+    far_mine = part(2, "hidden_across", True)
+    (far,) = call(
+        functools.partial(relay, chunk),
+        "relay",
+        [((total, 2 * chunk + 128), BF16)],
+        [far_mine, x, far_beside],
+    )
+    far_came = swap(far, "ffn", 2)
+    near_came = swap(part(1, "hidden_beside", False), "ffn", 1)
+    near_mine = part(0, "hidden_own", True)
+    (active,) = call(
+        functools.partial(activate, chunk),
+        "activate",
+        [((total, chunk), BF16)],
+        [near_mine, x, near_came, far_came],
+    )
+
+    active_across = swap(active, "ffn", 2)
+    active_beside = swap(active, "ffn", 1)
+    active_diagonal = swap(active_across, "ffn", 1)
+
+    def fold(j, name, value, acc, last=False):
+        ins = [value] if acc is None else [value, acc]
+        if last:
+            outs = [((own_rows, width), BF16)] * (attn - 1) + [((own_rows, width), F32)]
+            scratch = [pltpu.VMEM((attn, own_rows, width), F32)]
+        else:
+            outs, scratch = [((total, width), F32)], []
+        return call(
+            functools.partial(down, j, acc is None, last, attn, chunk),
+            name,
+            outs,
+            ins,
+            scratch,
+            weights=[w_down],
+            flops=2 * total * width * chunk,
+            moved=2 * width * chunk,
+        )
+
+    (acc,) = fold(0, "down_own", active, None)
+    (acc,) = fold(1, "down_beside", active_beside, acc)
+    (acc,) = fold(2, "down_across", active_across, acc)
+    *sends, own = fold(3, "down_diagonal", active_diagonal, acc, True)
+    came = [swap(sends[k - 1], "attn", k) for k in range(1, attn)]
+    (mixed,) = call(
+        functools.partial(finish, attn),
+        "finish",
+        [((own_rows, width), BF16)],
+        [state, own, *came],
+    )
+    return mixed
+
+
+def local(query, cache, lengths, resid, out_weight, norm_gain, w_gate, w_up, w_down):
+    attn, ffn = lax.axis_size("attn"), lax.axis_size("ffn")
+    head_dim = cache.shape[2] // 2
+    per = query.shape[1] // head_dim // attn
+    fits = (
+        ffn == 4
+        and attn == 4
+        and per % 16 == 0
+        and head_dim % 128 == 0
+        and resid.shape[0] % 16 == 0
+        and resid.shape[1] % 128 == 0
+        and w_gate.shape[1] % (128 * ffn) == 0
+    )
+    body = fast if fits else plain
+    return body(query, cache, lengths, resid, out_weight, norm_gain, w_gate, w_up, w_down)
+
+
 def solution(mesh):
     placed = (
         P(("groups", "attn", "ffn"), None),

time: 195 us -> 101 us (0.52)
  waiting for transfers between devices: 106 us -> 31.4 us
  matrix products: 39.5 us -> 0 us
  local copies, waits for them, and re-layouts: 2.34 us -> 28.7 us
  blocking collectives: 21.4 us -> 0 us
  starting transfers between devices: 4.96 us -> 23.4 us
  Pallas kernels: 0 us -> 17.2 us
  between operations: 13.2 us -> 0.21 us
  other arithmetic: 6.47 us -> 0.01 us
    reduce_scatter x2 -> x0, waiting for transfers between devices: 54.8 us -> none  [the longest x1 33.3 us: local(): lax.psum_scatter(both_parts, 'ffn', scatter_dimension=0, tiled=True)]
    dot_general x6 -> x0, matrix products: 39.5 us -> none  [the longest x1 9.43 us: local(): jnp.dot(active, w_down, preferred_element_type=jnp.float32)]
    psum x1 -> x0, waiting for transfers between devices: 36.3 us -> none  [local(): state_all = lax.psum(partial_value, 'attn')]
    ppermute x0 -> x21, waiting for transfers between devices: none -> 31.4 us  [swap(): return lax.ppermute(x, axis, [(i, i ^ step) for i in range(count)])]
    unnamed x9 -> x25, local copies, waits for them, and re-layouts: 0.87 us -> 28 us
    ppermute x0 -> x21, starting transfers between devices: none -> 23.4 us  [swap(): return lax.ppermute(x, axis, [(i, i ^ step) for i in range(count)])]
    pallas_call x0 -> x16, Pallas kernels: none -> 17.2 us  [call(): pl.pallas_call(kernel, out_shape=[jax.ShapeDtypeStruct(s, t) for s, t in...]
    all_gather x2 -> x0, blocking collectives: 15.8 us -> none  [the longest x1 8.62 us: local(): grouped = lax.all_gather(attended, 'ffn', axis=0, tiled=True)]
  transfers between devices with their start and end apart: 4 -> 21, of which waited for: 4 -> 10; matrix products, arithmetic and copies ran while one was open for 0% -> 1% of each run, Pallas kernels for 0% -> 7%
where the time goes in v1:
time: 101 us
  waiting for transfers between devices  31.4 us (31%)
  local copies, waits for them, and re-layouts  28.7 us (28%)
  starting transfers between devices  23.4 us (23%)
  Pallas kernels  17.2 us (17%)
    ppermute x21, waiting for transfers between devices, swap(): return lax.ppermute(x, axis, [(i, i ^ step) for i in range(count)])  31.4 us
    unnamed x25, local copies, waits for them, and re-layouts  28 us
    ppermute x21, starting transfers between devices, swap(): return lax.ppermute(x, axis, [(i, i ^ step) for i in range(count)])  23.4 us
    pallas_call x16, Pallas kernels, call(): pl.pallas_call(kernel, out_shape=[jax.ShapeDtypeStruct(s, t) for s, t in...  17.2 us
  transfers between devices with their start and end apart: 21, of which 10 were waited for; matrix products, arithmetic and copies ran while one was open for 1% of the time, Pallas kernels for 7%

profile of v1, /device:TPU:0, one launch (start us, length us, event | category | flops | bytes accessed | tf_op | source)
XLA Modules:
  0.0 101.0 jit_solution(16619868184581147802)
XLA Ops:
  1.1 2.4 %copy-done.5 = bf16[4,1024,512]{2,1,0:T(8,128)(2,1)S(1)} copy-done((bf16[4,1024,512]{2,1,0:T(8,128)(2,1)S(1)}, bf16[4,1024,512]{2,1,0:T(8,128)(2,1)}, u32[]{:S(2)}) %copy-start.5) | copy-done | bytes 4194328
  4.5 3.9 %attend.1 = (bf16[4,16,256]{2,1,0:T(8,128)(2,1)S(1)}, bf16[4,16,256]{2,1,0:T(8,128)(2,1)S(1)}, bf16[4,16,256]{2,1,0:T(8,128)(2,1)S(1)}, bf16[4,16,256]{2,1,0:T(8,128)(2,1)S(1)}) custom-call(s32[4]{0:T(128)S(1)} %copy-done.7, bf16[4,64,256]{2,1,0:T(8,128)(2,1)S(1)} %bitcast.6, bf16[4,1024,512]{2,1,0:T(8,128)(2,1)S(1)} %copy-done.5), custom_call_target="tpu_custom_call" | custom-call | flops 268435456 | bytes 4194304 | tf_op jit(solution)/shard_map/attend/pallas_call | solution.py:75
  8.4 3.1 %collective-permute-start = (bf16[4,16,256]{2,1,0:T(8,128)(2,1)S(1)}, bf16[4,16,256]{2,1,0:T(8,128)(2,1)S(1)}, u32[]{:S(2)}, u32[]{:S(2)}) collective-permute-start(bf16[4,16,256]{2,1,0:T(8,128)(2,1)S(1)} %get-tuple-element.20), channel_id=1, source_target_pairs={{0,4},{4,0},{8,12},{12,8},{1,5},{5,1},{9,13},{13,9},{2,6},{6,2},{1... | collective-permute-start | bytes 98312 | tf_op jit(solution)/shard_map/ppermute | solution.py:89
  11.5 2.6 %collective-permute-start.1 = (bf16[4,16,256]{2,1,0:T(8,128)(2,1)S(1)}, bf16[4,16,256]{2,1,0:T(8,128)(2,1)S(1)}, u32[]{:S(2)}, u32[]{:S(2)}) collective-permute-start(bf16[4,16,256]{2,1,0:T(8,128)(2,1)S(1)} %get-tuple-element.21), channel_id=1, source_target_pairs={{0,8},{4,12},{8,0},{12,4},{1,9},{5,13},{9,1},{13,5},{2,10},{6,14},... | collective-permute-start | bytes 98312 | tf_op jit(solution)/shard_map/ppermute | solution.py:89
  14.1 2.8 %collective-permute-done.1.refs_2_ = bf16[4,16,256]{2,1,0:T(8,128)(2,1)S(1)} collective-permute-done((bf16[4,16,256]{2,1,0:T(8,128)(2,1)S(1)}, bf16[4,16,256]{2,1,0:T(8,128)(2,1)S(1)}, u32[]{:S(2)}, u32[]{:S(2)}) %collective-permute-start.1) | collective-permute-done | bytes 32800 | tf_op jit(solution)/shard_map/ppermute | solution.py:89
  16.9 2.9 %collective-permute-done.2.refs_3_ = bf16[4,16,256]{2,1,0:T(8,128)(2,1)S(1)} collective-permute-done((bf16[4,16,256]{2,1,0:T(8,128)(2,1)S(1)}, bf16[4,16,256]{2,1,0:T(8,128)(2,1)S(1)}, u32[]{:S(2)}, u32[]{:S(2)}) %collective-permute-start.2) | collective-permute-done | bytes 32800 | tf_op jit(solution)/shard_map/ppermute | solution.py:89
  21.4 3.5 %collective-permute-done.4.refs_2_ = bf16[4,4,16,256]{3,2,1,0:T(8,128)(2,1)S(1)} collective-permute-done((bf16[4,4,16,256]{3,2,1,0:T(8,128)(2,1)S(1)}, bf16[4,4,16,256]{3,2,1,0:T(8,128)(2,1)S(1)}, u32[]{:S(2)}, u32[]{:S(2)}) %collective-permute-start.4) | collective-permute-done | bytes 131104 | tf_op jit(solution)/shard_map/ppermute | solution.py:89
  26.2 5.2 %copy-done.4 = bf16[4096,1792]{1,0:T(8,128)(2,1)S(1)} copy-done((bf16[4096,1792]{1,0:T(8,128)(2,1)S(1)}, bf16[4096,1792]{1,0:T(8,128)(2,1)}, u32[]{:S(2)}) %copy-start.4) | copy-done | bytes 14680088
  32.2 3.0 %project.1 = (bf16[16,1792]{1,0:T(8,128)(2,1)S(1)}, bf16[16,1792]{1,0:T(8,128)(2,1)S(1)}, bf16[16,1792]{1,0:T(8,128)(2,1)S(1)}, f32[16,1792]{1,0:T(8,128)S(1)}) custom-call(bf16[4,4,16,256]{3,2,1,0:T(8,128)(2,1)S(1)} %pack.1.refs_0_, bf16[4,4,16,256]{3,2,1,0:T(8,128)(2,1)S(1)} %collective-permute-done.3.refs_1_, ...), custom_call_target="tpu_custom_call" | custom-call | flops 939524096 | bytes 14680064 | tf_op jit(solution)/shard_map/project/pallas_call | solution.py:75
  36.2 3.5 %collective-permute-start.8 = (bf16[16,1792]{1,0:T(8,128)(2,1)S(1)}, bf16[16,1792]{1,0:T(8,128)(2,1)S(1)}, u32[]{:S(2)}, u32[]{:S(2)}) collective-permute-start(bf16[16,1792]{1,0:T(8,128)(2,1)S(1)} %get-tuple-element.26), channel_id=1, source_target_pairs={{0,12},{4,8},{8,4},{12,0},{1,13},{5,9},{9,5},{13,1},{2,14},{6,10},... | collective-permute-start | bytes 172040 | tf_op jit(solution)/shard_map/ppermute | solution.py:89
  40.3 2.9 %collective-permute-done.7.refs_2_ = bf16[16,1792]{1,0:T(8,128)(2,1)S(1)} collective-permute-done((bf16[16,1792]{1,0:T(8,128)(2,1)S(1)}, bf16[16,1792]{1,0:T(8,128)(2,1)S(1)}, u32[]{:S(2)}, u32[]{:S(2)}) %collective-permute-start.7) | collective-permute-done | bytes 57376 | tf_op jit(solution)/shard_map/ppermute | solution.py:89
  43.9 3.0 %collective-permute-start.11 = (bf16[16,1920]{1,0:T(8,128)(2,1)S(1)}, bf16[16,1920]{1,0:T(8,128)(2,1)S(1)}, u32[]{:S(2)}, u32[]{:S(2)}) collective-permute-start(bf16[16,1920]{1,0:T(8,128)(2,1)S(1)} %get-tuple-element.28.refs_0_), channel_id=1, source_target_pairs={{0,12},{4,8},{8,4},{12,0},{1,13},{5,9},{9,5},{13,1},{2,14},{6,10},... | collective-permute-start | bytes 184328 | tf_op jit(solution)/shard_map/ppermute | solution.py:89
  46.9 3.5 %collective-permute-done.10.refs_2_ = bf16[16,1920]{1,0:T(8,128)(2,1)S(1)} collective-permute-done((bf16[16,1920]{1,0:T(8,128)(2,1)S(1)}, bf16[16,1920]{1,0:T(8,128)(2,1)S(1)}, u32[]{:S(2)}, u32[]{:S(2)}) %collective-permute-start.10) | collective-permute-done | bytes 61472 | tf_op jit(solution)/shard_map/ppermute | solution.py:89
  51.2 5.7 %copy-done.1 = bf16[1792,4608]{1,0:T(8,128)(2,1)S(1)} copy-done((bf16[1792,4608]{1,0:T(8,128)(2,1)S(1)}, bf16[1792,4608]{1,0:T(8,128)(2,1)}, u32[]{:S(2)}) %copy-start.1) | copy-done | bytes 16515096
  56.9 1.6 %hidden_diagonal.1 = bf16[64,2432]{1,0:T(8,128)(2,1)S(1)} custom-call(bf16[4,16,1920]{2,1,0:T(8,128)(2,1)S(1)} %gather_rows.1.x, bf16[1792,4608]{1,0:T(8,128)(2,1)S(1)} %copy-done, bf16[1792,4608]{1,0:T(8,128)(2,1)S(1)} %copy-done.1), custom_call_target="tpu_custom_call" | custom-call | flops 528482304 | bytes 8257536 | tf_op jit(solution)/shard_map/hidden_diagonal/pallas_call | solution.py:75
  58.6 1.6 %hidden_beside.1 = bf16[64,2432]{1,0:T(8,128)(2,1)S(1)} custom-call(bf16[4,16,1920]{2,1,0:T(8,128)(2,1)S(1)} %gather_rows.1.x, bf16[1792,4608]{1,0:T(8,128)(2,1)S(1)} %copy-done, bf16[1792,4608]{1,0:T(8,128)(2,1)S(1)} %copy-done.1), custom_call_target="tpu_custom_call" | custom-call | flops 528482304 | bytes 8257536 | tf_op jit(solution)/shard_map/hidden_beside/pallas_call | solution.py:75
  60.7 1.6 %hidden_across.1.mine = f32[64,2304]{1,0:T(8,128)S(1)} custom-call(bf16[4,16,1920]{2,1,0:T(8,128)(2,1)S(1)} %gather_rows.1.x, bf16[1792,4608]{1,0:T(8,128)(2,1)S(1)} %copy-done, bf16[1792,4608]{1,0:T(8,128)(2,1)S(1)} %copy-done.1), custom_call_target="tpu_custom_call" | custom-call | flops 528482304 | bytes 8257536 | tf_op jit(solution)/shard_map/hidden_across/pallas_call | solution.py:75
  66.1 5.8 %collective-permute-done.14.far = bf16[64,2432]{1,0:T(8,128)(2,1)S(1)} collective-permute-done((bf16[64,2432]{1,0:T(8,128)(2,1)S(1)}, bf16[64,2432]{1,0:T(8,128)(2,1)S(1)}, u32[]{:S(2)}, u32[]{:S(2)}) %collective-permute-start.14) | collective-permute-done | bytes 311328 | tf_op jit(solution)/shard_map/ppermute | solution.py:89
  73.7 3.6 %collective-permute-done.15.refs_0_ = bf16[64,1152]{1,0:T(8,128)(2,1)S(1)} collective-permute-done((bf16[64,1152]{1,0:T(8,128)(2,1)S(1)}, bf16[64,1152]{1,0:T(8,128)(2,1)S(1)}, u32[]{:S(2)}, u32[]{:S(2)}) %collective-permute-start.15) | collective-permute-done | bytes 147488 | tf_op jit(solution)/shard_map/ppermute | solution.py:89
  77.3 5.7 %copy-done.2 = bf16[4608,1792]{1,0:T(8,128)(2,1)S(1)} copy-done((bf16[4608,1792]{1,0:T(8,128)(2,1)S(1)}, bf16[4608,1792]{1,0:T(8,128)(2,1)}, u32[]{:S(2)}) %copy-start.2) | copy-done | bytes 16515096
  83.7 5.7 %copy-done.3 = bf16[4608,1792]{1,0:T(8,128)(2,1)S(1)} copy-done((bf16[4608,1792]{1,0:T(8,128)(2,1)S(1)}, bf16[4608,1792]{1,0:T(8,128)(2,1)}, u32[]{:S(2)}) %copy-start.3) | copy-done | bytes 16515096
  92.3 1.7 %collective-permute-start.19 = (bf16[16,1792]{1,0:T(8,128)(2,1)S(1)}, bf16[16,1792]{1,0:T(8,128)(2,1)S(1)}, u32[]{:S(2)}, u32[]{:S(2)}) collective-permute-start(bf16[16,1792]{1,0:T(8,128)(2,1)S(1)} %get-tuple-element.31), channel_id=1, source_target_pairs={{0,8},{4,12},{8,0},{12,4},{1,9},{5,13},{9,1},{13,5},{2,10},{6,14},... | collective-permute-start | bytes 172040 | tf_op jit(solution)/shard_map/ppermute | solution.py:89
  94.0 2.0 %collective-permute-start.20 = (bf16[16,1792]{1,0:T(8,128)(2,1)S(1)}, bf16[16,1792]{1,0:T(8,128)(2,1)S(1)}, u32[]{:S(2)}, u32[]{:S(2)}) collective-permute-start(bf16[16,1792]{1,0:T(8,128)(2,1)S(1)} %get-tuple-element.32), channel_id=1, source_target_pairs={{0,12},{4,8},{8,4},{12,0},{1,13},{5,9},{9,5},{13,1},{2,14},{6,10},... | collective-permute-start | bytes 172040 | tf_op jit(solution)/shard_map/ppermute | solution.py:89
  96.0 4.3 %collective-permute-done.19.refs_3_ = bf16[16,1792]{1,0:T(8,128)(2,1)S(1)} collective-permute-done((bf16[16,1792]{1,0:T(8,128)(2,1)S(1)}, bf16[16,1792]{1,0:T(8,128)(2,1)S(1)}, u32[]{:S(2)}, u32[]{:S(2)}) %collective-permute-start.19) | collective-permute-done | bytes 57376 | tf_op jit(solution)/shard_map/ppermute | solution.py:89
  (61 shorter events, 19.4 us)
Async XLA Ops:
  0.0 51.2 %copy-start = (bf16[1792,4608]{1,0:T(8,128)(2,1)S(1)}, bf16[1792,4608]{1,0:T(8,128)(2,1)}, u32[]{:S(2)}) copy-start(bf16[1792,4608]{1,0:T(8,128)(2,1)} %wg.7) | copy-start | bytes 49545220
  8.4 5.7 %collective-permute-start = (bf16[4,16,256]{2,1,0:T(8,128)(2,1)S(1)}, bf16[4,16,256]{2,1,0:T(8,128)(2,1)S(1)}, u32[]{:S(2)}, u32[]{:S(2)}) collective-permute-start(bf16[4,16,256]{2,1,0:T(8,128)(2,1)S(1)} %get-tuple-element.20), channel_id=1, source_target_pairs={{0,4},{4,0},{8,12},{12,8},{1,5},{5,1},{9,13},{13,9},{2,6},{6,2},{1... | collective-permute-start | bytes 98312 | tf_op jit(solution)/shard_map/ppermute | solution.py:89
  11.5 5.4 %collective-permute-start.1 = (bf16[4,16,256]{2,1,0:T(8,128)(2,1)S(1)}, bf16[4,16,256]{2,1,0:T(8,128)(2,1)S(1)}, u32[]{:S(2)}, u32[]{:S(2)}) collective-permute-start(bf16[4,16,256]{2,1,0:T(8,128)(2,1)S(1)} %get-tuple-element.21), channel_id=1, source_target_pairs={{0,8},{4,12},{8,0},{12,4},{1,9},{5,13},{9,1},{13,5},{2,10},{6,14},... | collective-permute-start | bytes 98312 | tf_op jit(solution)/shard_map/ppermute | solution.py:89
  14.1 5.7 %collective-permute-start.2 = (bf16[4,16,256]{2,1,0:T(8,128)(2,1)S(1)}, bf16[4,16,256]{2,1,0:T(8,128)(2,1)S(1)}, u32[]{:S(2)}, u32[]{:S(2)}) collective-permute-start(bf16[4,16,256]{2,1,0:T(8,128)(2,1)S(1)} %get-tuple-element.22), channel_id=1, source_target_pairs={{0,12},{4,8},{8,4},{12,0},{1,13},{5,9},{9,5},{13,1},{2,14},{6,10},... | collective-permute-start | bytes 98312 | tf_op jit(solution)/shard_map/ppermute | solution.py:89
  19.8 5.0 %collective-permute-start.4 = (bf16[4,4,16,256]{3,2,1,0:T(8,128)(2,1)S(1)}, bf16[4,4,16,256]{3,2,1,0:T(8,128)(2,1)S(1)}, u32[]{:S(2)}, u32[]{:S(2)}) collective-permute-start(bf16[4,4,16,256]{3,2,1,0:T(8,128)(2,1)S(1)} %pack.1.refs_0_), channel_id=1, source_target_pairs={{0,2},{1,3},{2,0},{3,1},{4,6},{5,7},{6,4},{7,5},{8,10},{9,11},{10,... | collective-permute-start | bytes 393224 | tf_op jit(solution)/shard_map/ppermute | solution.py:89
  21.4 3.5 %collective-permute-start.3 = (bf16[4,4,16,256]{3,2,1,0:T(8,128)(2,1)S(1)}, bf16[4,4,16,256]{3,2,1,0:T(8,128)(2,1)S(1)}, u32[]{:S(2)}, u32[]{:S(2)}) collective-permute-start(bf16[4,4,16,256]{3,2,1,0:T(8,128)(2,1)S(1)} %pack.1.refs_0_), channel_id=1, source_target_pairs={{0,1},{1,0},{2,3},{3,2},{4,5},{5,4},{6,7},{7,6},{8,9},{9,8},{10,11... | collective-permute-start | bytes 393224 | tf_op jit(solution)/shard_map/ppermute | solution.py:89
  24.8 1.3 %collective-permute-start.5 = (bf16[4,4,16,256]{3,2,1,0:T(8,128)(2,1)S(1)}, bf16[4,4,16,256]{3,2,1,0:T(8,128)(2,1)S(1)}, u32[]{:S(2)}, u32[]{:S(2)}) collective-permute-start(bf16[4,4,16,256]{3,2,1,0:T(8,128)(2,1)S(1)} %collective-permute-done.4.refs_2_), channel_id=1, source_target_pairs={{0,1},{1,0},{2,3},{3,2},{4,5},{5,4},{6,7},{7,6},{8,9},{9,8},{10,11... | collective-permute-start | bytes 393224 | tf_op jit(solution)/shard_map/ppermute | solution.py:89
  35.2 5.2 %collective-permute-start.6 = (bf16[16,1792]{1,0:T(8,128)(2,1)S(1)}, bf16[16,1792]{1,0:T(8,128)(2,1)S(1)}, u32[]{:S(2)}, u32[]{:S(2)}) collective-permute-start(bf16[16,1792]{1,0:T(8,128)(2,1)S(1)} %get-tuple-element.24), channel_id=1, source_target_pairs={{0,4},{4,0},{8,12},{12,8},{1,5},{5,1},{9,13},{13,9},{2,6},{6,2},{1... | collective-permute-start | bytes 172040 | tf_op jit(solution)/shard_map/ppermute | solution.py:89
  35.3 8.0 %collective-permute-start.7 = (bf16[16,1792]{1,0:T(8,128)(2,1)S(1)}, bf16[16,1792]{1,0:T(8,128)(2,1)S(1)}, u32[]{:S(2)}, u32[]{:S(2)}) collective-permute-start(bf16[16,1792]{1,0:T(8,128)(2,1)S(1)} %get-tuple-element.25), channel_id=1, source_target_pairs={{0,8},{4,12},{8,0},{12,4},{1,9},{5,13},{9,1},{13,5},{2,10},{6,14},... | collective-permute-start | bytes 172040 | tf_op jit(solution)/shard_map/ppermute | solution.py:89
  36.2 7.1 %collective-permute-start.8 = (bf16[16,1792]{1,0:T(8,128)(2,1)S(1)}, bf16[16,1792]{1,0:T(8,128)(2,1)S(1)}, u32[]{:S(2)}, u32[]{:S(2)}) collective-permute-start(bf16[16,1792]{1,0:T(8,128)(2,1)S(1)} %get-tuple-element.26), channel_id=1, source_target_pairs={{0,12},{4,8},{8,4},{12,0},{1,13},{5,9},{9,5},{13,1},{2,14},{6,10},... | collective-permute-start | bytes 172040 | tf_op jit(solution)/shard_map/ppermute | solution.py:89
  43.4 7.1 %collective-permute-start.10 = (bf16[16,1920]{1,0:T(8,128)(2,1)S(1)}, bf16[16,1920]{1,0:T(8,128)(2,1)S(1)}, u32[]{:S(2)}, u32[]{:S(2)}) collective-permute-start(bf16[16,1920]{1,0:T(8,128)(2,1)S(1)} %get-tuple-element.28.refs_0_), channel_id=1, source_target_pairs={{0,8},{4,12},{8,0},{12,4},{1,9},{5,13},{9,1},{13,5},{2,10},{6,14},... | collective-permute-start | bytes 184328 | tf_op jit(solution)/shard_map/ppermute | solution.py:89
  43.9 6.6 %collective-permute-start.11 = (bf16[16,1920]{1,0:T(8,128)(2,1)S(1)}, bf16[16,1920]{1,0:T(8,128)(2,1)S(1)}, u32[]{:S(2)}, u32[]{:S(2)}) collective-permute-start(bf16[16,1920]{1,0:T(8,128)(2,1)S(1)} %get-tuple-element.28.refs_0_), channel_id=1, source_target_pairs={{0,12},{4,8},{8,4},{12,0},{1,13},{5,9},{9,5},{13,1},{2,14},{6,10},... | collective-permute-start | bytes 184328 | tf_op jit(solution)/shard_map/ppermute | solution.py:89
  46.9 4.2 %collective-permute-start.9 = (bf16[16,1920]{1,0:T(8,128)(2,1)S(1)}, bf16[16,1920]{1,0:T(8,128)(2,1)S(1)}, u32[]{:S(2)}, u32[]{:S(2)}) collective-permute-start(bf16[16,1920]{1,0:T(8,128)(2,1)S(1)} %get-tuple-element.28.refs_0_), channel_id=1, source_target_pairs={{0,4},{4,0},{8,12},{12,8},{1,5},{5,1},{9,13},{13,9},{2,6},{6,2},{1... | collective-permute-start | bytes 184328 | tf_op jit(solution)/shard_map/ppermute | solution.py:89
  51.2 5.7 %copy-start.1 = (bf16[1792,4608]{1,0:T(8,128)(2,1)S(1)}, bf16[1792,4608]{1,0:T(8,128)(2,1)}, u32[]{:S(2)}) copy-start(bf16[1792,4608]{1,0:T(8,128)(2,1)} %wu.7) | copy-start | bytes 49545220
  58.5 3.8 %collective-permute-start.13 = (bf16[64,2432]{1,0:T(8,128)(2,1)S(1)}, bf16[64,2432]{1,0:T(8,128)(2,1)S(1)}, u32[]{:S(2)}, u32[]{:S(2)}) collective-permute-start(bf16[64,2432]{1,0:T(8,128)(2,1)S(1)} %hidden_diagonal.1), channel_id=1, source_target_pairs={{0,1},{1,0},{2,3},{3,2},{4,5},{5,4},{6,7},{7,6},{8,9},{9,8},{10,11... | collective-permute-start | bytes 933896 | tf_op jit(solution)/shard_map/ppermute | solution.py:89
  60.2 5.9 %collective-permute-start.12 = (bf16[64,2432]{1,0:T(8,128)(2,1)S(1)}, bf16[64,2432]{1,0:T(8,128)(2,1)S(1)}, u32[]{:S(2)}, u32[]{:S(2)}) collective-permute-start(bf16[64,2432]{1,0:T(8,128)(2,1)S(1)} %hidden_beside.1), channel_id=1, source_target_pairs={{0,1},{1,0},{2,3},{3,2},{4,5},{5,4},{6,7},{7,6},{8,9},{9,8},{10,11... | collective-permute-start | bytes 933896 | tf_op jit(solution)/shard_map/ppermute | solution.py:89
  62.5 9.4 %collective-permute-start.14 = (bf16[64,2432]{1,0:T(8,128)(2,1)S(1)}, bf16[64,2432]{1,0:T(8,128)(2,1)S(1)}, u32[]{:S(2)}, u32[]{:S(2)}) collective-permute-start(bf16[64,2432]{1,0:T(8,128)(2,1)S(1)} %relay.1), channel_id=1, source_target_pairs={{0,2},{1,3},{2,0},{3,1},{4,6},{5,7},{6,4},{7,5},{8,10},{9,11},{10,... | collective-permute-start | bytes 933896 | tf_op jit(solution)/shard_map/ppermute | solution.py:89
  72.1 5.2 %collective-permute-start.15 = (bf16[64,1152]{1,0:T(8,128)(2,1)S(1)}, bf16[64,1152]{1,0:T(8,128)(2,1)S(1)}, u32[]{:S(2)}, u32[]{:S(2)}) collective-permute-start(bf16[64,1152]{1,0:T(8,128)(2,1)S(1)} %activate.1.refs_0_), channel_id=1, source_target_pairs={{0,2},{1,3},{2,0},{3,1},{4,6},{5,7},{6,4},{7,5},{8,10},{9,11},{10,... | collective-permute-start | bytes 442376 | tf_op jit(solution)/shard_map/ppermute | solution.py:89
  73.7 10.0 %collective-permute-start.17 = (bf16[64,1152]{1,0:T(8,128)(2,1)S(1)}, bf16[64,1152]{1,0:T(8,128)(2,1)S(1)}, u32[]{:S(2)}, u32[]{:S(2)}) collective-permute-start(bf16[64,1152]{1,0:T(8,128)(2,1)S(1)} %activate.1.refs_0_), channel_id=1, source_target_pairs={{0,1},{1,0},{2,3},{3,2},{4,5},{5,4},{6,7},{7,6},{8,9},{9,8},{10,11... | collective-permute-start | bytes 442376 | tf_op jit(solution)/shard_map/ppermute | solution.py:89
  77.3 13.5 %collective-permute-start.16 = (bf16[64,1152]{1,0:T(8,128)(2,1)S(1)}, bf16[64,1152]{1,0:T(8,128)(2,1)S(1)}, u32[]{:S(2)}, u32[]{:S(2)}) collective-permute-start(bf16[64,1152]{1,0:T(8,128)(2,1)S(1)} %collective-permute-done.15.refs_0_), channel_id=1, source_target_pairs={{0,1},{1,0},{2,3},{3,2},{4,5},{5,4},{6,7},{7,6},{8,9},{9,8},{10,11... | collective-permute-start | bytes 442376 | tf_op jit(solution)/shard_map/ppermute | solution.py:89
  83.7 5.7 %copy-start.3 = (bf16[4608,1792]{1,0:T(8,128)(2,1)S(1)}, bf16[4608,1792]{1,0:T(8,128)(2,1)}, u32[]{:S(2)}) copy-start(bf16[4608,1792]{1,0:T(8,128)(2,1)} %refs_2_.5) | copy-start | bytes 49545220
  91.6 4.5 %collective-permute-start.18 = (bf16[16,1792]{1,0:T(8,128)(2,1)S(1)}, bf16[16,1792]{1,0:T(8,128)(2,1)S(1)}, u32[]{:S(2)}, u32[]{:S(2)}) collective-permute-start(bf16[16,1792]{1,0:T(8,128)(2,1)S(1)} %get-tuple-element.30), channel_id=1, source_target_pairs={{0,4},{4,0},{8,12},{12,8},{1,5},{5,1},{9,13},{13,9},{2,6},{6,2},{1... | collective-permute-start | bytes 172040 | tf_op jit(solution)/shard_map/ppermute | solution.py:89
  92.3 8.0 %collective-permute-start.19 = (bf16[16,1792]{1,0:T(8,128)(2,1)S(1)}, bf16[16,1792]{1,0:T(8,128)(2,1)S(1)}, u32[]{:S(2)}, u32[]{:S(2)}) collective-permute-start(bf16[16,1792]{1,0:T(8,128)(2,1)S(1)} %get-tuple-element.31), channel_id=1, source_target_pairs={{0,8},{4,12},{8,0},{12,4},{1,9},{5,13},{9,1},{13,5},{2,10},{6,14},... | collective-permute-start | bytes 172040 | tf_op jit(solution)/shard_map/ppermute | solution.py:89
  94.0 6.3 %collective-permute-start.20 = (bf16[16,1792]{1,0:T(8,128)(2,1)S(1)}, bf16[16,1792]{1,0:T(8,128)(2,1)S(1)}, u32[]{:S(2)}, u32[]{:S(2)}) collective-permute-start(bf16[16,1792]{1,0:T(8,128)(2,1)S(1)} %get-tuple-element.32), channel_id=1, source_target_pairs={{0,12},{4,8},{8,4},{12,0},{1,13},{5,9},{9,5},{13,1},{2,14},{6,10},... | collective-permute-start | bytes 172040 | tf_op jit(solution)/shard_map/ppermute | solution.py:89
  (9 other events, 34.4 us)

commit v2 on v1

--- a/solution.py
+++ b/solution.py
@@ -11,6 +11,14 @@
 F32 = jnp.float32
 BF16 = jnp.bfloat16
 MIB = 1 << 20
+US = 10**9
+ATTEND_US = 20
+SETTLE_US = 3
+GATHER_US = 3
+ACTIVATE_US = 10
+HIDDEN_US = 1.5
+DOWN_US = 0.7
+PROJECT_US = 3
 
 
 def plain(query, cache, lengths, resid, out_weight, norm_gain, w_gate, w_up, w_down):
@@ -68,9 +76,10 @@
 
 
 VM = pl.BlockSpec(memory_space=pltpu.VMEM)
-
-
-def call(kernel, name, outs, ins, scratch=(), weights=(), specs=None, flops=0, moved=0, limit=8):
+ANY = pl.BlockSpec(memory_space=pl.ANY)
+
+
+def call(kernel, name, outs, ins, scratch=(), weights=(), specs=None, flops=0, moved=0, limit=4):
     weights = [pltpu.with_memory_space_constraint(w, pltpu.VMEM) for w in weights]
     return pl.pallas_call(
         kernel,
@@ -107,21 +116,34 @@
     return jnp.sum(block.astype(F32), axis=1, keepdims=True)
 
 
-def attend(attn, rows, heads, hd, length, lens, q, cache, *refs):
-    outs, (kv, sems, att) = refs[:attn], refs[attn:]
+def attend(attn, rows, heads, hd, length, lens_any, q_any, cache, *refs):
+    outs, (kv, lens, query, qs, sems, att) = refs[:attn], refs[attn:]
+    first = [
+        pltpu.make_async_copy(q_any, query, sems.at[rows]),
+        pltpu.make_async_copy(lens_any, lens, sems.at[rows + 1]),
+    ]
     copies = [pltpu.make_async_copy(cache.at[r], kv.at[r], sems.at[r]) for r in range(rows)]
-    for c in copies:
+    for c in first + copies:
         c.start()
+    for c in first:
+        c.wait()
+    for h in range(heads):
+        for c in range(hd // 128):
+            s = h * hd + c * 128
+            qs[c, h * rows : (h + 1) * rows, :] = query[:, s : s + 128].astype(F32)
     position = lax.broadcasted_iota(jnp.int32, (1, length), 1)
     per = heads // attn
     for r in range(rows):
         copies[r].wait()
+        q = jnp.concatenate(
+            [qs[c, pl.ds(r, heads, stride=rows), :].astype(BF16) for c in range(hd // 128)], axis=1
+        )
         s = lax.dot_general(
-            q[r], kv[r, :, :hd], (((1,), (1,)), ((), ())), preferred_element_type=F32
+            q, kv[r, :, :hd], (((1,), (1,)), ((), ())), preferred_element_type=F32
         ) * hd ** (-0.5)
         s = jnp.where(position < lens[r], s, -jnp.inf)
         p = jnp.exp(s - jnp.max(s, axis=1, keepdims=True))
-        p = (p / jnp.sum(p, axis=1, keepdims=True)).astype(BF16)
+        p = (p * (1.0 / jnp.sum(p, axis=1, keepdims=True))).astype(BF16)
         o = jnp.dot(p, kv[r, :, hd:], preferred_element_type=F32).astype(BF16)
         att[r] = o.reshape(attn, per, hd)
     me = lax.axis_index("attn")
@@ -178,7 +200,8 @@
         x[a ^ k] = refs[k][...]
 
 
-def hidden(j, ffn, chunk, x, wg, wu, out):
+def hidden(j, ffn, chunk, *refs):
+    x, (wg, wu, out) = refs[0], refs[-3:]
     start = (lax.axis_index("ffn") ^ j) * chunk
     rows, width = x.shape[0] * x.shape[1], wg.shape[0]
     lhs = x[:, :, :width].reshape(rows, width)
@@ -197,26 +220,21 @@
         y = jnp.dot(lhs, w, preferred_element_type=F32).astype(out.dtype)
         out[:, whole:chunk] = y[:, :rest]
         out[:, chunk + whole : 2 * chunk] = y[:, rest:]
-    if out.dtype == BF16:
+    if out.shape[1] > 2 * chunk:
         out[:, 2 * chunk :] = x[:, :, width:].reshape(rows, 128)
 
 
-def relay(chunk, mine, x, theirs, out):
+def relay(chunk, mine, x, theirs, out, squares):
     rows = mine.shape[0]
     width = x.shape[2] - 128
     out[:, : 2 * chunk] = (mine[...] + theirs[:, : 2 * chunk].astype(F32)).astype(BF16)
-    squares = join3(x[:, :, width:].reshape(rows, 128)) + join3(theirs[:, 2 * chunk :])
-    out[:, 2 * chunk :] = split3(squares)
-
-
-def activate(chunk, mine, x, near, far, out):
-    rows = mine.shape[0]
-    width = x.shape[2] - 128
-    squares = (
-        join3(x[:, :, width:].reshape(rows, 128))
-        + join3(near[:, 2 * chunk :])
-        + join3(far[:, 2 * chunk :])
-    )
+    both = join3(x[:, :, width:].reshape(rows, 128)) + join3(theirs[:, 2 * chunk :])
+    squares[...] = jnp.broadcast_to(both, squares.shape)
+    out[:, 2 * chunk :] = split3(both)
+
+
+def activate(chunk, mine, squares, near, far, out):
+    squares = squares[:, :1] + join3(far[:, 2 * chunk :])
     scale = lax.rsqrt(squares / D + 1e-06)
     for s, n in tiles(chunk, 384):
         gate, up = (
@@ -274,20 +292,18 @@
         functools.partial(attend, attn, rows, heads, hd, length),
         "attend",
         [(block, BF16)] * attn,
-        [lengths, query.reshape(rows, heads, hd), cache],
+        [pltpu.with_memory_space_constraint(v, pltpu.HBM) for v in (lengths, query, cache)],
         [
             pltpu.VMEM(cache.shape, BF16),
-            pltpu.SemaphoreType.DMA((rows,)),
+            pltpu.SMEM((rows,), jnp.int32),
+            pltpu.VMEM(query.shape, BF16),
+            pltpu.VMEM((hd // 128, heads * rows, 128), F32),
+            pltpu.SemaphoreType.DMA((rows + 2,)),
             pltpu.VMEM((rows, attn, per, hd), BF16),
         ],
-        specs=[
-            pl.BlockSpec(memory_space=pltpu.SMEM),
-            VM,
-            pl.BlockSpec(memory_space=pltpu.HBM),
-        ],
-        flops=4 * rows * heads * length * hd,
-        moved=cache.size * 2,
-        limit=16,
+        specs=[pl.BlockSpec(memory_space=pltpu.HBM)] * 3,
+        flops=int(ATTEND_US * US),
+        limit=7,
     )
     parts = [parts[0]] + [swap(parts[k], "attn", k) for k in range(1, attn)]
     (mine,) = call(functools.partial(pack, attn), "pack", [((attn, *block), BF16)], parts)
@@ -306,8 +322,7 @@
             pltpu.VMEM((attn, own_rows, width), F32),
         ],
         [out_weight],
-        flops=2 * total * out_weight.size,
-        moved=out_weight.size * 2,
+        flops=int(PROJECT_US * US),
     )
     came = [swap(sends[k - 1], "attn", k) for k in range(1, attn)]
     state, xg = call(
@@ -315,6 +330,7 @@
         "settle",
         [((own_rows, width), F32), ((own_rows, width + 128), BF16)],
         [own, *came, norm_gain.reshape(1, width)],
+        flops=int(SETTLE_US * US),
     )
     xs = [xg] + [swap(xg, "attn", k) for k in range(1, attn)]
     (x,) = call(
@@ -322,41 +338,42 @@
         "gather_rows",
         [((attn, own_rows, width + 128), BF16)],
         xs,
-    )
-
-    def part(j, name, wide):
-        shape = ((total, 2 * chunk), F32) if wide else ((total, 2 * chunk + 128), BF16)
+        flops=int(GATHER_US * US),
+    )
+
+    def part(j, name, kind, after=(), more=0):
+        shape = ((total, 2 * chunk + more), kind)
         return call(
             functools.partial(hidden, j, ffn, chunk),
             name,
             [shape],
-            [x],
+            [x, *after],
             weights=[w_gate, w_up],
-            flops=4 * total * width * chunk,
-            moved=4 * width * chunk,
+            specs=[VM] + [ANY] * len(after),
+            flops=int(HIDDEN_US * US),
         )[0]
 
-    far_beside = swap(part(3, "hidden_diagonal", False), "ffn", 1)
-    far_mine = part(2, "hidden_across", True)
-    (far,) = call(
+    far_beside = swap(part(3, "hidden_diagonal", BF16, more=128), "ffn", 1)
+    far_mine = part(2, "hidden_across", F32)
+    far, squares = call(
         functools.partial(relay, chunk),
         "relay",
-        [((total, 2 * chunk + 128), BF16)],
+        [((total, 2 * chunk + 128), BF16), ((total, 128), F32)],
         [far_mine, x, far_beside],
     )
     far_came = swap(far, "ffn", 2)
-    near_came = swap(part(1, "hidden_beside", False), "ffn", 1)
-    near_mine = part(0, "hidden_own", True)
+    near_came = swap(part(1, "hidden_beside", BF16, [far]), "ffn", 1)
+    near_mine = part(0, "hidden_own", F32, [far])
     (active,) = call(
         functools.partial(activate, chunk),
         "activate",
         [((total, chunk), BF16)],
-        [near_mine, x, near_came, far_came],
+        [near_mine, squares, near_came, far_came],
+        flops=int(ACTIVATE_US * US),
     )
 
     active_across = swap(active, "ffn", 2)
     active_beside = swap(active, "ffn", 1)
-    active_diagonal = swap(active_across, "ffn", 1)
 
     def fold(j, name, value, acc, last=False):
         ins = [value] if acc is None else [value, acc]
@@ -372,12 +389,13 @@
             ins,
             scratch,
             weights=[w_down],
-            flops=2 * total * width * chunk,
-            moved=2 * width * chunk,
+            flops=int(DOWN_US * US),
         )
 
     (acc,) = fold(0, "down_own", active, None)
     (acc,) = fold(1, "down_beside", active_beside, acc)
+    active_across, acc = lax.optimization_barrier((active_across, acc))
+    active_diagonal = swap(active_across, "ffn", 1)
     (acc,) = fold(2, "down_across", active_across, acc)
     *sends, own = fold(3, "down_diagonal", active_diagonal, acc, True)
     came = [swap(sends[k - 1], "attn", k) for k in range(1, attn)]

time: 101 us -> 73.6 us (0.73)
  local copies, waits for them, and re-layouts: 28.7 us -> 1.59 us
  waiting for transfers between devices: 31.4 us -> 29.7 us
    unnamed x25 -> x30, local copies, waits for them, and re-layouts: 28 us -> 1.59 us
    ppermute x21, waiting for transfers between devices: 31.4 us -> 29.7 us  [swap(): return lax.ppermute(x, axis, [(i, i ^ step) for i in range(count)])]
  transfers between devices with their start and end apart: 21 -> 21, of which waited for: 10 -> 15; matrix products, arithmetic and copies ran while one was open for 1% -> 0% of each run, Pallas kernels for 7% -> 9%
where the time goes in v2:
time: 73.6 us; the launch traced here: 73.5 us
  waiting for transfers between devices  29.7 us (40%)
  starting transfers between devices  24.1 us (33%)
  Pallas kernels  17.8 us (24%)
  local copies, waits for them, and re-layouts  1.59 us (2%)
    ppermute x21, waiting for transfers between devices, swap(): return lax.ppermute(x, axis, [(i, i ^ step) for i in range(count)])  29.7 us
    ppermute x21, starting transfers between devices, swap(): return lax.ppermute(x, axis, [(i, i ^ step) for i in range(count)])  24.1 us
    pallas_call x16, Pallas kernels, call(): pl.pallas_call(kernel, out_shape=[jax.ShapeDtypeStruct(s, t) for s, t in...  17.8 us
    unnamed x30, local copies, waits for them, and re-layouts  1.59 us
  transfers between devices with their start and end apart: 21, of which 15 were waited for; matrix products, arithmetic and copies ran while one was open for 0% of the time, Pallas kernels for 9%

profile of v2, /device:TPU:0, one launch (start us, length us, event | category | flops | bytes accessed | tf_op | source)
XLA Modules:
  0.0 73.5 jit_solution(17121053687529012013)
XLA Ops:
  0.0 4.5 %attend.1 = (bf16[4,16,256]{2,1,0:T(8,128)(2,1)S(1)}, bf16[4,16,256]{2,1,0:T(8,128)(2,1)S(1)}, bf16[4,16,256]{2,1,0:T(8,128)(2,1)S(1)}, bf16[4,16,256]{2,1,0:T(8,128)(2,1)S(1)}) custom-call(s32[4]{0:T(128)} %lens_any.1, bf16[4,16384]{1,0:T(4,128)(2,1)} %q_any.1, bf16[4,1024,512]{2,1,0:T(8,128)(2,1)} %cache.1), custom_call_target="tpu_custom_call" | custom-call | flops 20000000000 | tf_op jit(solution)/shard_map/attend/pallas_call | solution.py:84
  4.5 3.1 %collective-permute-start = (bf16[4,16,256]{2,1,0:T(8,128)(2,1)S(1)}, bf16[4,16,256]{2,1,0:T(8,128)(2,1)S(1)}, u32[]{:S(2)}, u32[]{:S(2)}) collective-permute-start(bf16[4,16,256]{2,1,0:T(8,128)(2,1)S(1)} %get-tuple-element.24), channel_id=1, source_target_pairs={{0,4},{4,0},{8,12},{12,8},{1,5},{5,1},{9,13},{13,9},{2,6},{6,2},{1... | collective-permute-start | bytes 98312 | tf_op jit(solution)/shard_map/ppermute | solution.py:98
  7.7 2.6 %collective-permute-start.1 = (bf16[4,16,256]{2,1,0:T(8,128)(2,1)S(1)}, bf16[4,16,256]{2,1,0:T(8,128)(2,1)S(1)}, u32[]{:S(2)}, u32[]{:S(2)}) collective-permute-start(bf16[4,16,256]{2,1,0:T(8,128)(2,1)S(1)} %get-tuple-element.25), channel_id=1, source_target_pairs={{0,8},{4,12},{8,0},{12,4},{1,9},{5,13},{9,1},{13,5},{2,10},{6,14},... | collective-permute-start | bytes 98312 | tf_op jit(solution)/shard_map/ppermute | solution.py:98
  10.3 2.8 %collective-permute-done.1.refs_2_ = bf16[4,16,256]{2,1,0:T(8,128)(2,1)S(1)} collective-permute-done((bf16[4,16,256]{2,1,0:T(8,128)(2,1)S(1)}, bf16[4,16,256]{2,1,0:T(8,128)(2,1)S(1)}, u32[]{:S(2)}, u32[]{:S(2)}) %collective-permute-start.1) | collective-permute-done | bytes 32800 | tf_op jit(solution)/shard_map/ppermute | solution.py:98
  13.1 2.9 %collective-permute-done.2.refs_3_ = bf16[4,16,256]{2,1,0:T(8,128)(2,1)S(1)} collective-permute-done((bf16[4,16,256]{2,1,0:T(8,128)(2,1)S(1)}, bf16[4,16,256]{2,1,0:T(8,128)(2,1)S(1)}, u32[]{:S(2)}, u32[]{:S(2)}) %collective-permute-start.2) | collective-permute-done | bytes 32800 | tf_op jit(solution)/shard_map/ppermute | solution.py:98
  16.0 1.6 %collective-permute-start.4 = (bf16[4,4,16,256]{3,2,1,0:T(8,128)(2,1)S(1)}, bf16[4,4,16,256]{3,2,1,0:T(8,128)(2,1)S(1)}, u32[]{:S(2)}, u32[]{:S(2)}) collective-permute-start(bf16[4,4,16,256]{3,2,1,0:T(8,128)(2,1)S(1)} %pack.1.refs_0_), channel_id=1, source_target_pairs={{0,2},{1,3},{2,0},{3,1},{4,6},{5,7},{6,4},{7,5},{8,10},{9,11},{10,... | collective-permute-start | bytes 393224 | tf_op jit(solution)/shard_map/ppermute | solution.py:98
  17.6 3.5 %collective-permute-done.4.refs_2_ = bf16[4,4,16,256]{3,2,1,0:T(8,128)(2,1)S(1)} collective-permute-done((bf16[4,4,16,256]{3,2,1,0:T(8,128)(2,1)S(1)}, bf16[4,4,16,256]{3,2,1,0:T(8,128)(2,1)S(1)}, u32[]{:S(2)}, u32[]{:S(2)}) %collective-permute-start.4) | collective-permute-done | bytes 131104 | tf_op jit(solution)/shard_map/ppermute | solution.py:98
  22.4 2.9 %project.1 = (bf16[16,1792]{1,0:T(8,128)(2,1)S(1)}, bf16[16,1792]{1,0:T(8,128)(2,1)S(1)}, bf16[16,1792]{1,0:T(8,128)(2,1)S(1)}, f32[16,1792]{1,0:T(8,128)S(1)}) custom-call(bf16[4,4,16,256]{3,2,1,0:T(8,128)(2,1)S(1)} %pack.1.refs_0_, bf16[4,4,16,256]{3,2,1,0:T(8,128)(2,1)S(1)} %collective-permute-done.3.refs_1_, ...), custom_call_target="tpu_custom_call" | custom-call | flops 3000000000 | tf_op jit(solution)/shard_map/project/pallas_call | solution.py:84
  26.3 3.5 %collective-permute-start.8 = (bf16[16,1792]{1,0:T(8,128)(2,1)S(1)}, bf16[16,1792]{1,0:T(8,128)(2,1)S(1)}, u32[]{:S(2)}, u32[]{:S(2)}) collective-permute-start(bf16[16,1792]{1,0:T(8,128)(2,1)S(1)} %get-tuple-element.30), channel_id=1, source_target_pairs={{0,12},{4,8},{8,4},{12,0},{1,13},{5,9},{9,5},{13,1},{2,14},{6,10},... | collective-permute-start | bytes 172040 | tf_op jit(solution)/shard_map/ppermute | solution.py:98
  30.4 3.0 %collective-permute-done.7.refs_2_ = bf16[16,1792]{1,0:T(8,128)(2,1)S(1)} collective-permute-done((bf16[16,1792]{1,0:T(8,128)(2,1)S(1)}, bf16[16,1792]{1,0:T(8,128)(2,1)S(1)}, u32[]{:S(2)}, u32[]{:S(2)}) %collective-permute-start.7) | collective-permute-done | bytes 57376 | tf_op jit(solution)/shard_map/ppermute | solution.py:98
  34.8 1.7 %collective-permute-start.10 = (bf16[16,1920]{1,0:T(8,128)(2,1)S(1)}, bf16[16,1920]{1,0:T(8,128)(2,1)S(1)}, u32[]{:S(2)}, u32[]{:S(2)}) collective-permute-start(bf16[16,1920]{1,0:T(8,128)(2,1)S(1)} %get-tuple-element.32.refs_0_), channel_id=1, source_target_pairs={{0,8},{4,12},{8,0},{12,4},{1,9},{5,13},{9,1},{13,5},{2,10},{6,14},... | collective-permute-start | bytes 184328 | tf_op jit(solution)/shard_map/ppermute | solution.py:98
  38.5 2.4 %collective-permute-done.10.refs_2_ = bf16[16,1920]{1,0:T(8,128)(2,1)S(1)} collective-permute-done((bf16[16,1920]{1,0:T(8,128)(2,1)S(1)}, bf16[16,1920]{1,0:T(8,128)(2,1)S(1)}, u32[]{:S(2)}, u32[]{:S(2)}) %collective-permute-start.10) | collective-permute-done | bytes 61472 | tf_op jit(solution)/shard_map/ppermute | solution.py:98
  40.8 1.7 %collective-permute-done.11.refs_3_ = bf16[16,1920]{1,0:T(8,128)(2,1)S(1)} collective-permute-done((bf16[16,1920]{1,0:T(8,128)(2,1)S(1)}, bf16[16,1920]{1,0:T(8,128)(2,1)S(1)}, u32[]{:S(2)}, u32[]{:S(2)}) %collective-permute-start.11) | collective-permute-done | bytes 61472 | tf_op jit(solution)/shard_map/ppermute | solution.py:98
  42.6 1.6 %hidden_diagonal.1 = bf16[64,2432]{1,0:T(8,128)(2,1)S(1)} custom-call(bf16[4,16,1920]{2,1,0:T(8,128)(2,1)S(1)} %gather_rows.1.refs_0_.x, bf16[1792,4608]{1,0:T(8,128)(2,1)S(1)} %bitcast.1, bf16[1792,4608]{1,0:T(8,128)(2,1)S(1)} %bitcast.3), custom_call_target="tpu_custom_call" | custom-call | flops 1500000000 | tf_op jit(solution)/shard_map/hidden_diagonal/pallas_call | solution.py:84
  44.3 1.6 %hidden_across.1.mine = f32[64,2304]{1,0:T(8,128)S(1)} custom-call(bf16[4,16,1920]{2,1,0:T(8,128)(2,1)S(1)} %gather_rows.1.refs_0_.x, bf16[1792,4608]{1,0:T(8,128)(2,1)S(1)} %bitcast.1, bf16[1792,4608]{1,0:T(8,128)(2,1)S(1)} %bitcast.3), custom_call_target="tpu_custom_call" | custom-call | flops 1500000000 | tf_op jit(solution)/shard_map/hidden_across/pallas_call | solution.py:84
  46.1 1.5 %collective-permute-start.14 = (bf16[64,2432]{1,0:T(8,128)(2,1)S(1)}, bf16[64,2432]{1,0:T(8,128)(2,1)S(1)}, u32[]{:S(2)}, u32[]{:S(2)}) collective-permute-start(bf16[64,2432]{1,0:T(8,128)(2,1)S(1)} %get-tuple-element.33.refs_1_), channel_id=1, source_target_pairs={{0,2},{1,3},{2,0},{3,1},{4,6},{5,7},{6,4},{7,5},{8,10},{9,11},{10,... | collective-permute-start | bytes 933896 | tf_op jit(solution)/shard_map/ppermute | solution.py:98
  47.7 1.6 %hidden_beside.1 = bf16[64,2304]{1,0:T(8,128)(2,1)S(1)} custom-call(bf16[4,16,1920]{2,1,0:T(8,128)(2,1)S(1)} %gather_rows.1.refs_0_.x, bf16[64,2432]{1,0:T(8,128)(2,1)S(1)} %get-tuple-element.33.refs_1_, bf16[1792,4608]{1,0:T(8,128)(2,1)S(1)} %bitcast.1, bf16[1792,4608]{1,0:T(8,128)(2,1)S(1)} %bitcast.3), custom_call_target="tpu_custom_call" | custom-call | flops 1500000000 | tf_op jit(solution)/shard_map/hidden_beside/pallas_call | solution.py:84
  49.5 1.6 %hidden_own.1.mine = f32[64,2304]{1,0:T(8,128)S(1)} custom-call(bf16[4,16,1920]{2,1,0:T(8,128)(2,1)S(1)} %gather_rows.1.refs_0_.x, bf16[64,2432]{1,0:T(8,128)(2,1)S(1)} %get-tuple-element.33.refs_1_, bf16[1792,4608]{1,0:T(8,128)(2,1)S(1)} %bitcast.1, bf16[1792,4608]{1,0:T(8,128)(2,1)S(1)} %bitcast.3), custom_call_target="tpu_custom_call" | custom-call | flops 1500000000 | tf_op jit(solution)/shard_map/hidden_own/pallas_call | solution.py:84
  51.1 4.8 %collective-permute-done.14.far = bf16[64,2432]{1,0:T(8,128)(2,1)S(1)} collective-permute-done((bf16[64,2432]{1,0:T(8,128)(2,1)S(1)}, bf16[64,2432]{1,0:T(8,128)(2,1)S(1)}, u32[]{:S(2)}, u32[]{:S(2)}) %collective-permute-start.14) | collective-permute-done | bytes 311328 | tf_op jit(solution)/shard_map/ppermute | solution.py:98
  56.3 1.6 %collective-permute-start.15 = (bf16[64,1152]{1,0:T(8,128)(2,1)S(1)}, bf16[64,1152]{1,0:T(8,128)(2,1)S(1)}, u32[]{:S(2)}, u32[]{:S(2)}) collective-permute-start(bf16[64,1152]{1,0:T(8,128)(2,1)S(1)} %activate.1.refs_0_), channel_id=1, source_target_pairs={{0,2},{1,3},{2,0},{3,1},{4,6},{5,7},{6,4},{7,5},{8,10},{9,11},{10,... | collective-permute-start | bytes 442376 | tf_op jit(solution)/shard_map/ppermute | solution.py:98
  60.8 1.8 %collective-permute-done.15.refs_0_ = bf16[64,1152]{1,0:T(8,128)(2,1)S(1)} collective-permute-done((bf16[64,1152]{1,0:T(8,128)(2,1)S(1)}, bf16[64,1152]{1,0:T(8,128)(2,1)S(1)}, u32[]{:S(2)}, u32[]{:S(2)}) %collective-permute-start.15) | collective-permute-done | bytes 147488 | tf_op jit(solution)/shard_map/ppermute | solution.py:98
  64.7 2.0 %collective-permute-start.19 = (bf16[16,1792]{1,0:T(8,128)(2,1)S(1)}, bf16[16,1792]{1,0:T(8,128)(2,1)S(1)}, u32[]{:S(2)}, u32[]{:S(2)}) collective-permute-start(bf16[16,1792]{1,0:T(8,128)(2,1)S(1)} %get-tuple-element.39), channel_id=1, source_target_pairs={{0,8},{4,12},{8,0},{12,4},{1,9},{5,13},{9,1},{13,5},{2,10},{6,14},... | collective-permute-start | bytes 172040 | tf_op jit(solution)/shard_map/ppermute | solution.py:98
  66.8 2.3 %collective-permute-start.20 = (bf16[16,1792]{1,0:T(8,128)(2,1)S(1)}, bf16[16,1792]{1,0:T(8,128)(2,1)S(1)}, u32[]{:S(2)}, u32[]{:S(2)}) collective-permute-start(bf16[16,1792]{1,0:T(8,128)(2,1)S(1)} %get-tuple-element.40), channel_id=1, source_target_pairs={{0,12},{4,8},{8,4},{12,0},{1,13},{5,9},{9,5},{13,1},{2,14},{6,10},... | collective-permute-start | bytes 172040 | tf_op jit(solution)/shard_map/ppermute | solution.py:98
  69.7 2.4 %collective-permute-done.19.refs_3_ = bf16[16,1792]{1,0:T(8,128)(2,1)S(1)} collective-permute-done((bf16[16,1792]{1,0:T(8,128)(2,1)S(1)}, bf16[16,1792]{1,0:T(8,128)(2,1)S(1)}, u32[]{:S(2)}, u32[]{:S(2)}) %collective-permute-start.19) | collective-permute-done | bytes 57376 | tf_op jit(solution)/shard_map/ppermute | solution.py:98
  (68 shorter events, 14.3 us)
Async XLA Ops:
  0.0 42.5 %slice-start.4 = ((s8[16515072]{0:T(1024)(128)(4,1)}), s8[4194304]{0:T(1024)(128)(4,1)S(1)}, s32[]{:S(2)}) async-start(s8[16515072]{0:T(1024)(128)(4,1)} %bitcast.2), calls=%async_computation.4 | async-start | bytes 8388608
  0.0 42.5 %slice-start.5 = ((s8[16515072]{0:T(1024)(128)(4,1)}), s8[4194304]{0:T(1024)(128)(4,1)S(1)}, s32[]{:S(2)}) async-start(s8[16515072]{0:T(1024)(128)(4,1)} %bitcast.2), calls=%async_computation.5 | async-start | bytes 8388608
  0.0 42.5 %slice-start.6 = ((s8[16515072]{0:T(1024)(128)(4,1)}), s8[4194304]{0:T(1024)(128)(4,1)S(1)}, s32[]{:S(2)}) async-start(s8[16515072]{0:T(1024)(128)(4,1)} %bitcast.2), calls=%async_computation.6 | async-start | bytes 8388608
  4.5 5.7 %collective-permute-start = (bf16[4,16,256]{2,1,0:T(8,128)(2,1)S(1)}, bf16[4,16,256]{2,1,0:T(8,128)(2,1)S(1)}, u32[]{:S(2)}, u32[]{:S(2)}) collective-permute-start(bf16[4,16,256]{2,1,0:T(8,128)(2,1)S(1)} %get-tuple-element.24), channel_id=1, source_target_pairs={{0,4},{4,0},{8,12},{12,8},{1,5},{5,1},{9,13},{13,9},{2,6},{6,2},{1... | collective-permute-start | bytes 98312 | tf_op jit(solution)/shard_map/ppermute | solution.py:98
  7.7 5.4 %collective-permute-start.1 = (bf16[4,16,256]{2,1,0:T(8,128)(2,1)S(1)}, bf16[4,16,256]{2,1,0:T(8,128)(2,1)S(1)}, u32[]{:S(2)}, u32[]{:S(2)}) collective-permute-start(bf16[4,16,256]{2,1,0:T(8,128)(2,1)S(1)} %get-tuple-element.25), channel_id=1, source_target_pairs={{0,8},{4,12},{8,0},{12,4},{1,9},{5,13},{9,1},{13,5},{2,10},{6,14},... | collective-permute-start | bytes 98312 | tf_op jit(solution)/shard_map/ppermute | solution.py:98
  10.2 5.7 %collective-permute-start.2 = (bf16[4,16,256]{2,1,0:T(8,128)(2,1)S(1)}, bf16[4,16,256]{2,1,0:T(8,128)(2,1)S(1)}, u32[]{:S(2)}, u32[]{:S(2)}) collective-permute-start(bf16[4,16,256]{2,1,0:T(8,128)(2,1)S(1)} %get-tuple-element.26), channel_id=1, source_target_pairs={{0,12},{4,8},{8,4},{12,0},{1,13},{5,9},{9,5},{13,1},{2,14},{6,10},... | collective-permute-start | bytes 98312 | tf_op jit(solution)/shard_map/ppermute | solution.py:98
  16.0 5.0 %collective-permute-start.4 = (bf16[4,4,16,256]{3,2,1,0:T(8,128)(2,1)S(1)}, bf16[4,4,16,256]{3,2,1,0:T(8,128)(2,1)S(1)}, u32[]{:S(2)}, u32[]{:S(2)}) collective-permute-start(bf16[4,4,16,256]{3,2,1,0:T(8,128)(2,1)S(1)} %pack.1.refs_0_), channel_id=1, source_target_pairs={{0,2},{1,3},{2,0},{3,1},{4,6},{5,7},{6,4},{7,5},{8,10},{9,11},{10,... | collective-permute-start | bytes 393224 | tf_op jit(solution)/shard_map/ppermute | solution.py:98
  17.6 3.5 %collective-permute-start.3 = (bf16[4,4,16,256]{3,2,1,0:T(8,128)(2,1)S(1)}, bf16[4,4,16,256]{3,2,1,0:T(8,128)(2,1)S(1)}, u32[]{:S(2)}, u32[]{:S(2)}) collective-permute-start(bf16[4,4,16,256]{3,2,1,0:T(8,128)(2,1)S(1)} %pack.1.refs_0_), channel_id=1, source_target_pairs={{0,1},{1,0},{2,3},{3,2},{4,5},{5,4},{6,7},{7,6},{8,9},{9,8},{10,11... | collective-permute-start | bytes 393224 | tf_op jit(solution)/shard_map/ppermute | solution.py:98
  21.1 1.3 %collective-permute-start.5 = (bf16[4,4,16,256]{3,2,1,0:T(8,128)(2,1)S(1)}, bf16[4,4,16,256]{3,2,1,0:T(8,128)(2,1)S(1)}, u32[]{:S(2)}, u32[]{:S(2)}) collective-permute-start(bf16[4,4,16,256]{3,2,1,0:T(8,128)(2,1)S(1)} %collective-permute-done.4.refs_2_), channel_id=1, source_target_pairs={{0,1},{1,0},{2,3},{3,2},{4,5},{5,4},{6,7},{7,6},{8,9},{9,8},{10,11... | collective-permute-start | bytes 393224 | tf_op jit(solution)/shard_map/ppermute | solution.py:98
  25.3 5.1 %collective-permute-start.6 = (bf16[16,1792]{1,0:T(8,128)(2,1)S(1)}, bf16[16,1792]{1,0:T(8,128)(2,1)S(1)}, u32[]{:S(2)}, u32[]{:S(2)}) collective-permute-start(bf16[16,1792]{1,0:T(8,128)(2,1)S(1)} %get-tuple-element.28), channel_id=1, source_target_pairs={{0,4},{4,0},{8,12},{12,8},{1,5},{5,1},{9,13},{13,9},{2,6},{6,2},{1... | collective-permute-start | bytes 172040 | tf_op jit(solution)/shard_map/ppermute | solution.py:98
  25.4 8.0 %collective-permute-start.7 = (bf16[16,1792]{1,0:T(8,128)(2,1)S(1)}, bf16[16,1792]{1,0:T(8,128)(2,1)S(1)}, u32[]{:S(2)}, u32[]{:S(2)}) collective-permute-start(bf16[16,1792]{1,0:T(8,128)(2,1)S(1)} %get-tuple-element.29), channel_id=1, source_target_pairs={{0,8},{4,12},{8,0},{12,4},{1,9},{5,13},{9,1},{13,5},{2,10},{6,14},... | collective-permute-start | bytes 172040 | tf_op jit(solution)/shard_map/ppermute | solution.py:98
  26.3 7.1 %collective-permute-start.8 = (bf16[16,1792]{1,0:T(8,128)(2,1)S(1)}, bf16[16,1792]{1,0:T(8,128)(2,1)S(1)}, u32[]{:S(2)}, u32[]{:S(2)}) collective-permute-start(bf16[16,1792]{1,0:T(8,128)(2,1)S(1)} %get-tuple-element.30), channel_id=1, source_target_pairs={{0,12},{4,8},{8,4},{12,0},{1,13},{5,9},{9,5},{13,1},{2,14},{6,10},... | collective-permute-start | bytes 172040 | tf_op jit(solution)/shard_map/ppermute | solution.py:98
  33.5 4.9 %collective-permute-start.9 = (bf16[16,1920]{1,0:T(8,128)(2,1)S(1)}, bf16[16,1920]{1,0:T(8,128)(2,1)S(1)}, u32[]{:S(2)}, u32[]{:S(2)}) collective-permute-start(bf16[16,1920]{1,0:T(8,128)(2,1)S(1)} %get-tuple-element.32.refs_0_), channel_id=1, source_target_pairs={{0,4},{4,0},{8,12},{12,8},{1,5},{5,1},{9,13},{13,9},{2,6},{6,2},{1... | collective-permute-start | bytes 184328 | tf_op jit(solution)/shard_map/ppermute | solution.py:98
  34.8 6.1 %collective-permute-start.10 = (bf16[16,1920]{1,0:T(8,128)(2,1)S(1)}, bf16[16,1920]{1,0:T(8,128)(2,1)S(1)}, u32[]{:S(2)}, u32[]{:S(2)}) collective-permute-start(bf16[16,1920]{1,0:T(8,128)(2,1)S(1)} %get-tuple-element.32.refs_0_), channel_id=1, source_target_pairs={{0,8},{4,12},{8,0},{12,4},{1,9},{5,13},{9,1},{13,5},{2,10},{6,14},... | collective-permute-start | bytes 184328 | tf_op jit(solution)/shard_map/ppermute | solution.py:98
  36.5 6.0 %collective-permute-start.11 = (bf16[16,1920]{1,0:T(8,128)(2,1)S(1)}, bf16[16,1920]{1,0:T(8,128)(2,1)S(1)}, u32[]{:S(2)}, u32[]{:S(2)}) collective-permute-start(bf16[16,1920]{1,0:T(8,128)(2,1)S(1)} %get-tuple-element.32.refs_0_), channel_id=1, source_target_pairs={{0,12},{4,8},{8,4},{12,0},{1,13},{5,9},{9,5},{13,1},{2,14},{6,10},... | collective-permute-start | bytes 184328 | tf_op jit(solution)/shard_map/ppermute | solution.py:98
  44.2 1.7 %collective-permute-start.12 = (bf16[64,2432]{1,0:T(8,128)(2,1)S(1)}, bf16[64,2432]{1,0:T(8,128)(2,1)S(1)}, u32[]{:S(2)}, u32[]{:S(2)}) collective-permute-start(bf16[64,2432]{1,0:T(8,128)(2,1)S(1)} %hidden_diagonal.1), channel_id=1, source_target_pairs={{0,1},{1,0},{2,3},{3,2},{4,5},{5,4},{6,7},{7,6},{8,9},{9,8},{10,11... | collective-permute-start | bytes 933896 | tf_op jit(solution)/shard_map/ppermute | solution.py:98
  46.1 9.8 %collective-permute-start.14 = (bf16[64,2432]{1,0:T(8,128)(2,1)S(1)}, bf16[64,2432]{1,0:T(8,128)(2,1)S(1)}, u32[]{:S(2)}, u32[]{:S(2)}) collective-permute-start(bf16[64,2432]{1,0:T(8,128)(2,1)S(1)} %get-tuple-element.33.refs_1_), channel_id=1, source_target_pairs={{0,2},{1,3},{2,0},{3,1},{4,6},{5,7},{6,4},{7,5},{8,10},{9,11},{10,... | collective-permute-start | bytes 933896 | tf_op jit(solution)/shard_map/ppermute | solution.py:98
  49.2 1.8 %collective-permute-start.13 = (bf16[64,2304]{1,0:T(8,128)(2,1)S(1)}, bf16[64,2304]{1,0:T(8,128)(2,1)S(1)}, u32[]{:S(2)}, u32[]{:S(2)}) collective-permute-start(bf16[64,2304]{1,0:T(8,128)(2,1)S(1)} %hidden_beside.1), channel_id=1, source_target_pairs={{0,1},{1,0},{2,3},{3,2},{4,5},{5,4},{6,7},{7,6},{8,9},{9,8},{10,11... | collective-permute-start | bytes 884744 | tf_op jit(solution)/shard_map/ppermute | solution.py:98
  56.2 3.9 %collective-permute-start.16 = (bf16[64,1152]{1,0:T(8,128)(2,1)S(1)}, bf16[64,1152]{1,0:T(8,128)(2,1)S(1)}, u32[]{:S(2)}, u32[]{:S(2)}) collective-permute-start(bf16[64,1152]{1,0:T(8,128)(2,1)S(1)} %activate.1.refs_0_), channel_id=1, source_target_pairs={{0,1},{1,0},{2,3},{3,2},{4,5},{5,4},{6,7},{7,6},{8,9},{9,8},{10,11... | collective-permute-start | bytes 442376 | tf_op jit(solution)/shard_map/ppermute | solution.py:98
  56.3 6.3 %collective-permute-start.15 = (bf16[64,1152]{1,0:T(8,128)(2,1)S(1)}, bf16[64,1152]{1,0:T(8,128)(2,1)S(1)}, u32[]{:S(2)}, u32[]{:S(2)}) collective-permute-start(bf16[64,1152]{1,0:T(8,128)(2,1)S(1)} %activate.1.refs_0_), channel_id=1, source_target_pairs={{0,2},{1,3},{2,0},{3,1},{4,6},{5,7},{6,4},{7,5},{8,10},{9,11},{10,... | collective-permute-start | bytes 442376 | tf_op jit(solution)/shard_map/ppermute | solution.py:98
  62.6 1.4 %collective-permute-start.17 = (bf16[64,1152]{1,0:T(8,128)(2,1)S(1)}, bf16[64,1152]{1,0:T(8,128)(2,1)S(1)}, u32[]{:S(2)}, u32[]{:S(2)}) collective-permute-start(bf16[64,1152]{1,0:T(8,128)(2,1)S(1)} %collective-permute-done.15.refs_0_), channel_id=1, source_target_pairs={{0,1},{1,0},{2,3},{3,2},{4,5},{5,4},{6,7},{7,6},{8,9},{9,8},{10,11... | collective-permute-start | bytes 442376 | tf_op jit(solution)/shard_map/ppermute | solution.py:98
  64.7 5.1 %collective-permute-start.18 = (bf16[16,1792]{1,0:T(8,128)(2,1)S(1)}, bf16[16,1792]{1,0:T(8,128)(2,1)S(1)}, u32[]{:S(2)}, u32[]{:S(2)}) collective-permute-start(bf16[16,1792]{1,0:T(8,128)(2,1)S(1)} %get-tuple-element.38), channel_id=1, source_target_pairs={{0,4},{4,0},{8,12},{12,8},{1,5},{5,1},{9,13},{13,9},{2,6},{6,2},{1... | collective-permute-start | bytes 172040 | tf_op jit(solution)/shard_map/ppermute | solution.py:98
  64.7 7.4 %collective-permute-start.19 = (bf16[16,1792]{1,0:T(8,128)(2,1)S(1)}, bf16[16,1792]{1,0:T(8,128)(2,1)S(1)}, u32[]{:S(2)}, u32[]{:S(2)}) collective-permute-start(bf16[16,1792]{1,0:T(8,128)(2,1)S(1)} %get-tuple-element.39), channel_id=1, source_target_pairs={{0,8},{4,12},{8,0},{12,4},{1,9},{5,13},{9,1},{13,5},{2,10},{6,14},... | collective-permute-start | bytes 172040 | tf_op jit(solution)/shard_map/ppermute | solution.py:98
  66.8 6.0 %collective-permute-start.20 = (bf16[16,1792]{1,0:T(8,128)(2,1)S(1)}, bf16[16,1792]{1,0:T(8,128)(2,1)S(1)}, u32[]{:S(2)}, u32[]{:S(2)}) collective-permute-start(bf16[16,1792]{1,0:T(8,128)(2,1)S(1)} %get-tuple-element.40), channel_id=1, source_target_pairs={{0,12},{4,8},{8,4},{12,0},{1,13},{5,9},{9,5},{13,1},{2,14},{6,10},... | collective-permute-start | bytes 172040 | tf_op jit(solution)/shard_map/ppermute | solution.py:98
  (12 other events, 195.0 us)

commit v3 on v2

--- a/solution.py
+++ b/solution.py
@@ -98,6 +98,14 @@
     return lax.ppermute(x, axis, [(i, i ^ step) for i in range(count)])
 
 
+def spread(blocks, axis):
+    return [swap(blocks[k], axis, k) for k in reversed(range(1, len(blocks)))]
+
+
+def partners(count):
+    return [0, *reversed(range(1, count))]
+
+
 def tiles(width, tile=256):
     return [(s, min(tile, width - s)) for s in range(0, width, tile)]
 
@@ -133,6 +141,7 @@
             qs[c, h * rows : (h + 1) * rows, :] = query[:, s : s + 128].astype(F32)
     position = lax.broadcasted_iota(jnp.int32, (1, length), 1)
     per = heads // attn
+    scores = []
     for r in range(rows):
         copies[r].wait()
         q = jnp.concatenate(
@@ -141,7 +150,8 @@
         s = lax.dot_general(
             q, kv[r, :, :hd], (((1,), (1,)), ((), ())), preferred_element_type=F32
         ) * hd ** (-0.5)
-        s = jnp.where(position < lens[r], s, -jnp.inf)
+        scores.append(jnp.where(position < lens[r], s, -jnp.inf))
+    for r, s in enumerate(scores):
         p = jnp.exp(s - jnp.max(s, axis=1, keepdims=True))
         p = (p * (1.0 / jnp.sum(p, axis=1, keepdims=True))).astype(BF16)
         o = jnp.dot(p, kv[r, :, hd:], preferred_element_type=F32).astype(BF16)
@@ -154,8 +164,8 @@
 def pack(attn, *refs):
     out = refs[attn]
     me = lax.axis_index("attn")
-    for k in range(attn):
-        out[me ^ k] = refs[k][...]
+    for ref, k in zip(refs, partners(attn)):
+        out[me ^ k] = ref[...]
 
 
 def project(attn, ffn, rows, per, hd, *refs):
@@ -196,8 +206,8 @@
 def gather_rows(attn, *refs):
     x = refs[attn]
     a = lax.axis_index("attn")
-    for k in range(attn):
-        x[a ^ k] = refs[k][...]
+    for ref, k in zip(refs, partners(attn)):
+        x[a ^ k] = ref[...]
 
 
 def hidden(j, ffn, chunk, *refs):
@@ -305,7 +315,7 @@
         flops=int(ATTEND_US * US),
         limit=7,
     )
-    parts = [parts[0]] + [swap(parts[k], "attn", k) for k in range(1, attn)]
+    parts = [parts[0], *spread(parts, "attn")]
     (mine,) = call(functools.partial(pack, attn), "pack", [((attn, *block), BF16)], parts)
     across = swap(mine, "ffn", 2)
     beside = swap(mine, "ffn", 1)
@@ -324,7 +334,7 @@
         [out_weight],
         flops=int(PROJECT_US * US),
     )
-    came = [swap(sends[k - 1], "attn", k) for k in range(1, attn)]
+    came = spread([None, *sends], "attn")
     state, xg = call(
         functools.partial(settle, attn),
         "settle",
@@ -332,7 +342,7 @@
         [own, *came, norm_gain.reshape(1, width)],
         flops=int(SETTLE_US * US),
     )
-    xs = [xg] + [swap(xg, "attn", k) for k in range(1, attn)]
+    xs = [xg, *spread([xg] * attn, "attn")]
     (x,) = call(
         functools.partial(gather_rows, attn),
         "gather_rows",
@@ -398,7 +408,7 @@
     active_diagonal = swap(active_across, "ffn", 1)
     (acc,) = fold(2, "down_across", active_across, acc)
     *sends, own = fold(3, "down_diagonal", active_diagonal, acc, True)
-    came = [swap(sends[k - 1], "attn", k) for k in range(1, attn)]
+    came = spread([None, *sends], "attn")
     (mixed,) = call(
         functools.partial(finish, attn),
         "finish",

time: 73.6 us -> 70.5 us (0.958)
  waiting for transfers between devices: 29.7 us -> 27.8 us
  Pallas kernels: 17.8 us -> 16.5 us
    ppermute x21, waiting for transfers between devices: 29.7 us -> 27.8 us  [swap(): return lax.ppermute(x, axis, [(i, i ^ step) for i in range(count)])]
    pallas_call x16, Pallas kernels: 17.8 us -> 16.5 us  [call(): pl.pallas_call(kernel, out_shape=[jax.ShapeDtypeStruct(s, t) for s, t in...]
  transfers between devices with their start and end apart: 21 -> 21, of which waited for: 15 -> 13; matrix products, arithmetic and copies ran while one was open for 0% -> 0% of each run, Pallas kernels for 9% -> 10%
where the time goes in v3:
time: 70.5 us; the launch traced here: 70.4 us
  waiting for transfers between devices  27.8 us (39%)
  starting transfers between devices  24.2 us (34%)
  Pallas kernels  16.5 us (23%)
  local copies, waits for them, and re-layouts  1.6 us (2%)
    ppermute x21, waiting for transfers between devices, swap(): return lax.ppermute(x, axis, [(i, i ^ step) for i in range(count)])  27.8 us
    ppermute x21, starting transfers between devices, swap(): return lax.ppermute(x, axis, [(i, i ^ step) for i in range(count)])  24.2 us
    pallas_call x16, Pallas kernels, call(): pl.pallas_call(kernel, out_shape=[jax.ShapeDtypeStruct(s, t) for s, t in...  16.5 us
    unnamed x30, local copies, waits for them, and re-layouts  1.59 us
  transfers between devices with their start and end apart: 21, of which 13 were waited for; matrix products, arithmetic and copies ran while one was open for 0% of the time, Pallas kernels for 10%

profile of v3, /device:TPU:0, one launch (start us, length us, event | category | flops | bytes accessed | tf_op | source)
XLA Modules:
  0.0 70.4 jit_solution(15393083826066975136)
XLA Ops:
  0.0 3.2 %attend.1 = (bf16[4,16,256]{2,1,0:T(8,128)(2,1)S(1)}, bf16[4,16,256]{2,1,0:T(8,128)(2,1)S(1)}, bf16[4,16,256]{2,1,0:T(8,128)(2,1)S(1)}, bf16[4,16,256]{2,1,0:T(8,128)(2,1)S(1)}) custom-call(s32[4]{0:T(128)} %lens_any.1, bf16[4,16384]{1,0:T(4,128)(2,1)} %q_any.1, bf16[4,1024,512]{2,1,0:T(8,128)(2,1)} %cache.1), custom_call_target="tpu_custom_call" | custom-call | flops 20000000000 | tf_op jit(solution)/shard_map/attend/pallas_call | solution.py:84
  3.3 5.1 %collective-permute-start = (bf16[4,16,256]{2,1,0:T(8,128)(2,1)S(1)}, bf16[4,16,256]{2,1,0:T(8,128)(2,1)S(1)}, u32[]{:S(2)}, u32[]{:S(2)}) collective-permute-start(bf16[4,16,256]{2,1,0:T(8,128)(2,1)S(1)} %get-tuple-element.24), channel_id=1, source_target_pairs={{0,12},{4,8},{8,4},{12,0},{1,13},{5,9},{9,5},{13,1},{2,14},{6,10},... | collective-permute-start | bytes 98312 | tf_op jit(solution)/shard_map/ppermute | solution.py:98
  10.3 2.9 %collective-permute-done.1.refs_2_ = bf16[4,16,256]{2,1,0:T(8,128)(2,1)S(1)} collective-permute-done((bf16[4,16,256]{2,1,0:T(8,128)(2,1)S(1)}, bf16[4,16,256]{2,1,0:T(8,128)(2,1)S(1)}, u32[]{:S(2)}, u32[]{:S(2)}) %collective-permute-start.1) | collective-permute-done | bytes 32800 | tf_op jit(solution)/shard_map/ppermute | solution.py:98
  13.3 1.6 %collective-permute-start.4 = (bf16[4,4,16,256]{3,2,1,0:T(8,128)(2,1)S(1)}, bf16[4,4,16,256]{3,2,1,0:T(8,128)(2,1)S(1)}, u32[]{:S(2)}, u32[]{:S(2)}) collective-permute-start(bf16[4,4,16,256]{3,2,1,0:T(8,128)(2,1)S(1)} %pack.1.refs_0_), channel_id=1, source_target_pairs={{0,2},{1,3},{2,0},{3,1},{4,6},{5,7},{6,4},{7,5},{8,10},{9,11},{10,... | collective-permute-start | bytes 393224 | tf_op jit(solution)/shard_map/ppermute | solution.py:98
  14.8 3.5 %collective-permute-done.4.refs_2_ = bf16[4,4,16,256]{3,2,1,0:T(8,128)(2,1)S(1)} collective-permute-done((bf16[4,4,16,256]{3,2,1,0:T(8,128)(2,1)S(1)}, bf16[4,4,16,256]{3,2,1,0:T(8,128)(2,1)S(1)}, u32[]{:S(2)}, u32[]{:S(2)}) %collective-permute-start.4) | collective-permute-done | bytes 131104 | tf_op jit(solution)/shard_map/ppermute | solution.py:98
  19.7 2.9 %project.1 = (bf16[16,1792]{1,0:T(8,128)(2,1)S(1)}, bf16[16,1792]{1,0:T(8,128)(2,1)S(1)}, bf16[16,1792]{1,0:T(8,128)(2,1)S(1)}, f32[16,1792]{1,0:T(8,128)S(1)}) custom-call(bf16[4,4,16,256]{3,2,1,0:T(8,128)(2,1)S(1)} %pack.1.refs_0_, bf16[4,4,16,256]{3,2,1,0:T(8,128)(2,1)S(1)} %collective-permute-done.3.refs_1_, ...), custom_call_target="tpu_custom_call" | custom-call | flops 3000000000 | tf_op jit(solution)/shard_map/project/pallas_call | solution.py:84
  24.7 2.3 %collective-permute-start.8 = (bf16[16,1792]{1,0:T(8,128)(2,1)S(1)}, bf16[16,1792]{1,0:T(8,128)(2,1)S(1)}, u32[]{:S(2)}, u32[]{:S(2)}) collective-permute-start(bf16[16,1792]{1,0:T(8,128)(2,1)S(1)} %get-tuple-element.30), channel_id=1, source_target_pairs={{0,4},{4,0},{8,12},{12,8},{1,5},{5,1},{9,13},{13,9},{2,6},{6,2},{1... | collective-permute-start | bytes 172040 | tf_op jit(solution)/shard_map/ppermute | solution.py:98
  27.0 2.2 %collective-permute-done.6.refs_1_ = bf16[16,1792]{1,0:T(8,128)(2,1)S(1)} collective-permute-done((bf16[16,1792]{1,0:T(8,128)(2,1)S(1)}, bf16[16,1792]{1,0:T(8,128)(2,1)S(1)}, u32[]{:S(2)}, u32[]{:S(2)}) %collective-permute-start.6) | collective-permute-done | bytes 57376 | tf_op jit(solution)/shard_map/ppermute | solution.py:98
  29.2 1.7 %collective-permute-done.7.refs_2_ = bf16[16,1792]{1,0:T(8,128)(2,1)S(1)} collective-permute-done((bf16[16,1792]{1,0:T(8,128)(2,1)S(1)}, bf16[16,1792]{1,0:T(8,128)(2,1)S(1)}, u32[]{:S(2)}, u32[]{:S(2)}) %collective-permute-start.7) | collective-permute-done | bytes 57376 | tf_op jit(solution)/shard_map/ppermute | solution.py:98
  31.0 2.4 %collective-permute-start.9 = (bf16[16,1920]{1,0:T(8,128)(2,1)S(1)}, bf16[16,1920]{1,0:T(8,128)(2,1)S(1)}, u32[]{:S(2)}, u32[]{:S(2)}) collective-permute-start(bf16[16,1920]{1,0:T(8,128)(2,1)S(1)} %get-tuple-element.32.refs_0_), channel_id=1, source_target_pairs={{0,12},{4,8},{8,4},{12,0},{1,13},{5,9},{9,5},{13,1},{2,14},{6,10},... | collective-permute-start | bytes 184328 | tf_op jit(solution)/shard_map/ppermute | solution.py:98
  33.4 2.0 %collective-permute-start.11 = (bf16[16,1920]{1,0:T(8,128)(2,1)S(1)}, bf16[16,1920]{1,0:T(8,128)(2,1)S(1)}, u32[]{:S(2)}, u32[]{:S(2)}) collective-permute-start(bf16[16,1920]{1,0:T(8,128)(2,1)S(1)} %get-tuple-element.32.refs_0_), channel_id=1, source_target_pairs={{0,4},{4,0},{8,12},{12,8},{1,5},{5,1},{9,13},{13,9},{2,6},{6,2},{1... | collective-permute-start | bytes 184328 | tf_op jit(solution)/shard_map/ppermute | solution.py:98
  35.4 2.0 %collective-permute-done.9.refs_1_ = bf16[16,1920]{1,0:T(8,128)(2,1)S(1)} collective-permute-done((bf16[16,1920]{1,0:T(8,128)(2,1)S(1)}, bf16[16,1920]{1,0:T(8,128)(2,1)S(1)}, u32[]{:S(2)}, u32[]{:S(2)}) %collective-permute-start.9) | collective-permute-done | bytes 61472 | tf_op jit(solution)/shard_map/ppermute | solution.py:98
  37.5 1.8 %collective-permute-done.10.refs_2_ = bf16[16,1920]{1,0:T(8,128)(2,1)S(1)} collective-permute-done((bf16[16,1920]{1,0:T(8,128)(2,1)S(1)}, bf16[16,1920]{1,0:T(8,128)(2,1)S(1)}, u32[]{:S(2)}, u32[]{:S(2)}) %collective-permute-start.10) | collective-permute-done | bytes 61472 | tf_op jit(solution)/shard_map/ppermute | solution.py:98
  39.4 1.6 %hidden_diagonal.1 = bf16[64,2432]{1,0:T(8,128)(2,1)S(1)} custom-call(bf16[4,16,1920]{2,1,0:T(8,128)(2,1)S(1)} %gather_rows.1.refs_0_.x, bf16[1792,4608]{1,0:T(8,128)(2,1)S(1)} %bitcast.1, bf16[1792,4608]{1,0:T(8,128)(2,1)S(1)} %bitcast.3), custom_call_target="tpu_custom_call" | custom-call | flops 1500000000 | tf_op jit(solution)/shard_map/hidden_diagonal/pallas_call | solution.py:84
  41.1 1.6 %hidden_across.1.mine = f32[64,2304]{1,0:T(8,128)S(1)} custom-call(bf16[4,16,1920]{2,1,0:T(8,128)(2,1)S(1)} %gather_rows.1.refs_0_.x, bf16[1792,4608]{1,0:T(8,128)(2,1)S(1)} %bitcast.1, bf16[1792,4608]{1,0:T(8,128)(2,1)S(1)} %bitcast.3), custom_call_target="tpu_custom_call" | custom-call | flops 1500000000 | tf_op jit(solution)/shard_map/hidden_across/pallas_call | solution.py:84
  44.4 1.6 %hidden_beside.1 = bf16[64,2304]{1,0:T(8,128)(2,1)S(1)} custom-call(bf16[4,16,1920]{2,1,0:T(8,128)(2,1)S(1)} %gather_rows.1.refs_0_.x, bf16[64,2432]{1,0:T(8,128)(2,1)S(1)} %get-tuple-element.33.refs_1_, bf16[1792,4608]{1,0:T(8,128)(2,1)S(1)} %bitcast.1, bf16[1792,4608]{1,0:T(8,128)(2,1)S(1)} %bitcast.3), custom_call_target="tpu_custom_call" | custom-call | flops 1500000000 | tf_op jit(solution)/shard_map/hidden_beside/pallas_call | solution.py:84
  46.3 1.6 %hidden_own.1.mine = f32[64,2304]{1,0:T(8,128)S(1)} custom-call(bf16[4,16,1920]{2,1,0:T(8,128)(2,1)S(1)} %gather_rows.1.refs_0_.x, bf16[64,2432]{1,0:T(8,128)(2,1)S(1)} %get-tuple-element.33.refs_1_, bf16[1792,4608]{1,0:T(8,128)(2,1)S(1)} %bitcast.1, bf16[1792,4608]{1,0:T(8,128)(2,1)S(1)} %bitcast.3), custom_call_target="tpu_custom_call" | custom-call | flops 1500000000 | tf_op jit(solution)/shard_map/hidden_own/pallas_call | solution.py:84
  47.9 4.8 %collective-permute-done.14.far = bf16[64,2432]{1,0:T(8,128)(2,1)S(1)} collective-permute-done((bf16[64,2432]{1,0:T(8,128)(2,1)S(1)}, bf16[64,2432]{1,0:T(8,128)(2,1)S(1)}, u32[]{:S(2)}, u32[]{:S(2)}) %collective-permute-start.14) | collective-permute-done | bytes 311328 | tf_op jit(solution)/shard_map/ppermute | solution.py:98
  53.1 1.6 %collective-permute-start.15 = (bf16[64,1152]{1,0:T(8,128)(2,1)S(1)}, bf16[64,1152]{1,0:T(8,128)(2,1)S(1)}, u32[]{:S(2)}, u32[]{:S(2)}) collective-permute-start(bf16[64,1152]{1,0:T(8,128)(2,1)S(1)} %activate.1.refs_0_), channel_id=1, source_target_pairs={{0,2},{1,3},{2,0},{3,1},{4,6},{5,7},{6,4},{7,5},{8,10},{9,11},{10,... | collective-permute-start | bytes 442376 | tf_op jit(solution)/shard_map/ppermute | solution.py:98
  57.6 1.8 %collective-permute-done.15.refs_0_ = bf16[64,1152]{1,0:T(8,128)(2,1)S(1)} collective-permute-done((bf16[64,1152]{1,0:T(8,128)(2,1)S(1)}, bf16[64,1152]{1,0:T(8,128)(2,1)S(1)}, u32[]{:S(2)}, u32[]{:S(2)}) %collective-permute-start.15) | collective-permute-done | bytes 147488 | tf_op jit(solution)/shard_map/ppermute | solution.py:98
  61.4 2.2 %collective-permute-start.18 = (bf16[16,1792]{1,0:T(8,128)(2,1)S(1)}, bf16[16,1792]{1,0:T(8,128)(2,1)S(1)}, u32[]{:S(2)}, u32[]{:S(2)}) collective-permute-start(bf16[16,1792]{1,0:T(8,128)(2,1)S(1)} %get-tuple-element.38), channel_id=1, source_target_pairs={{0,12},{4,8},{8,4},{12,0},{1,13},{5,9},{9,5},{13,1},{2,14},{6,10},... | collective-permute-start | bytes 172040 | tf_op jit(solution)/shard_map/ppermute | solution.py:98
  63.7 2.2 %collective-permute-start.20 = (bf16[16,1792]{1,0:T(8,128)(2,1)S(1)}, bf16[16,1792]{1,0:T(8,128)(2,1)S(1)}, u32[]{:S(2)}, u32[]{:S(2)}) collective-permute-start(bf16[16,1792]{1,0:T(8,128)(2,1)S(1)} %get-tuple-element.40), channel_id=1, source_target_pairs={{0,4},{4,0},{8,12},{12,8},{1,5},{5,1},{9,13},{13,9},{2,6},{6,2},{1... | collective-permute-start | bytes 172040 | tf_op jit(solution)/shard_map/ppermute | solution.py:98
  65.9 2.1 %collective-permute-done.18.refs_2_ = bf16[16,1792]{1,0:T(8,128)(2,1)S(1)} collective-permute-done((bf16[16,1792]{1,0:T(8,128)(2,1)S(1)}, bf16[16,1792]{1,0:T(8,128)(2,1)S(1)}, u32[]{:S(2)}, u32[]{:S(2)}) %collective-permute-start.18) | collective-permute-done | bytes 57376 | tf_op jit(solution)/shard_map/ppermute | solution.py:98
  68.0 1.7 %collective-permute-done.19.refs_3_ = bf16[16,1792]{1,0:T(8,128)(2,1)S(1)} collective-permute-done((bf16[16,1792]{1,0:T(8,128)(2,1)S(1)}, bf16[16,1792]{1,0:T(8,128)(2,1)S(1)}, u32[]{:S(2)}, u32[]{:S(2)}) %collective-permute-start.19) | collective-permute-done | bytes 57376 | tf_op jit(solution)/shard_map/ppermute | solution.py:98
  (68 shorter events, 13.8 us)
Async XLA Ops:
  0.0 39.3 %slice-start.4 = ((s8[16515072]{0:T(1024)(128)(4,1)}), s8[4194304]{0:T(1024)(128)(4,1)S(1)}, s32[]{:S(2)}) async-start(s8[16515072]{0:T(1024)(128)(4,1)} %bitcast.2), calls=%async_computation.4 | async-start | bytes 8388608
  0.0 39.3 %slice-start.5 = ((s8[16515072]{0:T(1024)(128)(4,1)}), s8[4194304]{0:T(1024)(128)(4,1)S(1)}, s32[]{:S(2)}) async-start(s8[16515072]{0:T(1024)(128)(4,1)} %bitcast.2), calls=%async_computation.5 | async-start | bytes 8388608
  0.0 39.3 %slice-start.6 = ((s8[16515072]{0:T(1024)(128)(4,1)}), s8[4194304]{0:T(1024)(128)(4,1)S(1)}, s32[]{:S(2)}) async-start(s8[16515072]{0:T(1024)(128)(4,1)} %bitcast.2), calls=%async_computation.6 | async-start | bytes 8388608
  3.3 7.0 %collective-permute-start = (bf16[4,16,256]{2,1,0:T(8,128)(2,1)S(1)}, bf16[4,16,256]{2,1,0:T(8,128)(2,1)S(1)}, u32[]{:S(2)}, u32[]{:S(2)}) collective-permute-start(bf16[4,16,256]{2,1,0:T(8,128)(2,1)S(1)} %get-tuple-element.24), channel_id=1, source_target_pairs={{0,12},{4,8},{8,4},{12,0},{1,13},{5,9},{9,5},{13,1},{2,14},{6,10},... | collective-permute-start | bytes 98312 | tf_op jit(solution)/shard_map/ppermute | solution.py:98
  8.4 4.8 %collective-permute-start.1 = (bf16[4,16,256]{2,1,0:T(8,128)(2,1)S(1)}, bf16[4,16,256]{2,1,0:T(8,128)(2,1)S(1)}, u32[]{:S(2)}, u32[]{:S(2)}) collective-permute-start(bf16[4,16,256]{2,1,0:T(8,128)(2,1)S(1)} %get-tuple-element.25), channel_id=1, source_target_pairs={{0,8},{4,12},{8,0},{12,4},{1,9},{5,13},{9,1},{13,5},{2,10},{6,14},... | collective-permute-start | bytes 98312 | tf_op jit(solution)/shard_map/ppermute | solution.py:98
  8.4 4.8 %collective-permute-start.2 = (bf16[4,16,256]{2,1,0:T(8,128)(2,1)S(1)}, bf16[4,16,256]{2,1,0:T(8,128)(2,1)S(1)}, u32[]{:S(2)}, u32[]{:S(2)}) collective-permute-start(bf16[4,16,256]{2,1,0:T(8,128)(2,1)S(1)} %get-tuple-element.26), channel_id=1, source_target_pairs={{0,4},{4,0},{8,12},{12,8},{1,5},{5,1},{9,13},{13,9},{2,6},{6,2},{1... | collective-permute-start | bytes 98312 | tf_op jit(solution)/shard_map/ppermute | solution.py:98
  13.3 5.0 %collective-permute-start.4 = (bf16[4,4,16,256]{3,2,1,0:T(8,128)(2,1)S(1)}, bf16[4,4,16,256]{3,2,1,0:T(8,128)(2,1)S(1)}, u32[]{:S(2)}, u32[]{:S(2)}) collective-permute-start(bf16[4,4,16,256]{3,2,1,0:T(8,128)(2,1)S(1)} %pack.1.refs_0_), channel_id=1, source_target_pairs={{0,2},{1,3},{2,0},{3,1},{4,6},{5,7},{6,4},{7,5},{8,10},{9,11},{10,... | collective-permute-start | bytes 393224 | tf_op jit(solution)/shard_map/ppermute | solution.py:98
  14.8 3.5 %collective-permute-start.3 = (bf16[4,4,16,256]{3,2,1,0:T(8,128)(2,1)S(1)}, bf16[4,4,16,256]{3,2,1,0:T(8,128)(2,1)S(1)}, u32[]{:S(2)}, u32[]{:S(2)}) collective-permute-start(bf16[4,4,16,256]{3,2,1,0:T(8,128)(2,1)S(1)} %pack.1.refs_0_), channel_id=1, source_target_pairs={{0,1},{1,0},{2,3},{3,2},{4,5},{5,4},{6,7},{7,6},{8,9},{9,8},{10,11... | collective-permute-start | bytes 393224 | tf_op jit(solution)/shard_map/ppermute | solution.py:98
  18.3 1.3 %collective-permute-start.5 = (bf16[4,4,16,256]{3,2,1,0:T(8,128)(2,1)S(1)}, bf16[4,4,16,256]{3,2,1,0:T(8,128)(2,1)S(1)}, u32[]{:S(2)}, u32[]{:S(2)}) collective-permute-start(bf16[4,4,16,256]{3,2,1,0:T(8,128)(2,1)S(1)} %collective-permute-done.4.refs_2_), channel_id=1, source_target_pairs={{0,1},{1,0},{2,3},{3,2},{4,5},{5,4},{6,7},{7,6},{8,9},{9,8},{10,11... | collective-permute-start | bytes 393224 | tf_op jit(solution)/shard_map/ppermute | solution.py:98
  22.6 6.6 %collective-permute-start.6 = (bf16[16,1792]{1,0:T(8,128)(2,1)S(1)}, bf16[16,1792]{1,0:T(8,128)(2,1)S(1)}, u32[]{:S(2)}, u32[]{:S(2)}) collective-permute-start(bf16[16,1792]{1,0:T(8,128)(2,1)S(1)} %get-tuple-element.28), channel_id=1, source_target_pairs={{0,12},{4,8},{8,4},{12,0},{1,13},{5,9},{9,5},{13,1},{2,14},{6,10},... | collective-permute-start | bytes 172040 | tf_op jit(solution)/shard_map/ppermute | solution.py:98
  24.1 6.8 %collective-permute-start.7 = (bf16[16,1792]{1,0:T(8,128)(2,1)S(1)}, bf16[16,1792]{1,0:T(8,128)(2,1)S(1)}, u32[]{:S(2)}, u32[]{:S(2)}) collective-permute-start(bf16[16,1792]{1,0:T(8,128)(2,1)S(1)} %get-tuple-element.29), channel_id=1, source_target_pairs={{0,8},{4,12},{8,0},{12,4},{1,9},{5,13},{9,1},{13,5},{2,10},{6,14},... | collective-permute-start | bytes 172040 | tf_op jit(solution)/shard_map/ppermute | solution.py:98
  24.7 6.1 %collective-permute-start.8 = (bf16[16,1792]{1,0:T(8,128)(2,1)S(1)}, bf16[16,1792]{1,0:T(8,128)(2,1)S(1)}, u32[]{:S(2)}, u32[]{:S(2)}) collective-permute-start(bf16[16,1792]{1,0:T(8,128)(2,1)S(1)} %get-tuple-element.30), channel_id=1, source_target_pairs={{0,4},{4,0},{8,12},{12,8},{1,5},{5,1},{9,13},{13,9},{2,6},{6,2},{1... | collective-permute-start | bytes 172040 | tf_op jit(solution)/shard_map/ppermute | solution.py:98
  31.0 6.5 %collective-permute-start.9 = (bf16[16,1920]{1,0:T(8,128)(2,1)S(1)}, bf16[16,1920]{1,0:T(8,128)(2,1)S(1)}, u32[]{:S(2)}, u32[]{:S(2)}) collective-permute-start(bf16[16,1920]{1,0:T(8,128)(2,1)S(1)} %get-tuple-element.32.refs_0_), channel_id=1, source_target_pairs={{0,12},{4,8},{8,4},{12,0},{1,13},{5,9},{9,5},{13,1},{2,14},{6,10},... | collective-permute-start | bytes 184328 | tf_op jit(solution)/shard_map/ppermute | solution.py:98
  33.4 5.9 %collective-permute-start.10 = (bf16[16,1920]{1,0:T(8,128)(2,1)S(1)}, bf16[16,1920]{1,0:T(8,128)(2,1)S(1)}, u32[]{:S(2)}, u32[]{:S(2)}) collective-permute-start(bf16[16,1920]{1,0:T(8,128)(2,1)S(1)} %get-tuple-element.32.refs_0_), channel_id=1, source_target_pairs={{0,8},{4,12},{8,0},{12,4},{1,9},{5,13},{9,1},{13,5},{2,10},{6,14},... | collective-permute-start | bytes 184328 | tf_op jit(solution)/shard_map/ppermute | solution.py:98
  33.4 5.9 %collective-permute-start.11 = (bf16[16,1920]{1,0:T(8,128)(2,1)S(1)}, bf16[16,1920]{1,0:T(8,128)(2,1)S(1)}, u32[]{:S(2)}, u32[]{:S(2)}) collective-permute-start(bf16[16,1920]{1,0:T(8,128)(2,1)S(1)} %get-tuple-element.32.refs_0_), channel_id=1, source_target_pairs={{0,4},{4,0},{8,12},{12,8},{1,5},{5,1},{9,13},{13,9},{2,6},{6,2},{1... | collective-permute-start | bytes 184328 | tf_op jit(solution)/shard_map/ppermute | solution.py:98
  41.0 1.7 %collective-permute-start.12 = (bf16[64,2432]{1,0:T(8,128)(2,1)S(1)}, bf16[64,2432]{1,0:T(8,128)(2,1)S(1)}, u32[]{:S(2)}, u32[]{:S(2)}) collective-permute-start(bf16[64,2432]{1,0:T(8,128)(2,1)S(1)} %hidden_diagonal.1), channel_id=1, source_target_pairs={{0,1},{1,0},{2,3},{3,2},{4,5},{5,4},{6,7},{7,6},{8,9},{9,8},{10,11... | collective-permute-start | bytes 933896 | tf_op jit(solution)/shard_map/ppermute | solution.py:98
  42.9 9.8 %collective-permute-start.14 = (bf16[64,2432]{1,0:T(8,128)(2,1)S(1)}, bf16[64,2432]{1,0:T(8,128)(2,1)S(1)}, u32[]{:S(2)}, u32[]{:S(2)}) collective-permute-start(bf16[64,2432]{1,0:T(8,128)(2,1)S(1)} %get-tuple-element.33.refs_1_), channel_id=1, source_target_pairs={{0,2},{1,3},{2,0},{3,1},{4,6},{5,7},{6,4},{7,5},{8,10},{9,11},{10,... | collective-permute-start | bytes 933896 | tf_op jit(solution)/shard_map/ppermute | solution.py:98
  46.0 1.8 %collective-permute-start.13 = (bf16[64,2304]{1,0:T(8,128)(2,1)S(1)}, bf16[64,2304]{1,0:T(8,128)(2,1)S(1)}, u32[]{:S(2)}, u32[]{:S(2)}) collective-permute-start(bf16[64,2304]{1,0:T(8,128)(2,1)S(1)} %hidden_beside.1), channel_id=1, source_target_pairs={{0,1},{1,0},{2,3},{3,2},{4,5},{5,4},{6,7},{7,6},{8,9},{9,8},{10,11... | collective-permute-start | bytes 884744 | tf_op jit(solution)/shard_map/ppermute | solution.py:98
  53.0 3.9 %collective-permute-start.16 = (bf16[64,1152]{1,0:T(8,128)(2,1)S(1)}, bf16[64,1152]{1,0:T(8,128)(2,1)S(1)}, u32[]{:S(2)}, u32[]{:S(2)}) collective-permute-start(bf16[64,1152]{1,0:T(8,128)(2,1)S(1)} %activate.1.refs_0_), channel_id=1, source_target_pairs={{0,1},{1,0},{2,3},{3,2},{4,5},{5,4},{6,7},{7,6},{8,9},{9,8},{10,11... | collective-permute-start | bytes 442376 | tf_op jit(solution)/shard_map/ppermute | solution.py:98
  53.1 6.3 %collective-permute-start.15 = (bf16[64,1152]{1,0:T(8,128)(2,1)S(1)}, bf16[64,1152]{1,0:T(8,128)(2,1)S(1)}, u32[]{:S(2)}, u32[]{:S(2)}) collective-permute-start(bf16[64,1152]{1,0:T(8,128)(2,1)S(1)} %activate.1.refs_0_), channel_id=1, source_target_pairs={{0,2},{1,3},{2,0},{3,1},{4,6},{5,7},{6,4},{7,5},{8,10},{9,11},{10,... | collective-permute-start | bytes 442376 | tf_op jit(solution)/shard_map/ppermute | solution.py:98
  59.3 1.4 %collective-permute-start.17 = (bf16[64,1152]{1,0:T(8,128)(2,1)S(1)}, bf16[64,1152]{1,0:T(8,128)(2,1)S(1)}, u32[]{:S(2)}, u32[]{:S(2)}) collective-permute-start(bf16[64,1152]{1,0:T(8,128)(2,1)S(1)} %collective-permute-done.15.refs_0_), channel_id=1, source_target_pairs={{0,1},{1,0},{2,3},{3,2},{4,5},{5,4},{6,7},{7,6},{8,9},{9,8},{10,11... | collective-permute-start | bytes 442376 | tf_op jit(solution)/shard_map/ppermute | solution.py:98
  61.4 6.6 %collective-permute-start.18 = (bf16[16,1792]{1,0:T(8,128)(2,1)S(1)}, bf16[16,1792]{1,0:T(8,128)(2,1)S(1)}, u32[]{:S(2)}, u32[]{:S(2)}) collective-permute-start(bf16[16,1792]{1,0:T(8,128)(2,1)S(1)} %get-tuple-element.38), channel_id=1, source_target_pairs={{0,12},{4,8},{8,4},{12,0},{1,13},{5,9},{9,5},{13,1},{2,14},{6,10},... | collective-permute-start | bytes 172040 | tf_op jit(solution)/shard_map/ppermute | solution.py:98
  63.7 6.1 %collective-permute-start.19 = (bf16[16,1792]{1,0:T(8,128)(2,1)S(1)}, bf16[16,1792]{1,0:T(8,128)(2,1)S(1)}, u32[]{:S(2)}, u32[]{:S(2)}) collective-permute-start(bf16[16,1792]{1,0:T(8,128)(2,1)S(1)} %get-tuple-element.39), channel_id=1, source_target_pairs={{0,8},{4,12},{8,0},{12,4},{1,9},{5,13},{9,1},{13,5},{2,10},{6,14},... | collective-permute-start | bytes 172040 | tf_op jit(solution)/shard_map/ppermute | solution.py:98
  63.7 6.1 %collective-permute-start.20 = (bf16[16,1792]{1,0:T(8,128)(2,1)S(1)}, bf16[16,1792]{1,0:T(8,128)(2,1)S(1)}, u32[]{:S(2)}, u32[]{:S(2)}) collective-permute-start(bf16[16,1792]{1,0:T(8,128)(2,1)S(1)} %get-tuple-element.40), channel_id=1, source_target_pairs={{0,4},{4,0},{8,12},{12,8},{1,5},{5,1},{9,13},{13,9},{2,6},{6,2},{1... | collective-permute-start | bytes 172040 | tf_op jit(solution)/shard_map/ppermute | solution.py:98
  (12 other events, 184.0 us)

commit v4 on v3

--- a/solution.py
+++ b/solution.py
@@ -12,12 +12,17 @@
 BF16 = jnp.bfloat16
 MIB = 1 << 20
 US = 10**9
+CUTS = 1
+STEPS = (2, 3, 1)
+HEADS_STEPS = STEPS
+ROWS_STEPS = STEPS
+END_STEPS = STEPS
 ATTEND_US = 20
 SETTLE_US = 3
 GATHER_US = 3
-ACTIVATE_US = 10
-HIDDEN_US = 1.5
-DOWN_US = 0.7
+ACTIVATE_US = 4
+OWN_US = 0.55
+DOWN_US = 0.05
 PROJECT_US = 3
 
 
@@ -98,12 +103,12 @@
     return lax.ppermute(x, axis, [(i, i ^ step) for i in range(count)])
 
 
-def spread(blocks, axis):
-    return [swap(blocks[k], axis, k) for k in reversed(range(1, len(blocks)))]
-
-
-def partners(count):
-    return [0, *reversed(range(1, count))]
+def spread(blocks, axis, steps=STEPS):
+    count = len(blocks)
+    return [
+        lax.ppermute(blocks[k], axis, [(i, (i + k) % count) for i in range(count)])
+        for k in steps
+    ]
 
 
 def tiles(width, tile=256):
@@ -127,11 +132,22 @@
 def attend(attn, rows, heads, hd, length, lens_any, q_any, cache, *refs):
     outs, (kv, lens, query, qs, sems, att) = refs[:attn], refs[attn:]
     first = [
-        pltpu.make_async_copy(q_any, query, sems.at[rows]),
-        pltpu.make_async_copy(lens_any, lens, sems.at[rows + 1]),
+        pltpu.make_async_copy(q_any, query, sems.at[rows * CUTS]),
+        pltpu.make_async_copy(lens_any, lens, sems.at[rows * CUTS + 1]),
     ]
-    copies = [pltpu.make_async_copy(cache.at[r], kv.at[r], sems.at[r]) for r in range(rows)]
-    for c in first + copies:
+    span = length // CUTS
+    copies = [
+        [
+            pltpu.make_async_copy(
+                cache.at[r, pl.ds(i * span, span)],
+                kv.at[r, pl.ds(i * span, span)],
+                sems.at[r * CUTS + i],
+            )
+            for i in range(CUTS)
+        ]
+        for r in range(rows)
+    ]
+    for c in first + sum(copies, []):
         c.start()
     for c in first:
         c.wait()
@@ -143,7 +159,8 @@
     per = heads // attn
     scores = []
     for r in range(rows):
-        copies[r].wait()
+        for c in copies[r]:
+            c.wait()
         q = jnp.concatenate(
             [qs[c, pl.ds(r, heads, stride=rows), :].astype(BF16) for c in range(hd // 128)], axis=1
         )
@@ -158,14 +175,14 @@
         att[r] = o.reshape(attn, per, hd)
     me = lax.axis_index("attn")
     for k in range(attn):
-        outs[k][...] = att[:, me ^ k]
+        outs[k][...] = att[:, (me + k) % attn]
 
 
 def pack(attn, *refs):
     out = refs[attn]
     me = lax.axis_index("attn")
-    for ref, k in zip(refs, partners(attn)):
-        out[me ^ k] = ref[...]
+    for ref, k in zip(refs, (0, *HEADS_STEPS)):
+        out[(me - k) % attn] = ref[...]
 
 
 def project(attn, ffn, rows, per, hd, *refs):
@@ -187,7 +204,7 @@
         y = jnp.dot(x[...], w[:, s : s + n], preferred_element_type=F32)
         res[:, :, s : s + n] = y.reshape(attn, ffn * rows, n)
     for k in range(1, attn):
-        sends[k - 1][...] = res[a ^ k].astype(BF16)
+        sends[k - 1][...] = res[(a + k) % attn].astype(BF16)
     own[...] = res[a] + resid[...].astype(F32)
 
 
@@ -206,77 +223,96 @@
 def gather_rows(attn, *refs):
     x = refs[attn]
     a = lax.axis_index("attn")
-    for ref, k in zip(refs, partners(attn)):
-        x[a ^ k] = ref[...]
-
-
-def hidden(j, ffn, chunk, *refs):
-    x, (wg, wu, out) = refs[0], refs[-3:]
-    start = (lax.axis_index("ffn") ^ j) * chunk
+    for ref, k in zip(refs, (0, *ROWS_STEPS)):
+        x[(a - k) % attn] = ref[...]
+
+
+def sums(x, wg, wu, start, cut, out):
     rows, width = x.shape[0] * x.shape[1], wg.shape[0]
     lhs = x[:, :, :width].reshape(rows, width)
-    whole = chunk // 256 * 256
+    whole = cut // 256 * 256
 
     def columns(w, s, n):
         return w[:, pl.ds(pl.multiple_of(start + s, 128), n)]
 
-    for base, w in ((0, wg), (chunk, wu)):
+    for base, w in ((0, wg), (cut, wu)):
         for s, n in tiles(whole):
             y = jnp.dot(lhs, columns(w, s, n), preferred_element_type=F32)
             out[:, base + s : base + s + n] = y.astype(out.dtype)
-    rest = chunk - whole
+    rest = cut - whole
     if rest:
         w = jnp.concatenate([columns(wg, whole, rest), columns(wu, whole, rest)], axis=1)
         y = jnp.dot(lhs, w, preferred_element_type=F32).astype(out.dtype)
-        out[:, whole:chunk] = y[:, :rest]
-        out[:, chunk + whole : 2 * chunk] = y[:, rest:]
-    if out.shape[1] > 2 * chunk:
-        out[:, 2 * chunk :] = x[:, :, width:].reshape(rows, 128)
-
-
-def relay(chunk, mine, x, theirs, out, squares):
+        out[:, whole:cut] = y[:, :rest]
+        out[:, cut + whole : 2 * cut] = y[:, rest:]
+    if out.shape[1] > 2 * cut:
+        out[:, 2 * cut :] = x[:, :, width:].reshape(rows, 128)
+
+
+def hidden(chunk, jobs, *refs):
+    x, (wg, wu) = refs[0], refs[-2 - len(jobs) : -len(jobs)]
+    f = lax.axis_index("ffn")
+    for (j, low, high), out in zip(jobs, refs[-len(jobs) :]):
+        sums(x, wg, wu, (f ^ j) * chunk + low, high - low, out)
+
+
+def relay(cut, mine, x, near, out, *squares):
     rows = mine.shape[0]
     width = x.shape[2] - 128
-    out[:, : 2 * chunk] = (mine[...] + theirs[:, : 2 * chunk].astype(F32)).astype(BF16)
-    both = join3(x[:, :, width:].reshape(rows, 128)) + join3(theirs[:, 2 * chunk :])
-    squares[...] = jnp.broadcast_to(both, squares.shape)
-    out[:, 2 * chunk :] = split3(both)
-
-
-def activate(chunk, mine, squares, near, far, out):
-    squares = squares[:, :1] + join3(far[:, 2 * chunk :])
-    scale = lax.rsqrt(squares / D + 1e-06)
-    for s, n in tiles(chunk, 384):
-        gate, up = (
-            (
-                mine[:, b : b + n] + near[:, b : b + n].astype(F32) + far[:, b : b + n].astype(F32)
-            )
-            * scale
-            for b in (s, chunk + s)
-        )
-        out[:, s : s + n] = (gate / (1.0 + jnp.exp(-gate)) * up).astype(BF16)
-
-
-def down(j, first, last, attn, chunk, *refs):
-    refs = list(refs)
-    active = refs.pop(0)
+    out[:, : 2 * cut] = (mine[...] + near[:, : 2 * cut].astype(F32)).astype(BF16)
+    if squares:
+        both = join3(x[:, :, width:].reshape(rows, 128)) + join3(near[:, 2 * cut :])
+        squares[0][...] = jnp.broadcast_to(both, squares[0].shape)
+        out[:, 2 * cut :] = split3(both)
+
+
+def activate(chunk, low, high, thirds, mine, *refs):
+    near, (far, squares, out, *scales) = refs[: len(thirds)], refs[len(thirds) :]
+    cut = high - low
+    if scales:
+        total = squares[:, :1] + join3(far[:, 2 * cut :])
+        scale = lax.rsqrt(total / D + 1e-06)
+        scales[0][...] = jnp.broadcast_to(scale, scales[0].shape)
+    else:
+        scale = squares[:, :1]
+
+    def value(s, up):
+        place, ref = next((c, r) for c, r in zip(thirds, near) if c[0] <= s < c[1])
+        n = s - place[0] + up * (place[1] - place[0])
+        m = s + up * chunk
+        c = s - low + up * cut
+        return (
+            mine[:, m : m + 128]
+            + ref[:, n : n + 128].astype(F32)
+            + far[:, c : c + 128].astype(F32)
+        ) * scale
+
+    for s in range(low, high, 128):
+        gate, up = value(s, 0), value(s, 1)
+        out[:, s - low : s - low + 128] = (gate / (1.0 + jnp.exp(-gate)) * up).astype(BF16)
+
+
+def down(chunk, jobs, first, last, attn, *refs):
+    values, refs = refs[: len(jobs)], list(refs[len(jobs) :])
     acc = None if first else refs.pop(0)
     w = refs.pop(0)
-    start = pl.multiple_of((lax.axis_index("ffn") ^ j) * chunk, chunk)
-    rows = active.shape[0]
-    a = lax.axis_index("attn")
+    f, a = lax.axis_index("ffn"), lax.axis_index("attn")
+    rows = values[0].shape[0]
     res = refs[-1]
     for s, n in tiles(w.shape[1]):
-        y = jnp.dot(active[...], w[pl.ds(start, chunk), s : s + n], preferred_element_type=F32)
-        if acc is not None:
-            y = y + acc[:, s : s + n]
+        y = None if first else acc[:, s : s + n]
+        for (j, low, high), value in zip(jobs, values):
+            start = pl.multiple_of((f ^ j) * chunk + low, 128)
+            part = w[pl.ds(start, high - low), s : s + n]
+            z = jnp.dot(value[...], part, preferred_element_type=F32)
+            y = z if y is None else y + z
         if last:
             res[:, :, s : s + n] = y.reshape(attn, rows // attn, n)
         else:
             res[:, s : s + n] = y
     if last:
         for k in range(1, attn):
-            refs[k - 1][...] = res[a ^ k].astype(BF16)
+            refs[k - 1][...] = res[(a + k) % attn].astype(BF16)
         refs[attn - 1][...] = res[a]
 
 
@@ -308,14 +344,14 @@
             pltpu.SMEM((rows,), jnp.int32),
             pltpu.VMEM(query.shape, BF16),
             pltpu.VMEM((hd // 128, heads * rows, 128), F32),
-            pltpu.SemaphoreType.DMA((rows + 2,)),
+            pltpu.SemaphoreType.DMA((rows * CUTS + 2,)),
             pltpu.VMEM((rows, attn, per, hd), BF16),
         ],
         specs=[pl.BlockSpec(memory_space=pltpu.HBM)] * 3,
         flops=int(ATTEND_US * US),
         limit=7,
     )
-    parts = [parts[0], *spread(parts, "attn")]
+    parts = [parts[0], *spread(parts, "attn", HEADS_STEPS)]
     (mine,) = call(functools.partial(pack, attn), "pack", [((attn, *block), BF16)], parts)
     across = swap(mine, "ffn", 2)
     beside = swap(mine, "ffn", 1)
@@ -342,7 +378,7 @@
         [own, *came, norm_gain.reshape(1, width)],
         flops=int(SETTLE_US * US),
     )
-    xs = [xg, *spread([xg] * attn, "attn")]
+    xs = [xg, *spread([xg] * attn, "attn", ROWS_STEPS)]
     (x,) = call(
         functools.partial(gather_rows, attn),
         "gather_rows",
@@ -351,64 +387,85 @@
         flops=int(GATHER_US * US),
     )
 
-    def part(j, name, kind, after=(), more=0):
-        shape = ((total, 2 * chunk + more), kind)
+    middle = (chunk // 128 * 5 + 8) // 9 * 128
+    cuts = [(0, middle), (middle, chunk)]
+
+    def part(jobs, name, kinds, after, more=0, cost=0.0):
+        columns = [2 * (high - low) + more for _, low, high in jobs]
         return call(
-            functools.partial(hidden, j, ffn, chunk),
+            functools.partial(hidden, chunk, jobs),
             name,
-            [shape],
+            [((total, n), kind) for n, kind in zip(columns, kinds)],
             [x, *after],
             weights=[w_gate, w_up],
             specs=[VM] + [ANY] * len(after),
-            flops=int(HIDDEN_US * US),
-        )[0]
-
-    far_beside = swap(part(3, "hidden_diagonal", BF16, more=128), "ffn", 1)
-    far_mine = part(2, "hidden_across", F32)
-    far, squares = call(
-        functools.partial(relay, chunk),
-        "relay",
-        [((total, 2 * chunk + 128), BF16), ((total, 128), F32)],
-        [far_mine, x, far_beside],
-    )
-    far_came = swap(far, "ffn", 2)
-    near_came = swap(part(1, "hidden_beside", BF16, [far]), "ffn", 1)
-    near_mine = part(0, "hidden_own", F32, [far])
-    (active,) = call(
-        functools.partial(activate, chunk),
-        "activate",
-        [((total, chunk), BF16)],
-        [near_mine, squares, near_came, far_came],
-        flops=int(ACTIVATE_US * US),
-    )
-
-    active_across = swap(active, "ffn", 2)
-    active_beside = swap(active, "ffn", 1)
-
-    def fold(j, name, value, acc, last=False):
-        ins = [value] if acc is None else [value, acc]
+            flops=int(cost * US),
+        )
+
+    others, after = [], []
+    for i, cut in enumerate(cuts):
+        after = part([(3, *cut)], "hidden_diagonal", [BF16], after, 128 if i == 0 else 0)
+        others.append(swap(after[0], "ffn", 1))
+    far = []
+    for i, cut in enumerate(cuts):
+        mine = part([(2, *cut)], "hidden_across", [F32], after)
+        more = 128 if i == 0 else 0
+        after = call(
+            functools.partial(relay, cut[1] - cut[0]),
+            "relay",
+            [((total, 2 * (cut[1] - cut[0]) + more), BF16)] + [((total, 128), F32)] * (i == 0),
+            [*mine, x, others[i]],
+        )
+        far.append(swap(after[0], "ffn", 2))
+        if i == 0:
+            squares = after[1]
+    third = chunk // 384 * 128
+    thirds = [(0, third), (third, 2 * third), (2 * third, chunk)]
+    near = part([(1, *cut) for cut in thirds], "hidden_beside", [BF16] * 3, after[:1])
+    (mine,) = part([(0, 0, chunk)], "hidden_own", [F32], near[:1], cost=OWN_US)
+    near = [swap(v, "ffn", 1) for v in near]
+
+    own, beside, across = [], [], []
+    for i, cut in enumerate(cuts):
+        active, *scales = call(
+            functools.partial(activate, chunk, *cut, thirds),
+            "activate",
+            [((total, cut[1] - cut[0]), BF16)] + [((total, 128), F32)] * (i == 0),
+            [mine, *near, far[i], squares],
+            flops=int(ACTIVATE_US * US * i),
+        )
+        if i == 0:
+            squares = scales[0]
+        own.append(active)
+        across.append(swap(active, "ffn", 2))
+        beside.append(swap(active, "ffn", 1))
+
+    def fold(jobs, values, acc, last=False):
         if last:
             outs = [((own_rows, width), BF16)] * (attn - 1) + [((own_rows, width), F32)]
             scratch = [pltpu.VMEM((attn, own_rows, width), F32)]
         else:
             outs, scratch = [((total, width), F32)], []
         return call(
-            functools.partial(down, j, acc is None, last, attn, chunk),
-            name,
+            functools.partial(down, chunk, jobs, acc is None, last, attn),
+            "down",
             outs,
-            ins,
+            [*values] if acc is None else [*values, acc],
             scratch,
             weights=[w_down],
             flops=int(DOWN_US * US),
         )
 
-    (acc,) = fold(0, "down_own", active, None)
-    (acc,) = fold(1, "down_beside", active_beside, acc)
-    active_across, acc = lax.optimization_barrier((active_across, acc))
-    active_diagonal = swap(active_across, "ffn", 1)
-    (acc,) = fold(2, "down_across", active_across, acc)
-    *sends, own = fold(3, "down_diagonal", active_diagonal, acc, True)
-    came = spread([None, *sends], "attn")
+    first, second = cuts
+    (acc,) = fold([(0, *first), (0, *second), (1, *first)], [*own, beside[0]], None)
+    across[0], acc = lax.optimization_barrier((across[0], acc))
+    diagonal = swap(across[0], "ffn", 1)
+    (acc,) = fold([(1, *second), (2, *first)], [beside[1], across[0]], acc)
+    across[1], acc = lax.optimization_barrier((across[1], acc))
+    ending = swap(across[1], "ffn", 1)
+    (acc,) = fold([(3, *first), (2, *second)], [diagonal, across[1]], acc)
+    *sends, own = fold([(3, *second)], [ending], acc, True)
+    came = spread([None, *sends], "attn", END_STEPS)
     (mixed,) = call(
         functools.partial(finish, attn),
         "finish",
@@ -424,7 +481,7 @@
     per = query.shape[1] // head_dim // attn
     fits = (
         ffn == 4
-        and attn == 4
+        and attn == len(STEPS) + 1
         and per % 16 == 0
         and head_dim % 128 == 0
         and resid.shape[0] % 16 == 0

time: 70.5 us -> 67.4 us (0.956)
  starting transfers between devices: 24.2 us -> 22.2 us
  local copies, waits for them, and re-layouts: 1.6 us -> 0.55 us
    ppermute x21 -> x16, waiting for transfers between devices: 27.8 us -> 6.38 us  [swap(): return lax.ppermute(x, axis, [(i, i ^ step) for i in range(count)])]
    ppermute x0 -> x12, waiting for transfers between devices: none -> 20.8 us  [spread(): lax.ppermute(blocks[k], axis, [(i, (i + k) % count) for i in range(count)])]
    ppermute x21 -> x16, starting transfers between devices: 24.2 us -> 8.62 us  [swap(): return lax.ppermute(x, axis, [(i, i ^ step) for i in range(count)])]
    ppermute x0 -> x12, starting transfers between devices: none -> 13.6 us  [spread(): lax.ppermute(blocks[k], axis, [(i, (i + k) % count) for i in range(count)])]
    unnamed x30, local copies, waits for them, and re-layouts: 1.59 us -> 0.55 us
    pallas_call x16 -> x20, Pallas kernels: 16.5 us -> 17.1 us  [call(): pl.pallas_call(kernel, out_shape=[jax.ShapeDtypeStruct(s, t) for s, t in...]
  transfers between devices with their start and end apart: 21 -> 28, of which waited for: 13 -> 15; matrix products, arithmetic and copies ran while one was open for 0% -> 0% of each run, Pallas kernels for 10% -> 13%
where the time goes in v4:
time: 67.4 us; the launch traced here: 67.3 us
  waiting for transfers between devices  27.1 us (40%)
  starting transfers between devices  22.2 us (33%)
  Pallas kernels  17.1 us (25%)
    ppermute x12, waiting for transfers between devices, spread(): lax.ppermute(blocks[k], axis, [(i, (i + k) % count) for i in range(count)])  20.8 us
    pallas_call x20, Pallas kernels, call(): pl.pallas_call(kernel, out_shape=[jax.ShapeDtypeStruct(s, t) for s, t in...  17.1 us
    ppermute x12, starting transfers between devices, spread(): lax.ppermute(blocks[k], axis, [(i, (i + k) % count) for i in range(count)])  13.6 us
    ppermute x16, starting transfers between devices, swap(): return lax.ppermute(x, axis, [(i, i ^ step) for i in range(count)])  8.62 us
    ppermute x16, waiting for transfers between devices, swap(): return lax.ppermute(x, axis, [(i, i ^ step) for i in range(count)])  6.38 us
  transfers between devices with their start and end apart: 28, of which 15 were waited for; matrix products, arithmetic and copies ran while one was open for 0% of the time, Pallas kernels for 13%

profile of v4, /device:TPU:0, one launch (start us, length us, event | category | flops | bytes accessed | tf_op | source)
XLA Modules:
  0.0 67.3 jit_solution(3459113303460774108)
XLA Ops:
  0.0 3.2 %attend.1 = (bf16[4,16,256]{2,1,0:T(8,128)(2,1)S(1)}, bf16[4,16,256]{2,1,0:T(8,128)(2,1)S(1)}, bf16[4,16,256]{2,1,0:T(8,128)(2,1)S(1)}, bf16[4,16,256]{2,1,0:T(8,128)(2,1)S(1)}) custom-call(s32[4]{0:T(128)} %lens_any.1, bf16[4,16384]{1,0:T(4,128)(2,1)} %q_any.1, bf16[4,1024,512]{2,1,0:T(8,128)(2,1)} %cache.1), custom_call_target="tpu_custom_call" | custom-call | flops 20000000000 | tf_op jit(solution)/shard_map/attend/pallas_call | solution.py:89
  3.3 4.1 %collective-permute-start = (bf16[4,16,256]{2,1,0:T(8,128)(2,1)S(1)}, bf16[4,16,256]{2,1,0:T(8,128)(2,1)S(1)}, u32[]{:S(2)}, u32[]{:S(2)}) collective-permute-start(bf16[4,16,256]{2,1,0:T(8,128)(2,1)S(1)} %get-tuple-element.31), channel_id=1, source_target_pairs={{0,8},{4,12},{8,0},{12,4},{1,9},{5,13},{9,1},{13,5},{2,10},{6,14},... | collective-permute-start | bytes 98312 | tf_op jit(solution)/shard_map/ppermute | solution.py:109
  7.4 1.3 %collective-permute-start.1 = (bf16[4,16,256]{2,1,0:T(8,128)(2,1)S(1)}, bf16[4,16,256]{2,1,0:T(8,128)(2,1)S(1)}, u32[]{:S(2)}, u32[]{:S(2)}) collective-permute-start(bf16[4,16,256]{2,1,0:T(8,128)(2,1)S(1)} %get-tuple-element.32), channel_id=1, source_target_pairs={{0,12},{4,0},{8,4},{12,8},{1,13},{5,1},{9,5},{13,9},{2,14},{6,2},{... | collective-permute-start | bytes 98312 | tf_op jit(solution)/shard_map/ppermute | solution.py:109
  9.7 1.6 %collective-permute-done.1.refs_2_ = bf16[4,16,256]{2,1,0:T(8,128)(2,1)S(1)} collective-permute-done((bf16[4,16,256]{2,1,0:T(8,128)(2,1)S(1)}, bf16[4,16,256]{2,1,0:T(8,128)(2,1)S(1)}, u32[]{:S(2)}, u32[]{:S(2)}) %collective-permute-start.1) | collective-permute-done | bytes 32800 | tf_op jit(solution)/shard_map/ppermute | solution.py:109
  11.3 3.1 %collective-permute-done.2.refs_3_ = bf16[4,16,256]{2,1,0:T(8,128)(2,1)S(1)} collective-permute-done((bf16[4,16,256]{2,1,0:T(8,128)(2,1)S(1)}, bf16[4,16,256]{2,1,0:T(8,128)(2,1)S(1)}, u32[]{:S(2)}, u32[]{:S(2)}) %collective-permute-start.2) | collective-permute-done | bytes 32800 | tf_op jit(solution)/shard_map/ppermute | solution.py:109
  14.5 1.6 %collective-permute-start.4 = (bf16[4,4,16,256]{3,2,1,0:T(8,128)(2,1)S(1)}, bf16[4,4,16,256]{3,2,1,0:T(8,128)(2,1)S(1)}, u32[]{:S(2)}, u32[]{:S(2)}) collective-permute-start(bf16[4,4,16,256]{3,2,1,0:T(8,128)(2,1)S(1)} %pack.1.refs_0_), channel_id=1, source_target_pairs={{0,2},{1,3},{2,0},{3,1},{4,6},{5,7},{6,4},{7,5},{8,10},{9,11},{10,... | collective-permute-start | bytes 393224 | tf_op jit(solution)/shard_map/ppermute | solution.py:103
  16.1 3.5 %collective-permute-done.4.refs_2_ = bf16[4,4,16,256]{3,2,1,0:T(8,128)(2,1)S(1)} collective-permute-done((bf16[4,4,16,256]{3,2,1,0:T(8,128)(2,1)S(1)}, bf16[4,4,16,256]{3,2,1,0:T(8,128)(2,1)S(1)}, u32[]{:S(2)}, u32[]{:S(2)}) %collective-permute-start.4) | collective-permute-done | bytes 131104 | tf_op jit(solution)/shard_map/ppermute | solution.py:103
  19.5 1.3 %collective-permute-done.5.refs_3_ = bf16[4,4,16,256]{3,2,1,0:T(8,128)(2,1)S(1)} collective-permute-done((bf16[4,4,16,256]{3,2,1,0:T(8,128)(2,1)S(1)}, bf16[4,4,16,256]{3,2,1,0:T(8,128)(2,1)S(1)}, u32[]{:S(2)}, u32[]{:S(2)}) %collective-permute-start.5) | collective-permute-done | bytes 131104 | tf_op jit(solution)/shard_map/ppermute | solution.py:103
  20.9 2.9 %project.1 = (bf16[16,1792]{1,0:T(8,128)(2,1)S(1)}, bf16[16,1792]{1,0:T(8,128)(2,1)S(1)}, bf16[16,1792]{1,0:T(8,128)(2,1)S(1)}, f32[16,1792]{1,0:T(8,128)S(1)}) custom-call(bf16[4,4,16,256]{3,2,1,0:T(8,128)(2,1)S(1)} %pack.1.refs_0_, bf16[4,4,16,256]{3,2,1,0:T(8,128)(2,1)S(1)} %collective-permute-done.3.refs_1_, ...), custom_call_target="tpu_custom_call" | custom-call | flops 3000000000 | tf_op jit(solution)/shard_map/project/pallas_call | solution.py:89
  23.9 1.2 %collective-permute-start.7 = (bf16[16,1792]{1,0:T(8,128)(2,1)S(1)}, bf16[16,1792]{1,0:T(8,128)(2,1)S(1)}, u32[]{:S(2)}, u32[]{:S(2)}) collective-permute-start(bf16[16,1792]{1,0:T(8,128)(2,1)S(1)} %get-tuple-element.36), channel_id=1, source_target_pairs={{0,12},{4,0},{8,4},{12,8},{1,13},{5,1},{9,5},{13,9},{2,14},{6,2},{... | collective-permute-start | bytes 172040 | tf_op jit(solution)/shard_map/ppermute | solution.py:109
  26.0 3.4 %collective-permute-done.6.refs_1_ = bf16[16,1792]{1,0:T(8,128)(2,1)S(1)} collective-permute-done((bf16[16,1792]{1,0:T(8,128)(2,1)S(1)}, bf16[16,1792]{1,0:T(8,128)(2,1)S(1)}, u32[]{:S(2)}, u32[]{:S(2)}) %collective-permute-start.6) | collective-permute-done | bytes 57376 | tf_op jit(solution)/shard_map/ppermute | solution.py:109
  29.4 1.8 %collective-permute-done.8.refs_3_ = bf16[16,1792]{1,0:T(8,128)(2,1)S(1)} collective-permute-done((bf16[16,1792]{1,0:T(8,128)(2,1)S(1)}, bf16[16,1792]{1,0:T(8,128)(2,1)S(1)}, u32[]{:S(2)}, u32[]{:S(2)}) %collective-permute-start.8) | collective-permute-done | bytes 57376 | tf_op jit(solution)/shard_map/ppermute | solution.py:109
  31.9 1.8 %collective-permute-start.10 = (bf16[16,1920]{1,0:T(8,128)(2,1)S(1)}, bf16[16,1920]{1,0:T(8,128)(2,1)S(1)}, u32[]{:S(2)}, u32[]{:S(2)}) collective-permute-start(bf16[16,1920]{1,0:T(8,128)(2,1)S(1)} %get-tuple-element.39.refs_0_), channel_id=1, source_target_pairs={{0,12},{4,0},{8,4},{12,8},{1,13},{5,1},{9,5},{13,9},{2,14},{6,2},{... | collective-permute-start | bytes 184328 | tf_op jit(solution)/shard_map/ppermute | solution.py:109
  33.9 3.5 %collective-permute-done.9.refs_1_ = bf16[16,1920]{1,0:T(8,128)(2,1)S(1)} collective-permute-done((bf16[16,1920]{1,0:T(8,128)(2,1)S(1)}, bf16[16,1920]{1,0:T(8,128)(2,1)S(1)}, u32[]{:S(2)}, u32[]{:S(2)}) %collective-permute-start.9) | collective-permute-done | bytes 61472 | tf_op jit(solution)/shard_map/ppermute | solution.py:109
  37.5 2.2 %collective-permute-done.11.refs_3_ = bf16[16,1920]{1,0:T(8,128)(2,1)S(1)} collective-permute-done((bf16[16,1920]{1,0:T(8,128)(2,1)S(1)}, bf16[16,1920]{1,0:T(8,128)(2,1)S(1)}, u32[]{:S(2)}, u32[]{:S(2)}) %collective-permute-start.11) | collective-permute-done | bytes 61472 | tf_op jit(solution)/shard_map/ppermute | solution.py:109
  43.3 1.6 %collective-permute-start.18 = (bf16[64,1408]{1,0:T(8,128)(2,1)S(1)}, bf16[64,1408]{1,0:T(8,128)(2,1)S(1)}, u32[]{:S(2)}, u32[]{:S(2)}) collective-permute-start(bf16[64,1408]{1,0:T(8,128)(2,1)S(1)} %get-tuple-element.40.refs_1_), channel_id=1, source_target_pairs={{0,2},{1,3},{2,0},{3,1},{4,6},{5,7},{6,4},{7,5},{8,10},{9,11},{10,... | collective-permute-start | bytes 540680 | tf_op jit(solution)/shard_map/ppermute | solution.py:103
  46.2 1.6 %hidden_beside.1 = (bf16[64,768]{1,0:T(8,128)(2,1)S(1)}, bf16[64,768]{1,0:T(8,128)(2,1)S(1)}, bf16[64,768]{1,0:T(8,128)(2,1)S(1)}) custom-call(bf16[4,16,1920]{2,1,0:T(8,128)(2,1)S(1)} %gather_rows.1.refs_0_.x, bf16[64,1024]{1,0:T(8,128)(2,1)S(1)} %relay.3.refs_1_, bf16[1792,4608]{1,0:T(8,128)(2,1)S(1)} %bitcast.1, bf16[1792,4608]{1,0:T(8,128)(2,1)S(1)} %bitcast.3), custom_call_target="tpu_custom_call" | custom-call | tf_op jit(solution)/shard_map/hidden_beside/pallas_call | solution.py:89
  48.5 1.6 %hidden_own.1.mine = f32[64,2304]{1,0:T(8,128)S(1)} custom-call(bf16[4,16,1920]{2,1,0:T(8,128)(2,1)S(1)} %gather_rows.1.refs_0_.x, bf16[64,768]{1,0:T(8,128)(2,1)S(1)} %get-tuple-element.42.refs_1_, bf16[1792,4608]{1,0:T(8,128)(2,1)S(1)} %bitcast.1, bf16[1792,4608]{1,0:T(8,128)(2,1)S(1)} %bitcast.3), custom_call_target="tpu_custom_call" | custom-call | flops 550000000 | tf_op jit(solution)/shard_map/hidden_own/pallas_call | solution.py:89
  51.0 1.6 %collective-permute-start.21 = (bf16[64,640]{1,0:T(8,128)(2,1)S(1)}, bf16[64,640]{1,0:T(8,128)(2,1)S(1)}, u32[]{:S(2)}, u32[]{:S(2)}) collective-permute-start(bf16[64,640]{1,0:T(8,128)(2,1)S(1)} %get-tuple-element.46.refs_0_), channel_id=1, source_target_pairs={{0,2},{1,3},{2,0},{3,1},{4,6},{5,7},{6,4},{7,5},{8,10},{9,11},{10,... | collective-permute-start | bytes 245768 | tf_op jit(solution)/shard_map/ppermute | solution.py:103
  53.3 1.1 %collective-permute-start.19 = (bf16[64,512]{1,0:T(8,128)(2,1)S(1)}, bf16[64,512]{1,0:T(8,128)(2,1)S(1)}, u32[]{:S(2)}, u32[]{:S(2)}) collective-permute-start(bf16[64,512]{1,0:T(8,128)(2,1)S(1)} %activate.3.refs_1_), channel_id=1, source_target_pairs={{0,2},{1,3},{2,0},{3,1},{4,6},{5,7},{6,4},{7,5},{8,10},{9,11},{10,... | collective-permute-start | bytes 196616 | tf_op jit(solution)/shard_map/ppermute | solution.py:103
  54.9 1.2 %down.4.refs_2_ = f32[64,1792]{1,0:T(8,128)S(1)} custom-call(bf16[64,640]{1,0:T(8,128)(2,1)S(1)} %get-tuple-element.46.refs_0_, bf16[64,512]{1,0:T(8,128)(2,1)S(1)} %activate.3.refs_1_, bf16[64,640]{1,0:T(8,128)(2,1)S(1)} %collective-permute-done.22.refs_2_, bf16[4608,1792]{1,0:T(8,128)(2,1)S(1)} %bitcast.5), custom_call_target="tpu_custom_call" | custom-call | flops 50000000 | tf_op jit(solution)/shard_map/down/pallas_call | solution.py:89
  60.6 1.3 %collective-permute-start.27 = (bf16[16,1792]{1,0:T(8,128)(2,1)S(1)}, bf16[16,1792]{1,0:T(8,128)(2,1)S(1)}, u32[]{:S(2)}, u32[]{:S(2)}) collective-permute-start(bf16[16,1792]{1,0:T(8,128)(2,1)S(1)} %get-tuple-element.54), channel_id=1, source_target_pairs={{0,4},{4,8},{8,12},{12,0},{1,5},{5,9},{9,13},{13,1},{2,6},{6,10},{... | collective-permute-start | bytes 172040 | tf_op jit(solution)/shard_map/ppermute | solution.py:109
  61.9 2.9 %collective-permute-done.25.refs_2_ = bf16[16,1792]{1,0:T(8,128)(2,1)S(1)} collective-permute-done((bf16[16,1792]{1,0:T(8,128)(2,1)S(1)}, bf16[16,1792]{1,0:T(8,128)(2,1)S(1)}, u32[]{:S(2)}, u32[]{:S(2)}) %collective-permute-start.25) | collective-permute-done | bytes 57376 | tf_op jit(solution)/shard_map/ppermute | solution.py:109
  64.8 1.8 %collective-permute-done.27.refs_4_ = bf16[16,1792]{1,0:T(8,128)(2,1)S(1)} collective-permute-done((bf16[16,1792]{1,0:T(8,128)(2,1)S(1)}, bf16[16,1792]{1,0:T(8,128)(2,1)S(1)}, u32[]{:S(2)}, u32[]{:S(2)}) %collective-permute-start.27) | collective-permute-done | bytes 57376 | tf_op jit(solution)/shard_map/ppermute | solution.py:109
  (86 shorter events, 15.6 us)
Async XLA Ops:
  3.3 6.5 %collective-permute-start = (bf16[4,16,256]{2,1,0:T(8,128)(2,1)S(1)}, bf16[4,16,256]{2,1,0:T(8,128)(2,1)S(1)}, u32[]{:S(2)}, u32[]{:S(2)}) collective-permute-start(bf16[4,16,256]{2,1,0:T(8,128)(2,1)S(1)} %get-tuple-element.31), channel_id=1, source_target_pairs={{0,8},{4,12},{8,0},{12,4},{1,9},{5,13},{9,1},{13,5},{2,10},{6,14},... | collective-permute-start | bytes 98312 | tf_op jit(solution)/shard_map/ppermute | solution.py:109
  7.4 3.9 %collective-permute-start.1 = (bf16[4,16,256]{2,1,0:T(8,128)(2,1)S(1)}, bf16[4,16,256]{2,1,0:T(8,128)(2,1)S(1)}, u32[]{:S(2)}, u32[]{:S(2)}) collective-permute-start(bf16[4,16,256]{2,1,0:T(8,128)(2,1)S(1)} %get-tuple-element.32), channel_id=1, source_target_pairs={{0,12},{4,0},{8,4},{12,8},{1,13},{5,1},{9,5},{13,9},{2,14},{6,2},{... | collective-permute-start | bytes 98312 | tf_op jit(solution)/shard_map/ppermute | solution.py:109
  8.7 5.7 %collective-permute-start.2 = (bf16[4,16,256]{2,1,0:T(8,128)(2,1)S(1)}, bf16[4,16,256]{2,1,0:T(8,128)(2,1)S(1)}, u32[]{:S(2)}, u32[]{:S(2)}) collective-permute-start(bf16[4,16,256]{2,1,0:T(8,128)(2,1)S(1)} %get-tuple-element.33), channel_id=1, source_target_pairs={{0,4},{4,8},{8,12},{12,0},{1,5},{5,9},{9,13},{13,1},{2,6},{6,10},{... | collective-permute-start | bytes 98312 | tf_op jit(solution)/shard_map/ppermute | solution.py:109
  14.5 5.0 %collective-permute-start.4 = (bf16[4,4,16,256]{3,2,1,0:T(8,128)(2,1)S(1)}, bf16[4,4,16,256]{3,2,1,0:T(8,128)(2,1)S(1)}, u32[]{:S(2)}, u32[]{:S(2)}) collective-permute-start(bf16[4,4,16,256]{3,2,1,0:T(8,128)(2,1)S(1)} %pack.1.refs_0_), channel_id=1, source_target_pairs={{0,2},{1,3},{2,0},{3,1},{4,6},{5,7},{6,4},{7,5},{8,10},{9,11},{10,... | collective-permute-start | bytes 393224 | tf_op jit(solution)/shard_map/ppermute | solution.py:103
  16.1 3.5 %collective-permute-start.3 = (bf16[4,4,16,256]{3,2,1,0:T(8,128)(2,1)S(1)}, bf16[4,4,16,256]{3,2,1,0:T(8,128)(2,1)S(1)}, u32[]{:S(2)}, u32[]{:S(2)}) collective-permute-start(bf16[4,4,16,256]{3,2,1,0:T(8,128)(2,1)S(1)} %pack.1.refs_0_), channel_id=1, source_target_pairs={{0,1},{1,0},{2,3},{3,2},{4,5},{5,4},{6,7},{7,6},{8,9},{9,8},{10,11... | collective-permute-start | bytes 393224 | tf_op jit(solution)/shard_map/ppermute | solution.py:103
  23.8 5.6 %collective-permute-start.6 = (bf16[16,1792]{1,0:T(8,128)(2,1)S(1)}, bf16[16,1792]{1,0:T(8,128)(2,1)S(1)}, u32[]{:S(2)}, u32[]{:S(2)}) collective-permute-start(bf16[16,1792]{1,0:T(8,128)(2,1)S(1)} %get-tuple-element.35), channel_id=1, source_target_pairs={{0,8},{4,12},{8,0},{12,4},{1,9},{5,13},{9,1},{13,5},{2,10},{6,14},... | collective-permute-start | bytes 172040 | tf_op jit(solution)/shard_map/ppermute | solution.py:109
  23.9 5.5 %collective-permute-start.7 = (bf16[16,1792]{1,0:T(8,128)(2,1)S(1)}, bf16[16,1792]{1,0:T(8,128)(2,1)S(1)}, u32[]{:S(2)}, u32[]{:S(2)}) collective-permute-start(bf16[16,1792]{1,0:T(8,128)(2,1)S(1)} %get-tuple-element.36), channel_id=1, source_target_pairs={{0,12},{4,0},{8,4},{12,8},{1,13},{5,1},{9,5},{13,9},{2,14},{6,2},{... | collective-permute-start | bytes 172040 | tf_op jit(solution)/shard_map/ppermute | solution.py:109
  25.1 6.1 %collective-permute-start.8 = (bf16[16,1792]{1,0:T(8,128)(2,1)S(1)}, bf16[16,1792]{1,0:T(8,128)(2,1)S(1)}, u32[]{:S(2)}, u32[]{:S(2)}) collective-permute-start(bf16[16,1792]{1,0:T(8,128)(2,1)S(1)} %get-tuple-element.37), channel_id=1, source_target_pairs={{0,4},{4,8},{8,12},{12,0},{1,5},{5,9},{9,13},{13,1},{2,6},{6,10},{... | collective-permute-start | bytes 172040 | tf_op jit(solution)/shard_map/ppermute | solution.py:109
  31.3 6.2 %collective-permute-start.9 = (bf16[16,1920]{1,0:T(8,128)(2,1)S(1)}, bf16[16,1920]{1,0:T(8,128)(2,1)S(1)}, u32[]{:S(2)}, u32[]{:S(2)}) collective-permute-start(bf16[16,1920]{1,0:T(8,128)(2,1)S(1)} %get-tuple-element.39.refs_0_), channel_id=1, source_target_pairs={{0,8},{4,12},{8,0},{12,4},{1,9},{5,13},{9,1},{13,5},{2,10},{6,14},... | collective-permute-start | bytes 184328 | tf_op jit(solution)/shard_map/ppermute | solution.py:109
  31.9 5.5 %collective-permute-start.10 = (bf16[16,1920]{1,0:T(8,128)(2,1)S(1)}, bf16[16,1920]{1,0:T(8,128)(2,1)S(1)}, u32[]{:S(2)}, u32[]{:S(2)}) collective-permute-start(bf16[16,1920]{1,0:T(8,128)(2,1)S(1)} %get-tuple-element.39.refs_0_), channel_id=1, source_target_pairs={{0,12},{4,0},{8,4},{12,8},{1,13},{5,1},{9,5},{13,9},{2,14},{6,2},{... | collective-permute-start | bytes 184328 | tf_op jit(solution)/shard_map/ppermute | solution.py:109
  33.7 6.0 %collective-permute-start.11 = (bf16[16,1920]{1,0:T(8,128)(2,1)S(1)}, bf16[16,1920]{1,0:T(8,128)(2,1)S(1)}, u32[]{:S(2)}, u32[]{:S(2)}) collective-permute-start(bf16[16,1920]{1,0:T(8,128)(2,1)S(1)} %get-tuple-element.39.refs_0_), channel_id=1, source_target_pairs={{0,4},{4,8},{8,12},{12,0},{1,5},{5,9},{9,13},{13,1},{2,6},{6,10},{... | collective-permute-start | bytes 184328 | tf_op jit(solution)/shard_map/ppermute | solution.py:109
  40.8 2.4 %collective-permute-start.12 = (bf16[64,1408]{1,0:T(8,128)(2,1)S(1)}, bf16[64,1408]{1,0:T(8,128)(2,1)S(1)}, u32[]{:S(2)}, u32[]{:S(2)}) collective-permute-start(bf16[64,1408]{1,0:T(8,128)(2,1)S(1)} %hidden_diagonal.2.refs_1_), channel_id=1, source_target_pairs={{0,1},{1,0},{2,3},{3,2},{4,5},{5,4},{6,7},{7,6},{8,9},{9,8},{10,11... | collective-permute-start | bytes 540680 | tf_op jit(solution)/shard_map/ppermute | solution.py:103
  41.6 4.0 %collective-permute-start.13 = (bf16[64,1024]{1,0:T(8,128)(2,1)S(1)}, bf16[64,1024]{1,0:T(8,128)(2,1)S(1)}, u32[]{:S(2)}, u32[]{:S(2)}) collective-permute-start(bf16[64,1024]{1,0:T(8,128)(2,1)S(1)} %hidden_diagonal.3.refs_1_), channel_id=1, source_target_pairs={{0,1},{1,0},{2,3},{3,2},{4,5},{5,4},{6,7},{7,6},{8,9},{9,8},{10,11... | collective-permute-start | bytes 393224 | tf_op jit(solution)/shard_map/ppermute | solution.py:103
  43.3 7.5 %collective-permute-start.18 = (bf16[64,1408]{1,0:T(8,128)(2,1)S(1)}, bf16[64,1408]{1,0:T(8,128)(2,1)S(1)}, u32[]{:S(2)}, u32[]{:S(2)}) collective-permute-start(bf16[64,1408]{1,0:T(8,128)(2,1)S(1)} %get-tuple-element.40.refs_1_), channel_id=1, source_target_pairs={{0,2},{1,3},{2,0},{3,1},{4,6},{5,7},{6,4},{7,5},{8,10},{9,11},{10,... | collective-permute-start | bytes 540680 | tf_op jit(solution)/shard_map/ppermute | solution.py:103
  45.6 7.0 %collective-permute-start.17 = (bf16[64,1024]{1,0:T(8,128)(2,1)S(1)}, bf16[64,1024]{1,0:T(8,128)(2,1)S(1)}, u32[]{:S(2)}, u32[]{:S(2)}) collective-permute-start(bf16[64,1024]{1,0:T(8,128)(2,1)S(1)} %relay.3.refs_1_), channel_id=1, source_target_pairs={{0,2},{1,3},{2,0},{3,1},{4,6},{5,7},{6,4},{7,5},{8,10},{9,11},{10,... | collective-permute-start | bytes 393224 | tf_op jit(solution)/shard_map/ppermute | solution.py:103
  47.8 2.2 %collective-permute-start.14 = (bf16[64,768]{1,0:T(8,128)(2,1)S(1)}, bf16[64,768]{1,0:T(8,128)(2,1)S(1)}, u32[]{:S(2)}, u32[]{:S(2)}) collective-permute-start(bf16[64,768]{1,0:T(8,128)(2,1)S(1)} %get-tuple-element.42.refs_1_), channel_id=1, source_target_pairs={{0,1},{1,0},{2,3},{3,2},{4,5},{5,4},{6,7},{7,6},{8,9},{9,8},{10,11... | collective-permute-start | bytes 294920 | tf_op jit(solution)/shard_map/ppermute | solution.py:103
  47.9 2.2 %collective-permute-start.15 = (bf16[64,768]{1,0:T(8,128)(2,1)S(1)}, bf16[64,768]{1,0:T(8,128)(2,1)S(1)}, u32[]{:S(2)}, u32[]{:S(2)}) collective-permute-start(bf16[64,768]{1,0:T(8,128)(2,1)S(1)} %get-tuple-element.43), channel_id=1, source_target_pairs={{0,1},{1,0},{2,3},{3,2},{4,5},{5,4},{6,7},{7,6},{8,9},{9,8},{10,11... | collective-permute-start | bytes 294920 | tf_op jit(solution)/shard_map/ppermute | solution.py:103
  51.0 5.2 %collective-permute-start.21 = (bf16[64,640]{1,0:T(8,128)(2,1)S(1)}, bf16[64,640]{1,0:T(8,128)(2,1)S(1)}, u32[]{:S(2)}, u32[]{:S(2)}) collective-permute-start(bf16[64,640]{1,0:T(8,128)(2,1)S(1)} %get-tuple-element.46.refs_0_), channel_id=1, source_target_pairs={{0,2},{1,3},{2,0},{3,1},{4,6},{5,7},{6,4},{7,5},{8,10},{9,11},{10,... | collective-permute-start | bytes 245768 | tf_op jit(solution)/shard_map/ppermute | solution.py:103
  52.5 1.9 %collective-permute-start.22 = (bf16[64,640]{1,0:T(8,128)(2,1)S(1)}, bf16[64,640]{1,0:T(8,128)(2,1)S(1)}, u32[]{:S(2)}, u32[]{:S(2)}) collective-permute-start(bf16[64,640]{1,0:T(8,128)(2,1)S(1)} %get-tuple-element.46.refs_0_), channel_id=1, source_target_pairs={{0,1},{1,0},{2,3},{3,2},{4,5},{5,4},{6,7},{7,6},{8,9},{9,8},{10,11... | collective-permute-start | bytes 245768 | tf_op jit(solution)/shard_map/ppermute | solution.py:103
  52.8 3.8 %collective-permute-start.20 = (bf16[64,512]{1,0:T(8,128)(2,1)S(1)}, bf16[64,512]{1,0:T(8,128)(2,1)S(1)}, u32[]{:S(2)}, u32[]{:S(2)}) collective-permute-start(bf16[64,512]{1,0:T(8,128)(2,1)S(1)} %activate.3.refs_1_), channel_id=1, source_target_pairs={{0,1},{1,0},{2,3},{3,2},{4,5},{5,4},{6,7},{7,6},{8,9},{9,8},{10,11... | collective-permute-start | bytes 196616 | tf_op jit(solution)/shard_map/ppermute | solution.py:103
  53.3 4.3 %collective-permute-start.19 = (bf16[64,512]{1,0:T(8,128)(2,1)S(1)}, bf16[64,512]{1,0:T(8,128)(2,1)S(1)}, u32[]{:S(2)}, u32[]{:S(2)}) collective-permute-start(bf16[64,512]{1,0:T(8,128)(2,1)S(1)} %activate.3.refs_1_), channel_id=1, source_target_pairs={{0,2},{1,3},{2,0},{3,1},{4,6},{5,7},{6,4},{7,5},{8,10},{9,11},{10,... | collective-permute-start | bytes 196616 | tf_op jit(solution)/shard_map/ppermute | solution.py:103
  59.2 5.6 %collective-permute-start.25 = (bf16[16,1792]{1,0:T(8,128)(2,1)S(1)}, bf16[16,1792]{1,0:T(8,128)(2,1)S(1)}, u32[]{:S(2)}, u32[]{:S(2)}) collective-permute-start(bf16[16,1792]{1,0:T(8,128)(2,1)S(1)} %get-tuple-element.52), channel_id=1, source_target_pairs={{0,8},{4,12},{8,0},{12,4},{1,9},{5,13},{9,1},{13,5},{2,10},{6,14},... | collective-permute-start | bytes 172040 | tf_op jit(solution)/shard_map/ppermute | solution.py:109
  59.9 4.9 %collective-permute-start.26 = (bf16[16,1792]{1,0:T(8,128)(2,1)S(1)}, bf16[16,1792]{1,0:T(8,128)(2,1)S(1)}, u32[]{:S(2)}, u32[]{:S(2)}) collective-permute-start(bf16[16,1792]{1,0:T(8,128)(2,1)S(1)} %get-tuple-element.53), channel_id=1, source_target_pairs={{0,12},{4,0},{8,4},{12,8},{1,13},{5,1},{9,5},{13,9},{2,14},{6,2},{... | collective-permute-start | bytes 172040 | tf_op jit(solution)/shard_map/ppermute | solution.py:109
  60.6 6.1 %collective-permute-start.27 = (bf16[16,1792]{1,0:T(8,128)(2,1)S(1)}, bf16[16,1792]{1,0:T(8,128)(2,1)S(1)}, u32[]{:S(2)}, u32[]{:S(2)}) collective-permute-start(bf16[16,1792]{1,0:T(8,128)(2,1)S(1)} %get-tuple-element.54), channel_id=1, source_target_pairs={{0,4},{4,8},{8,12},{12,0},{1,5},{5,9},{9,13},{13,1},{2,6},{6,10},{... | collective-permute-start | bytes 172040 | tf_op jit(solution)/shard_map/ppermute | solution.py:109
  (19 other events, 305.9 us)

commit v5 on v4

--- a/solution.py
+++ b/solution.py
@@ -17,6 +17,11 @@
 HEADS_STEPS = STEPS
 ROWS_STEPS = STEPS
 END_STEPS = STEPS
+EARLY = 2
+HEADS_PAIRS = True
+SUMS_PAIRS = False
+ROWS_PAIRS = False
+END_PAIRS = False
 ATTEND_US = 20
 SETTLE_US = 3
 GATHER_US = 3
@@ -103,12 +108,20 @@
     return lax.ppermute(x, axis, [(i, i ^ step) for i in range(count)])
 
 
-def spread(blocks, axis, steps=STEPS):
+def spread(blocks, axis, steps, pairs):
     count = len(blocks)
     return [
-        lax.ppermute(blocks[k], axis, [(i, (i + k) % count) for i in range(count)])
+        lax.ppermute(blocks[k], axis, [(i, i ^ k if pairs else (i + k) % count) for i in range(count)])
         for k in steps
     ]
+
+
+def target(a, k, count, pairs):
+    return a ^ k if pairs else (a + k) % count
+
+
+def source(a, k, count, pairs):
+    return a ^ k if pairs else (a - k) % count
 
 
 def tiles(width, tile=256):
@@ -175,25 +188,26 @@
         att[r] = o.reshape(attn, per, hd)
     me = lax.axis_index("attn")
     for k in range(attn):
-        outs[k][...] = att[:, (me + k) % attn]
-
-
-def pack(attn, *refs):
-    out = refs[attn]
-    me = lax.axis_index("attn")
-    for ref, k in zip(refs, (0, *HEADS_STEPS)):
-        out[(me - k) % attn] = ref[...]
+        outs[k][...] = att[:, target(me, k, attn, HEADS_PAIRS)]
+
+
+def pack(*refs):
+    for i, ref in enumerate(refs[:-1]):
+        refs[-1][i] = ref[...]
 
 
 def project(attn, ffn, rows, per, hd, *refs):
-    blocks, (resid, w) = refs[:ffn], refs[ffn : ffn + 2]
-    sends, (own, xs, x, res) = refs[ffn + 2 : ffn + 1 + attn], refs[ffn + 1 + attn :]
+    early, late, refs = refs[:ffn], refs[ffn : 2 * ffn], refs[2 * ffn :]
+    resid, w = refs[:2]
+    sends, (own, xs, x, res) = refs[2 : 1 + attn], refs[1 + attn :]
     f, a = lax.axis_index("ffn"), lax.axis_index("attn")
     total = attn * ffn * rows
     for j in range(ffn):
-        for i in range(attn):
-            start = pl.multiple_of((i * ffn + (f ^ j)) * rows * per, rows * per)
-            value = blocks[j][i].reshape(rows * per, hd).astype(F32)
+        for i, k in enumerate((0, *HEADS_STEPS)):
+            place = source(a, k, attn, HEADS_PAIRS)
+            start = pl.multiple_of((place * ffn + (f ^ j)) * rows * per, rows * per)
+            block = early[j][i] if i < EARLY else late[j][i - EARLY]
+            value = block.reshape(rows * per, hd).astype(F32)
             for c in range(hd // 128):
                 xs[c, pl.ds(start, rows * per), :] = value[:, c * 128 : (c + 1) * 128]
     for h in range(per):
@@ -204,7 +218,7 @@
         y = jnp.dot(x[...], w[:, s : s + n], preferred_element_type=F32)
         res[:, :, s : s + n] = y.reshape(attn, ffn * rows, n)
     for k in range(1, attn):
-        sends[k - 1][...] = res[(a + k) % attn].astype(BF16)
+        sends[k - 1][...] = res[target(a, k, attn, SUMS_PAIRS)].astype(BF16)
     own[...] = res[a] + resid[...].astype(F32)
 
 
@@ -224,7 +238,7 @@
     x = refs[attn]
     a = lax.axis_index("attn")
     for ref, k in zip(refs, (0, *ROWS_STEPS)):
-        x[(a - k) % attn] = ref[...]
+        x[source(a, k, attn, ROWS_PAIRS)] = ref[...]
 
 
 def sums(x, wg, wu, start, cut, out):
@@ -312,7 +326,7 @@
             res[:, s : s + n] = y
     if last:
         for k in range(1, attn):
-            refs[k - 1][...] = res[(a + k) % attn].astype(BF16)
+            refs[k - 1][...] = res[target(a, k, attn, END_PAIRS)].astype(BF16)
         refs[attn - 1][...] = res[a]
 
 
@@ -351,17 +365,21 @@
         flops=int(ATTEND_US * US),
         limit=7,
     )
-    parts = [parts[0], *spread(parts, "attn", HEADS_STEPS)]
-    (mine,) = call(functools.partial(pack, attn), "pack", [((attn, *block), BF16)], parts)
-    across = swap(mine, "ffn", 2)
-    beside = swap(mine, "ffn", 1)
-    diagonal = swap(across, "ffn", 1)
+    parts = [parts[0], *spread(parts, "attn", HEADS_STEPS, HEADS_PAIRS)]
+    first, last = (
+        call(pack, name, [((len(v), *block), BF16)], v)[0]
+        for name, v in (("pack_early", parts[:EARLY]), ("pack_late", parts[EARLY:]))
+    )
+    early, late = [], []
+    for held, value in ((early, first), (late, last)):
+        across = swap(value, "ffn", 2)
+        held += [value, swap(value, "ffn", 1), across, swap(across, "ffn", 1)]
 
     *sends, own = call(
         functools.partial(project, attn, ffn, rows, per, hd),
         "project",
         [((own_rows, width), BF16)] * (attn - 1) + [((own_rows, width), F32)],
-        [mine, beside, across, diagonal, resid],
+        [*early, *late, resid],
         [
             pltpu.VMEM((hd // 128, total * per, 128), F32),
             pltpu.VMEM((total, per * hd), BF16),
@@ -370,7 +388,7 @@
         [out_weight],
         flops=int(PROJECT_US * US),
     )
-    came = spread([None, *sends], "attn")
+    came = spread([None, *sends], "attn", STEPS, SUMS_PAIRS)
     state, xg = call(
         functools.partial(settle, attn),
         "settle",
@@ -378,7 +396,7 @@
         [own, *came, norm_gain.reshape(1, width)],
         flops=int(SETTLE_US * US),
     )
-    xs = [xg, *spread([xg] * attn, "attn", ROWS_STEPS)]
+    xs = [xg, *spread([xg] * attn, "attn", ROWS_STEPS, ROWS_PAIRS)]
     (x,) = call(
         functools.partial(gather_rows, attn),
         "gather_rows",
@@ -465,7 +483,7 @@
     ending = swap(across[1], "ffn", 1)
     (acc,) = fold([(3, *first), (2, *second)], [diagonal, across[1]], acc)
     *sends, own = fold([(3, *second)], [ending], acc, True)
-    came = spread([None, *sends], "attn", END_STEPS)
+    came = spread([None, *sends], "attn", END_STEPS, END_PAIRS)
     (mixed,) = call(
         functools.partial(finish, attn),
         "finish",

time: 67.4 us -> 66.7 us (0.990)
  waiting for transfers between devices: 27.1 us -> 21.8 us
  starting transfers between devices: 22.2 us -> 26.7 us
    ppermute x12, waiting for transfers between devices: 20.8 us -> 16.8 us  [spread(): lax.ppermute(blocks[k], axis, [(i, i ^ k if pairs else (i + k) % count) f...]
    ppermute x12, starting transfers between devices: 13.6 us -> 16.1 us  [spread(): lax.ppermute(blocks[k], axis, [(i, i ^ k if pairs else (i + k) % count) f...]
    ppermute x16 -> x19, starting transfers between devices: 8.62 us -> 10.5 us  [swap(): return lax.ppermute(x, axis, [(i, i ^ step) for i in range(count)])]
    ppermute x16 -> x19, waiting for transfers between devices: 6.38 us -> 5.03 us  [swap(): return lax.ppermute(x, axis, [(i, i ^ step) for i in range(count)])]
    pallas_call x20 -> x21, Pallas kernels: 17.1 us -> 17.1 us  [call(): pl.pallas_call(kernel, out_shape=[jax.ShapeDtypeStruct(s, t) for s, t in...]
  transfers between devices with their start and end apart: 28 -> 31, of which waited for: 15 -> 17; matrix products, arithmetic and copies ran while one was open for 0% -> 0% of each run, Pallas kernels for 13% -> 13%
where the time goes in v5:
time: 66.7 us; the launch traced here: 66.6 us
  starting transfers between devices  26.7 us (40%)
  waiting for transfers between devices  21.8 us (33%)
  Pallas kernels  17.1 us (26%)
  local copies, waits for them, and re-layouts  0.73 us (1%)
    pallas_call x21, Pallas kernels, call(): pl.pallas_call(kernel, out_shape=[jax.ShapeDtypeStruct(s, t) for s, t in...  17.1 us
    ppermute x12, waiting for transfers between devices, spread(): lax.ppermute(blocks[k], axis, [(i, i ^ k if pairs else (i + k) % count) f...  16.8 us
    ppermute x12, starting transfers between devices, spread(): lax.ppermute(blocks[k], axis, [(i, i ^ k if pairs else (i + k) % count) f...  16.1 us
    ppermute x19, starting transfers between devices, swap(): return lax.ppermute(x, axis, [(i, i ^ step) for i in range(count)])  10.5 us
    ppermute x19, waiting for transfers between devices, swap(): return lax.ppermute(x, axis, [(i, i ^ step) for i in range(count)])  5.03 us
  transfers between devices with their start and end apart: 31, of which 17 were waited for; matrix products, arithmetic and copies ran while one was open for 0% of the time, Pallas kernels for 13%

profile of v5, /device:TPU:0, one launch (start us, length us, event | category | flops | bytes accessed | tf_op | source)
XLA Modules:
  0.0 66.6 jit_solution(4248258794319105249)
XLA Ops:
  0.0 3.2 %attend.1 = (bf16[4,16,256]{2,1,0:T(8,128)(2,1)S(1)}, bf16[4,16,256]{2,1,0:T(8,128)(2,1)S(1)}, bf16[4,16,256]{2,1,0:T(8,128)(2,1)S(1)}, bf16[4,16,256]{2,1,0:T(8,128)(2,1)S(1)}) custom-call(s32[4]{0:T(128)} %lens_any.1, bf16[4,16384]{1,0:T(4,128)(2,1)} %q_any.1, bf16[4,1024,512]{2,1,0:T(8,128)(2,1)} %cache.1), custom_call_target="tpu_custom_call" | custom-call | flops 20000000000 | tf_op jit(solution)/shard_map/attend/pallas_call | solution.py:94
  3.3 4.1 %collective-permute-start = (bf16[4,16,256]{2,1,0:T(8,128)(2,1)S(1)}, bf16[4,16,256]{2,1,0:T(8,128)(2,1)S(1)}, u32[]{:S(2)}, u32[]{:S(2)}) collective-permute-start(bf16[4,16,256]{2,1,0:T(8,128)(2,1)S(1)} %get-tuple-element.31), channel_id=1, source_target_pairs={{0,8},{4,12},{8,0},{12,4},{1,9},{5,13},{9,1},{13,5},{2,10},{6,14},... | collective-permute-start | bytes 98312 | tf_op jit(solution)/shard_map/ppermute | solution.py:114
  7.4 1.4 %collective-permute-start.4 = (bf16[4,16,256]{2,1,0:T(8,128)(2,1)S(1)}, bf16[4,16,256]{2,1,0:T(8,128)(2,1)S(1)}, u32[]{:S(2)}, u32[]{:S(2)}) collective-permute-start(bf16[4,16,256]{2,1,0:T(8,128)(2,1)S(1)} %get-tuple-element.32), channel_id=1, source_target_pairs={{0,12},{4,8},{8,4},{12,0},{1,13},{5,9},{9,5},{13,1},{2,14},{6,10},... | collective-permute-start | bytes 98312 | tf_op jit(solution)/shard_map/ppermute | solution.py:114
  9.6 1.7 %collective-permute-start.2 = (bf16[2,4,16,256]{3,2,1,0:T(8,128)(2,1)S(1)}, bf16[2,4,16,256]{3,2,1,0:T(8,128)(2,1)S(1)}, u32[]{:S(2)}, u32[]{:S(2)}) collective-permute-start(bf16[2,4,16,256]{3,2,1,0:T(8,128)(2,1)S(1)} %pack_early.1.refs_0_), channel_id=1, source_target_pairs={{0,2},{1,3},{2,0},{3,1},{4,6},{5,7},{6,4},{7,5},{8,10},{9,11},{10,... | collective-permute-start | bytes 196616 | tf_op jit(solution)/shard_map/ppermute | solution.py:108
  11.3 1.8 %collective-permute-done.4.refs_0_ = bf16[4,16,256]{2,1,0:T(8,128)(2,1)S(1)} collective-permute-done((bf16[4,16,256]{2,1,0:T(8,128)(2,1)S(1)}, bf16[4,16,256]{2,1,0:T(8,128)(2,1)S(1)}, u32[]{:S(2)}, u32[]{:S(2)}) %collective-permute-start.4) | collective-permute-done | bytes 32800 | tf_op jit(solution)/shard_map/ppermute | solution.py:114
  13.1 1.6 %collective-permute-start.7 = (bf16[2,4,16,256]{3,2,1,0:T(8,128)(2,1)S(1)}, bf16[2,4,16,256]{3,2,1,0:T(8,128)(2,1)S(1)}, u32[]{:S(2)}, u32[]{:S(2)}) collective-permute-start(bf16[2,4,16,256]{3,2,1,0:T(8,128)(2,1)S(1)} %pack_late.1.refs_4_), channel_id=1, source_target_pairs={{0,2},{1,3},{2,0},{3,1},{4,6},{5,7},{6,4},{7,5},{8,10},{9,11},{10,... | collective-permute-start | bytes 196616 | tf_op jit(solution)/shard_map/ppermute | solution.py:108
  15.2 2.3 %collective-permute-done.7.refs_6_ = bf16[2,4,16,256]{3,2,1,0:T(8,128)(2,1)S(1)} collective-permute-done((bf16[2,4,16,256]{3,2,1,0:T(8,128)(2,1)S(1)}, bf16[2,4,16,256]{3,2,1,0:T(8,128)(2,1)S(1)}, u32[]{:S(2)}, u32[]{:S(2)}) %collective-permute-start.7) | collective-permute-done | bytes 65568 | tf_op jit(solution)/shard_map/ppermute | solution.py:108
  17.5 1.2 %collective-permute-done.8.refs_7_ = bf16[2,4,16,256]{3,2,1,0:T(8,128)(2,1)S(1)} collective-permute-done((bf16[2,4,16,256]{3,2,1,0:T(8,128)(2,1)S(1)}, bf16[2,4,16,256]{3,2,1,0:T(8,128)(2,1)S(1)}, u32[]{:S(2)}, u32[]{:S(2)}) %collective-permute-start.8) | collective-permute-done | bytes 65568 | tf_op jit(solution)/shard_map/ppermute | solution.py:108
  18.7 2.9 %project.1 = (bf16[16,1792]{1,0:T(8,128)(2,1)S(1)}, bf16[16,1792]{1,0:T(8,128)(2,1)S(1)}, bf16[16,1792]{1,0:T(8,128)(2,1)S(1)}, f32[16,1792]{1,0:T(8,128)S(1)}) custom-call(bf16[2,4,16,256]{3,2,1,0:T(8,128)(2,1)S(1)} %pack_early.1.refs_0_, bf16[2,4,16,256]{3,2,1,0:T(8,128)(2,1)S(1)} %collective-permute-done.1.refs_1_, ...), custom_call_target="tpu_custom_call" | custom-call | flops 3000000000 | tf_op jit(solution)/shard_map/project/pallas_call | solution.py:94
  21.6 1.3 %collective-permute-start.9 = (bf16[16,1792]{1,0:T(8,128)(2,1)S(1)}, bf16[16,1792]{1,0:T(8,128)(2,1)S(1)}, u32[]{:S(2)}, u32[]{:S(2)}) collective-permute-start(bf16[16,1792]{1,0:T(8,128)(2,1)S(1)} %get-tuple-element.35), channel_id=1, source_target_pairs={{0,8},{4,12},{8,0},{12,4},{1,9},{5,13},{9,1},{13,5},{2,10},{6,14},... | collective-permute-start | bytes 172040 | tf_op jit(solution)/shard_map/ppermute | solution.py:114
  25.0 2.5 %collective-permute-done.9.refs_1_ = bf16[16,1792]{1,0:T(8,128)(2,1)S(1)} collective-permute-done((bf16[16,1792]{1,0:T(8,128)(2,1)S(1)}, bf16[16,1792]{1,0:T(8,128)(2,1)S(1)}, u32[]{:S(2)}, u32[]{:S(2)}) %collective-permute-start.9) | collective-permute-done | bytes 57376 | tf_op jit(solution)/shard_map/ppermute | solution.py:114
  28.0 2.0 %collective-permute-done.11.refs_3_ = bf16[16,1792]{1,0:T(8,128)(2,1)S(1)} collective-permute-done((bf16[16,1792]{1,0:T(8,128)(2,1)S(1)}, bf16[16,1792]{1,0:T(8,128)(2,1)S(1)}, u32[]{:S(2)}, u32[]{:S(2)}) %collective-permute-start.11) | collective-permute-done | bytes 57376 | tf_op jit(solution)/shard_map/ppermute | solution.py:114
  30.1 1.6 %collective-permute-start.12 = (bf16[16,1920]{1,0:T(8,128)(2,1)S(1)}, bf16[16,1920]{1,0:T(8,128)(2,1)S(1)}, u32[]{:S(2)}, u32[]{:S(2)}) collective-permute-start(bf16[16,1920]{1,0:T(8,128)(2,1)S(1)} %get-tuple-element.39.refs_0_), channel_id=1, source_target_pairs={{0,8},{4,12},{8,0},{12,4},{1,9},{5,13},{9,1},{13,5},{2,10},{6,14},... | collective-permute-start | bytes 184328 | tf_op jit(solution)/shard_map/ppermute | solution.py:114
  32.3 1.4 %collective-permute-start.14 = (bf16[16,1920]{1,0:T(8,128)(2,1)S(1)}, bf16[16,1920]{1,0:T(8,128)(2,1)S(1)}, u32[]{:S(2)}, u32[]{:S(2)}) collective-permute-start(bf16[16,1920]{1,0:T(8,128)(2,1)S(1)} %get-tuple-element.39.refs_0_), channel_id=1, source_target_pairs={{0,4},{4,8},{8,12},{12,0},{1,5},{5,9},{9,13},{13,1},{2,6},{6,10},{... | collective-permute-start | bytes 184328 | tf_op jit(solution)/shard_map/ppermute | solution.py:114
  33.7 2.1 %collective-permute-done.12.refs_1_ = bf16[16,1920]{1,0:T(8,128)(2,1)S(1)} collective-permute-done((bf16[16,1920]{1,0:T(8,128)(2,1)S(1)}, bf16[16,1920]{1,0:T(8,128)(2,1)S(1)}, u32[]{:S(2)}, u32[]{:S(2)}) %collective-permute-start.12) | collective-permute-done | bytes 61472 | tf_op jit(solution)/shard_map/ppermute | solution.py:114
  36.7 1.6 %collective-permute-done.14.refs_3_ = bf16[16,1920]{1,0:T(8,128)(2,1)S(1)} collective-permute-done((bf16[16,1920]{1,0:T(8,128)(2,1)S(1)}, bf16[16,1920]{1,0:T(8,128)(2,1)S(1)}, u32[]{:S(2)}, u32[]{:S(2)}) %collective-permute-start.14) | collective-permute-done | bytes 61472 | tf_op jit(solution)/shard_map/ppermute | solution.py:114
  41.9 1.4 %collective-permute-start.21 = (bf16[64,1408]{1,0:T(8,128)(2,1)S(1)}, bf16[64,1408]{1,0:T(8,128)(2,1)S(1)}, u32[]{:S(2)}, u32[]{:S(2)}) collective-permute-start(bf16[64,1408]{1,0:T(8,128)(2,1)S(1)} %get-tuple-element.40.refs_1_), channel_id=1, source_target_pairs={{0,2},{1,3},{2,0},{3,1},{4,6},{5,7},{6,4},{7,5},{8,10},{9,11},{10,... | collective-permute-start | bytes 540680 | tf_op jit(solution)/shard_map/ppermute | solution.py:108
  44.9 1.6 %hidden_beside.1 = (bf16[64,768]{1,0:T(8,128)(2,1)S(1)}, bf16[64,768]{1,0:T(8,128)(2,1)S(1)}, bf16[64,768]{1,0:T(8,128)(2,1)S(1)}) custom-call(bf16[4,16,1920]{2,1,0:T(8,128)(2,1)S(1)} %gather_rows.1.refs_0_.x, bf16[64,1024]{1,0:T(8,128)(2,1)S(1)} %relay.3.refs_1_, bf16[1792,4608]{1,0:T(8,128)(2,1)S(1)} %bitcast.1, bf16[1792,4608]{1,0:T(8,128)(2,1)S(1)} %bitcast.3), custom_call_target="tpu_custom_call" | custom-call | tf_op jit(solution)/shard_map/hidden_beside/pallas_call | solution.py:94
  47.1 1.6 %hidden_own.1.mine = f32[64,2304]{1,0:T(8,128)S(1)} custom-call(bf16[4,16,1920]{2,1,0:T(8,128)(2,1)S(1)} %gather_rows.1.refs_0_.x, bf16[64,768]{1,0:T(8,128)(2,1)S(1)} %get-tuple-element.42.refs_1_, bf16[1792,4608]{1,0:T(8,128)(2,1)S(1)} %bitcast.1, bf16[1792,4608]{1,0:T(8,128)(2,1)S(1)} %bitcast.3), custom_call_target="tpu_custom_call" | custom-call | flops 550000000 | tf_op jit(solution)/shard_map/hidden_own/pallas_call | solution.py:94
  49.6 1.4 %collective-permute-start.24 = (bf16[64,640]{1,0:T(8,128)(2,1)S(1)}, bf16[64,640]{1,0:T(8,128)(2,1)S(1)}, u32[]{:S(2)}, u32[]{:S(2)}) collective-permute-start(bf16[64,640]{1,0:T(8,128)(2,1)S(1)} %get-tuple-element.46.refs_0_), channel_id=1, source_target_pairs={{0,2},{1,3},{2,0},{3,1},{4,6},{5,7},{6,4},{7,5},{8,10},{9,11},{10,... | collective-permute-start | bytes 245768 | tf_op jit(solution)/shard_map/ppermute | solution.py:108
  53.5 1.2 %down.4.refs_2_ = f32[64,1792]{1,0:T(8,128)S(1)} custom-call(bf16[64,640]{1,0:T(8,128)(2,1)S(1)} %get-tuple-element.46.refs_0_, bf16[64,512]{1,0:T(8,128)(2,1)S(1)} %activate.3.refs_1_, bf16[64,640]{1,0:T(8,128)(2,1)S(1)} %collective-permute-done.25.refs_2_, bf16[4608,1792]{1,0:T(8,128)(2,1)S(1)} %bitcast.5), custom_call_target="tpu_custom_call" | custom-call | flops 50000000 | tf_op jit(solution)/shard_map/down/pallas_call | solution.py:94
  57.7 1.5 %collective-permute-start.28 = (bf16[16,1792]{1,0:T(8,128)(2,1)S(1)}, bf16[16,1792]{1,0:T(8,128)(2,1)S(1)}, u32[]{:S(2)}, u32[]{:S(2)}) collective-permute-start(bf16[16,1792]{1,0:T(8,128)(2,1)S(1)} %get-tuple-element.52), channel_id=1, source_target_pairs={{0,8},{4,12},{8,0},{12,4},{1,9},{5,13},{9,1},{13,5},{2,10},{6,14},... | collective-permute-start | bytes 172040 | tf_op jit(solution)/shard_map/ppermute | solution.py:114
  61.2 2.3 %collective-permute-done.28.refs_2_ = bf16[16,1792]{1,0:T(8,128)(2,1)S(1)} collective-permute-done((bf16[16,1792]{1,0:T(8,128)(2,1)S(1)}, bf16[16,1792]{1,0:T(8,128)(2,1)S(1)}, u32[]{:S(2)}, u32[]{:S(2)}) %collective-permute-start.28) | collective-permute-done | bytes 57376 | tf_op jit(solution)/shard_map/ppermute | solution.py:114
  63.9 2.0 %collective-permute-done.30.refs_4_ = bf16[16,1792]{1,0:T(8,128)(2,1)S(1)} collective-permute-done((bf16[16,1792]{1,0:T(8,128)(2,1)S(1)}, bf16[16,1792]{1,0:T(8,128)(2,1)S(1)}, u32[]{:S(2)}, u32[]{:S(2)}) %collective-permute-start.30) | collective-permute-done | bytes 57376 | tf_op jit(solution)/shard_map/ppermute | solution.py:114
  (93 shorter events, 20.8 us)
Async XLA Ops:
  3.3 6.4 %collective-permute-start = (bf16[4,16,256]{2,1,0:T(8,128)(2,1)S(1)}, bf16[4,16,256]{2,1,0:T(8,128)(2,1)S(1)}, u32[]{:S(2)}, u32[]{:S(2)}) collective-permute-start(bf16[4,16,256]{2,1,0:T(8,128)(2,1)S(1)} %get-tuple-element.31), channel_id=1, source_target_pairs={{0,8},{4,12},{8,0},{12,4},{1,9},{5,13},{9,1},{13,5},{2,10},{6,14},... | collective-permute-start | bytes 98312 | tf_op jit(solution)/shard_map/ppermute | solution.py:114
  7.4 5.7 %collective-permute-start.4 = (bf16[4,16,256]{2,1,0:T(8,128)(2,1)S(1)}, bf16[4,16,256]{2,1,0:T(8,128)(2,1)S(1)}, u32[]{:S(2)}, u32[]{:S(2)}) collective-permute-start(bf16[4,16,256]{2,1,0:T(8,128)(2,1)S(1)} %get-tuple-element.32), channel_id=1, source_target_pairs={{0,12},{4,8},{8,4},{12,0},{1,13},{5,9},{9,5},{13,1},{2,14},{6,10},... | collective-permute-start | bytes 98312 | tf_op jit(solution)/shard_map/ppermute | solution.py:114
  8.7 4.4 %collective-permute-start.5 = (bf16[4,16,256]{2,1,0:T(8,128)(2,1)S(1)}, bf16[4,16,256]{2,1,0:T(8,128)(2,1)S(1)}, u32[]{:S(2)}, u32[]{:S(2)}) collective-permute-start(bf16[4,16,256]{2,1,0:T(8,128)(2,1)S(1)} %get-tuple-element.33), channel_id=1, source_target_pairs={{0,4},{4,0},{8,12},{12,8},{1,5},{5,1},{9,13},{13,9},{2,6},{6,2},{1... | collective-permute-start | bytes 98312 | tf_op jit(solution)/shard_map/ppermute | solution.py:114
  9.6 5.6 %collective-permute-start.2 = (bf16[2,4,16,256]{3,2,1,0:T(8,128)(2,1)S(1)}, bf16[2,4,16,256]{3,2,1,0:T(8,128)(2,1)S(1)}, u32[]{:S(2)}, u32[]{:S(2)}) collective-permute-start(bf16[2,4,16,256]{3,2,1,0:T(8,128)(2,1)S(1)} %pack_early.1.refs_0_), channel_id=1, source_target_pairs={{0,2},{1,3},{2,0},{3,1},{4,6},{5,7},{6,4},{7,5},{8,10},{9,11},{10,... | collective-permute-start | bytes 196616 | tf_op jit(solution)/shard_map/ppermute | solution.py:108
  13.1 4.3 %collective-permute-start.7 = (bf16[2,4,16,256]{3,2,1,0:T(8,128)(2,1)S(1)}, bf16[2,4,16,256]{3,2,1,0:T(8,128)(2,1)S(1)}, u32[]{:S(2)}, u32[]{:S(2)}) collective-permute-start(bf16[2,4,16,256]{3,2,1,0:T(8,128)(2,1)S(1)} %pack_late.1.refs_4_), channel_id=1, source_target_pairs={{0,2},{1,3},{2,0},{3,1},{4,6},{5,7},{6,4},{7,5},{8,10},{9,11},{10,... | collective-permute-start | bytes 196616 | tf_op jit(solution)/shard_map/ppermute | solution.py:108
  14.7 2.8 %collective-permute-start.1 = (bf16[2,4,16,256]{3,2,1,0:T(8,128)(2,1)S(1)}, bf16[2,4,16,256]{3,2,1,0:T(8,128)(2,1)S(1)}, u32[]{:S(2)}, u32[]{:S(2)}) collective-permute-start(bf16[2,4,16,256]{3,2,1,0:T(8,128)(2,1)S(1)} %pack_early.1.refs_0_), channel_id=1, source_target_pairs={{0,1},{1,0},{2,3},{3,2},{4,5},{5,4},{6,7},{7,6},{8,9},{9,8},{10,11... | collective-permute-start | bytes 196616 | tf_op jit(solution)/shard_map/ppermute | solution.py:108
  14.7 2.8 %collective-permute-start.6 = (bf16[2,4,16,256]{3,2,1,0:T(8,128)(2,1)S(1)}, bf16[2,4,16,256]{3,2,1,0:T(8,128)(2,1)S(1)}, u32[]{:S(2)}, u32[]{:S(2)}) collective-permute-start(bf16[2,4,16,256]{3,2,1,0:T(8,128)(2,1)S(1)} %pack_late.1.refs_4_), channel_id=1, source_target_pairs={{0,1},{1,0},{2,3},{3,2},{4,5},{5,4},{6,7},{7,6},{8,9},{9,8},{10,11... | collective-permute-start | bytes 196616 | tf_op jit(solution)/shard_map/ppermute | solution.py:108
  15.2 2.3 %collective-permute-start.3 = (bf16[2,4,16,256]{3,2,1,0:T(8,128)(2,1)S(1)}, bf16[2,4,16,256]{3,2,1,0:T(8,128)(2,1)S(1)}, u32[]{:S(2)}, u32[]{:S(2)}) collective-permute-start(bf16[2,4,16,256]{3,2,1,0:T(8,128)(2,1)S(1)} %collective-permute-done.2.refs_2_), channel_id=1, source_target_pairs={{0,1},{1,0},{2,3},{3,2},{4,5},{5,4},{6,7},{7,6},{8,9},{9,8},{10,11... | collective-permute-start | bytes 196616 | tf_op jit(solution)/shard_map/ppermute | solution.py:108
  21.6 5.8 %collective-permute-start.9 = (bf16[16,1792]{1,0:T(8,128)(2,1)S(1)}, bf16[16,1792]{1,0:T(8,128)(2,1)S(1)}, u32[]{:S(2)}, u32[]{:S(2)}) collective-permute-start(bf16[16,1792]{1,0:T(8,128)(2,1)S(1)} %get-tuple-element.35), channel_id=1, source_target_pairs={{0,8},{4,12},{8,0},{12,4},{1,9},{5,13},{9,1},{13,5},{2,10},{6,14},... | collective-permute-start | bytes 172040 | tf_op jit(solution)/shard_map/ppermute | solution.py:114
  22.9 5.0 %collective-permute-start.10 = (bf16[16,1792]{1,0:T(8,128)(2,1)S(1)}, bf16[16,1792]{1,0:T(8,128)(2,1)S(1)}, u32[]{:S(2)}, u32[]{:S(2)}) collective-permute-start(bf16[16,1792]{1,0:T(8,128)(2,1)S(1)} %get-tuple-element.36), channel_id=1, source_target_pairs={{0,12},{4,0},{8,4},{12,8},{1,13},{5,1},{9,5},{13,9},{2,14},{6,2},{... | collective-permute-start | bytes 172040 | tf_op jit(solution)/shard_map/ppermute | solution.py:114
  24.0 6.0 %collective-permute-start.11 = (bf16[16,1792]{1,0:T(8,128)(2,1)S(1)}, bf16[16,1792]{1,0:T(8,128)(2,1)S(1)}, u32[]{:S(2)}, u32[]{:S(2)}) collective-permute-start(bf16[16,1792]{1,0:T(8,128)(2,1)S(1)} %get-tuple-element.37), channel_id=1, source_target_pairs={{0,4},{4,8},{8,12},{12,0},{1,5},{5,9},{9,13},{13,1},{2,6},{6,10},{... | collective-permute-start | bytes 172040 | tf_op jit(solution)/shard_map/ppermute | solution.py:114
  30.1 5.7 %collective-permute-start.12 = (bf16[16,1920]{1,0:T(8,128)(2,1)S(1)}, bf16[16,1920]{1,0:T(8,128)(2,1)S(1)}, u32[]{:S(2)}, u32[]{:S(2)}) collective-permute-start(bf16[16,1920]{1,0:T(8,128)(2,1)S(1)} %get-tuple-element.39.refs_0_), channel_id=1, source_target_pairs={{0,8},{4,12},{8,0},{12,4},{1,9},{5,13},{9,1},{13,5},{2,10},{6,14},... | collective-permute-start | bytes 184328 | tf_op jit(solution)/shard_map/ppermute | solution.py:114
  31.7 5.0 %collective-permute-start.13 = (bf16[16,1920]{1,0:T(8,128)(2,1)S(1)}, bf16[16,1920]{1,0:T(8,128)(2,1)S(1)}, u32[]{:S(2)}, u32[]{:S(2)}) collective-permute-start(bf16[16,1920]{1,0:T(8,128)(2,1)S(1)} %get-tuple-element.39.refs_0_), channel_id=1, source_target_pairs={{0,12},{4,0},{8,4},{12,8},{1,13},{5,1},{9,5},{13,9},{2,14},{6,2},{... | collective-permute-start | bytes 184328 | tf_op jit(solution)/shard_map/ppermute | solution.py:114
  32.3 6.0 %collective-permute-start.14 = (bf16[16,1920]{1,0:T(8,128)(2,1)S(1)}, bf16[16,1920]{1,0:T(8,128)(2,1)S(1)}, u32[]{:S(2)}, u32[]{:S(2)}) collective-permute-start(bf16[16,1920]{1,0:T(8,128)(2,1)S(1)} %get-tuple-element.39.refs_0_), channel_id=1, source_target_pairs={{0,4},{4,8},{8,12},{12,0},{1,5},{5,9},{9,13},{13,1},{2,6},{6,10},{... | collective-permute-start | bytes 184328 | tf_op jit(solution)/shard_map/ppermute | solution.py:114
  39.4 2.3 %collective-permute-start.15 = (bf16[64,1408]{1,0:T(8,128)(2,1)S(1)}, bf16[64,1408]{1,0:T(8,128)(2,1)S(1)}, u32[]{:S(2)}, u32[]{:S(2)}) collective-permute-start(bf16[64,1408]{1,0:T(8,128)(2,1)S(1)} %hidden_diagonal.2.refs_1_), channel_id=1, source_target_pairs={{0,1},{1,0},{2,3},{3,2},{4,5},{5,4},{6,7},{7,6},{8,9},{9,8},{10,11... | collective-permute-start | bytes 540680 | tf_op jit(solution)/shard_map/ppermute | solution.py:108
  40.3 3.8 %collective-permute-start.16 = (bf16[64,1024]{1,0:T(8,128)(2,1)S(1)}, bf16[64,1024]{1,0:T(8,128)(2,1)S(1)}, u32[]{:S(2)}, u32[]{:S(2)}) collective-permute-start(bf16[64,1024]{1,0:T(8,128)(2,1)S(1)} %hidden_diagonal.3.refs_1_), channel_id=1, source_target_pairs={{0,1},{1,0},{2,3},{3,2},{4,5},{5,4},{6,7},{7,6},{8,9},{9,8},{10,11... | collective-permute-start | bytes 393224 | tf_op jit(solution)/shard_map/ppermute | solution.py:108
  41.9 7.5 %collective-permute-start.21 = (bf16[64,1408]{1,0:T(8,128)(2,1)S(1)}, bf16[64,1408]{1,0:T(8,128)(2,1)S(1)}, u32[]{:S(2)}, u32[]{:S(2)}) collective-permute-start(bf16[64,1408]{1,0:T(8,128)(2,1)S(1)} %get-tuple-element.40.refs_1_), channel_id=1, source_target_pairs={{0,2},{1,3},{2,0},{3,1},{4,6},{5,7},{6,4},{7,5},{8,10},{9,11},{10,... | collective-permute-start | bytes 540680 | tf_op jit(solution)/shard_map/ppermute | solution.py:108
  44.1 7.2 %collective-permute-start.20 = (bf16[64,1024]{1,0:T(8,128)(2,1)S(1)}, bf16[64,1024]{1,0:T(8,128)(2,1)S(1)}, u32[]{:S(2)}, u32[]{:S(2)}) collective-permute-start(bf16[64,1024]{1,0:T(8,128)(2,1)S(1)} %relay.3.refs_1_), channel_id=1, source_target_pairs={{0,2},{1,3},{2,0},{3,1},{4,6},{5,7},{6,4},{7,5},{8,10},{9,11},{10,... | collective-permute-start | bytes 393224 | tf_op jit(solution)/shard_map/ppermute | solution.py:108
  49.6 5.2 %collective-permute-start.24 = (bf16[64,640]{1,0:T(8,128)(2,1)S(1)}, bf16[64,640]{1,0:T(8,128)(2,1)S(1)}, u32[]{:S(2)}, u32[]{:S(2)}) collective-permute-start(bf16[64,640]{1,0:T(8,128)(2,1)S(1)} %get-tuple-element.46.refs_0_), channel_id=1, source_target_pairs={{0,2},{1,3},{2,0},{3,1},{4,6},{5,7},{6,4},{7,5},{8,10},{9,11},{10,... | collective-permute-start | bytes 245768 | tf_op jit(solution)/shard_map/ppermute | solution.py:108
  51.4 3.7 %collective-permute-start.23 = (bf16[64,512]{1,0:T(8,128)(2,1)S(1)}, bf16[64,512]{1,0:T(8,128)(2,1)S(1)}, u32[]{:S(2)}, u32[]{:S(2)}) collective-permute-start(bf16[64,512]{1,0:T(8,128)(2,1)S(1)} %activate.3.refs_1_), channel_id=1, source_target_pairs={{0,1},{1,0},{2,3},{3,2},{4,5},{5,4},{6,7},{7,6},{8,9},{9,8},{10,11... | collective-permute-start | bytes 196616 | tf_op jit(solution)/shard_map/ppermute | solution.py:108
  51.7 4.3 %collective-permute-start.22 = (bf16[64,512]{1,0:T(8,128)(2,1)S(1)}, bf16[64,512]{1,0:T(8,128)(2,1)S(1)}, u32[]{:S(2)}, u32[]{:S(2)}) collective-permute-start(bf16[64,512]{1,0:T(8,128)(2,1)S(1)} %activate.3.refs_1_), channel_id=1, source_target_pairs={{0,2},{1,3},{2,0},{3,1},{4,6},{5,7},{6,4},{7,5},{8,10},{9,11},{10,... | collective-permute-start | bytes 196616 | tf_op jit(solution)/shard_map/ppermute | solution.py:108
  57.7 5.8 %collective-permute-start.28 = (bf16[16,1792]{1,0:T(8,128)(2,1)S(1)}, bf16[16,1792]{1,0:T(8,128)(2,1)S(1)}, u32[]{:S(2)}, u32[]{:S(2)}) collective-permute-start(bf16[16,1792]{1,0:T(8,128)(2,1)S(1)} %get-tuple-element.52), channel_id=1, source_target_pairs={{0,8},{4,12},{8,0},{12,4},{1,9},{5,13},{9,1},{13,5},{2,10},{6,14},... | collective-permute-start | bytes 172040 | tf_op jit(solution)/shard_map/ppermute | solution.py:114
  59.2 4.8 %collective-permute-start.29 = (bf16[16,1792]{1,0:T(8,128)(2,1)S(1)}, bf16[16,1792]{1,0:T(8,128)(2,1)S(1)}, u32[]{:S(2)}, u32[]{:S(2)}) collective-permute-start(bf16[16,1792]{1,0:T(8,128)(2,1)S(1)} %get-tuple-element.53), channel_id=1, source_target_pairs={{0,12},{4,0},{8,4},{12,8},{1,13},{5,1},{9,5},{13,9},{2,14},{6,2},{... | collective-permute-start | bytes 172040 | tf_op jit(solution)/shard_map/ppermute | solution.py:114
  60.0 6.0 %collective-permute-start.30 = (bf16[16,1792]{1,0:T(8,128)(2,1)S(1)}, bf16[16,1792]{1,0:T(8,128)(2,1)S(1)}, u32[]{:S(2)}, u32[]{:S(2)}) collective-permute-start(bf16[16,1792]{1,0:T(8,128)(2,1)S(1)} %get-tuple-element.54), channel_id=1, source_target_pairs={{0,4},{4,8},{8,12},{12,0},{1,5},{5,9},{9,13},{13,1},{2,6},{6,10},{... | collective-permute-start | bytes 172040 | tf_op jit(solution)/shard_map/ppermute | solution.py:114
  (22 other events, 301.9 us)

commit v6 on v5

--- a/solution.py
+++ b/solution.py
@@ -241,7 +241,7 @@
         x[source(a, k, attn, ROWS_PAIRS)] = ref[...]
 
 
-def sums(x, wg, wu, start, cut, out):
+def sums(x, wg, wu, start, cut, out, near=None):
     rows, width = x.shape[0] * x.shape[1], wg.shape[0]
     lhs = x[:, :, :width].reshape(rows, width)
     whole = cut // 256 * 256
@@ -249,17 +249,21 @@
     def columns(w, s, n):
         return w[:, pl.ds(pl.multiple_of(start + s, 128), n)]
 
+    def put(y, s, n):
+        y = y if near is None else y + near[:, s : s + n].astype(F32)
+        out[:, s : s + n] = y.astype(out.dtype)
+
     for base, w in ((0, wg), (cut, wu)):
         for s, n in tiles(whole):
             y = jnp.dot(lhs, columns(w, s, n), preferred_element_type=F32)
-            out[:, base + s : base + s + n] = y.astype(out.dtype)
+            put(y, base + s, n)
     rest = cut - whole
     if rest:
         w = jnp.concatenate([columns(wg, whole, rest), columns(wu, whole, rest)], axis=1)
-        y = jnp.dot(lhs, w, preferred_element_type=F32).astype(out.dtype)
-        out[:, whole:cut] = y[:, :rest]
-        out[:, cut + whole : 2 * cut] = y[:, rest:]
-    if out.shape[1] > 2 * cut:
+        y = jnp.dot(lhs, w, preferred_element_type=F32)
+        put(y[:, :rest], whole, rest)
+        put(y[:, rest:], cut + whole, rest)
+    if near is None and out.shape[1] > 2 * cut:
         out[:, 2 * cut :] = x[:, :, width:].reshape(rows, 128)
 
 
@@ -270,10 +274,11 @@
         sums(x, wg, wu, (f ^ j) * chunk + low, high - low, out)
 
 
-def relay(cut, mine, x, near, out, *squares):
-    rows = mine.shape[0]
-    width = x.shape[2] - 128
-    out[:, : 2 * cut] = (mine[...] + near[:, : 2 * cut].astype(F32)).astype(BF16)
+def relay(chunk, j, low, high, skip, x, near, *refs):
+    wg, wu, out, *squares = refs[skip:]
+    cut, width = high - low, wg.shape[0]
+    rows = x.shape[0] * x.shape[1]
+    sums(x, wg, wu, (lax.axis_index("ffn") ^ j) * chunk + low, cut, out, near)
     if squares:
         both = join3(x[:, :, width:].reshape(rows, 128)) + join3(near[:, 2 * cut :])
         squares[0][...] = jnp.broadcast_to(both, squares[0].shape)
@@ -426,13 +431,14 @@
         others.append(swap(after[0], "ffn", 1))
     far = []
     for i, cut in enumerate(cuts):
-        mine = part([(2, *cut)], "hidden_across", [F32], after)
         more = 128 if i == 0 else 0
         after = call(
-            functools.partial(relay, cut[1] - cut[0]),
-            "relay",
+            functools.partial(relay, chunk, 2, *cut, len(after)),
+            "hidden_across",
             [((total, 2 * (cut[1] - cut[0]) + more), BF16)] + [((total, 128), F32)] * (i == 0),
-            [*mine, x, others[i]],
+            [x, others[i], *after],
+            weights=[w_gate, w_up],
+            specs=[VM] * 2 + [ANY] * len(after),
         )
         far.append(swap(after[0], "ffn", 2))
         if i == 0:

time: 66.7 us -> 66.7 us (level)
    pallas_call x21 -> x19, Pallas kernels: 17.1 us -> 16.9 us  [call(): pl.pallas_call(kernel, out_shape=[jax.ShapeDtypeStruct(s, t) for s, t in...]
  transfers between devices with their start and end apart: 31 -> 31, of which waited for: 17 -> 18; matrix products, arithmetic and copies ran while one was open for 0% -> 0% of each run, Pallas kernels for 13% -> 13%
where the time goes in v6:
time: 66.7 us; the launch traced here: 66.6 us
  starting transfers between devices  26.4 us (40%)
  waiting for transfers between devices  22.3 us (33%)
  Pallas kernels  16.9 us (25%)
  local copies, waits for them, and re-layouts  0.7 us (1%)
    pallas_call x19, Pallas kernels, call(): pl.pallas_call(kernel, out_shape=[jax.ShapeDtypeStruct(s, t) for s, t in...  16.9 us
    ppermute x12, waiting for transfers between devices, spread(): lax.ppermute(blocks[k], axis, [(i, i ^ k if pairs else (i + k) % count) f...  16.8 us
    ppermute x12, starting transfers between devices, spread(): lax.ppermute(blocks[k], axis, [(i, i ^ k if pairs else (i + k) % count) f...  16.1 us
    ppermute x19, starting transfers between devices, swap(): return lax.ppermute(x, axis, [(i, i ^ step) for i in range(count)])  10.3 us
    ppermute x19, waiting for transfers between devices, swap(): return lax.ppermute(x, axis, [(i, i ^ step) for i in range(count)])  5.49 us
  transfers between devices with their start and end apart: 31, of which 18 were waited for; matrix products, arithmetic and copies ran while one was open for 0% of the time, Pallas kernels for 13%

profile of v6, /device:TPU:0, one launch (start us, length us, event | category | flops | bytes accessed | tf_op | source)
XLA Modules:
  0.0 66.6 jit_solution(12955761998825218025)
XLA Ops:
  0.0 3.2 %attend.1 = (bf16[4,16,256]{2,1,0:T(8,128)(2,1)S(1)}, bf16[4,16,256]{2,1,0:T(8,128)(2,1)S(1)}, bf16[4,16,256]{2,1,0:T(8,128)(2,1)S(1)}, bf16[4,16,256]{2,1,0:T(8,128)(2,1)S(1)}) custom-call(s32[4]{0:T(128)} %lens_any.1, bf16[4,16384]{1,0:T(4,128)(2,1)} %q_any.1, bf16[4,1024,512]{2,1,0:T(8,128)(2,1)} %cache.1), custom_call_target="tpu_custom_call" | custom-call | flops 20000000000 | tf_op jit(solution)/shard_map/attend/pallas_call | solution.py:94
  3.3 4.1 %collective-permute-start = (bf16[4,16,256]{2,1,0:T(8,128)(2,1)S(1)}, bf16[4,16,256]{2,1,0:T(8,128)(2,1)S(1)}, u32[]{:S(2)}, u32[]{:S(2)}) collective-permute-start(bf16[4,16,256]{2,1,0:T(8,128)(2,1)S(1)} %get-tuple-element.31), channel_id=1, source_target_pairs={{0,8},{4,12},{8,0},{12,4},{1,9},{5,13},{9,1},{13,5},{2,10},{6,14},... | collective-permute-start | bytes 98312 | tf_op jit(solution)/shard_map/ppermute | solution.py:114
  7.4 1.4 %collective-permute-start.4 = (bf16[4,16,256]{2,1,0:T(8,128)(2,1)S(1)}, bf16[4,16,256]{2,1,0:T(8,128)(2,1)S(1)}, u32[]{:S(2)}, u32[]{:S(2)}) collective-permute-start(bf16[4,16,256]{2,1,0:T(8,128)(2,1)S(1)} %get-tuple-element.32), channel_id=1, source_target_pairs={{0,12},{4,8},{8,4},{12,0},{1,13},{5,9},{9,5},{13,1},{2,14},{6,10},... | collective-permute-start | bytes 98312 | tf_op jit(solution)/shard_map/ppermute | solution.py:114
  9.6 1.7 %collective-permute-start.2 = (bf16[2,4,16,256]{3,2,1,0:T(8,128)(2,1)S(1)}, bf16[2,4,16,256]{3,2,1,0:T(8,128)(2,1)S(1)}, u32[]{:S(2)}, u32[]{:S(2)}) collective-permute-start(bf16[2,4,16,256]{3,2,1,0:T(8,128)(2,1)S(1)} %pack_early.1.refs_0_), channel_id=1, source_target_pairs={{0,2},{1,3},{2,0},{3,1},{4,6},{5,7},{6,4},{7,5},{8,10},{9,11},{10,... | collective-permute-start | bytes 196616 | tf_op jit(solution)/shard_map/ppermute | solution.py:108
  11.3 1.8 %collective-permute-done.4.refs_0_ = bf16[4,16,256]{2,1,0:T(8,128)(2,1)S(1)} collective-permute-done((bf16[4,16,256]{2,1,0:T(8,128)(2,1)S(1)}, bf16[4,16,256]{2,1,0:T(8,128)(2,1)S(1)}, u32[]{:S(2)}, u32[]{:S(2)}) %collective-permute-start.4) | collective-permute-done | bytes 32800 | tf_op jit(solution)/shard_map/ppermute | solution.py:114
  13.1 1.6 %collective-permute-start.7 = (bf16[2,4,16,256]{3,2,1,0:T(8,128)(2,1)S(1)}, bf16[2,4,16,256]{3,2,1,0:T(8,128)(2,1)S(1)}, u32[]{:S(2)}, u32[]{:S(2)}) collective-permute-start(bf16[2,4,16,256]{3,2,1,0:T(8,128)(2,1)S(1)} %pack_late.1.refs_4_), channel_id=1, source_target_pairs={{0,2},{1,3},{2,0},{3,1},{4,6},{5,7},{6,4},{7,5},{8,10},{9,11},{10,... | collective-permute-start | bytes 196616 | tf_op jit(solution)/shard_map/ppermute | solution.py:108
  15.2 2.3 %collective-permute-done.7.refs_6_ = bf16[2,4,16,256]{3,2,1,0:T(8,128)(2,1)S(1)} collective-permute-done((bf16[2,4,16,256]{3,2,1,0:T(8,128)(2,1)S(1)}, bf16[2,4,16,256]{3,2,1,0:T(8,128)(2,1)S(1)}, u32[]{:S(2)}, u32[]{:S(2)}) %collective-permute-start.7) | collective-permute-done | bytes 65568 | tf_op jit(solution)/shard_map/ppermute | solution.py:108
  17.5 1.2 %collective-permute-done.8.refs_7_ = bf16[2,4,16,256]{3,2,1,0:T(8,128)(2,1)S(1)} collective-permute-done((bf16[2,4,16,256]{3,2,1,0:T(8,128)(2,1)S(1)}, bf16[2,4,16,256]{3,2,1,0:T(8,128)(2,1)S(1)}, u32[]{:S(2)}, u32[]{:S(2)}) %collective-permute-start.8) | collective-permute-done | bytes 65568 | tf_op jit(solution)/shard_map/ppermute | solution.py:108
  18.7 2.9 %project.1 = (bf16[16,1792]{1,0:T(8,128)(2,1)S(1)}, bf16[16,1792]{1,0:T(8,128)(2,1)S(1)}, bf16[16,1792]{1,0:T(8,128)(2,1)S(1)}, f32[16,1792]{1,0:T(8,128)S(1)}) custom-call(bf16[2,4,16,256]{3,2,1,0:T(8,128)(2,1)S(1)} %pack_early.1.refs_0_, bf16[2,4,16,256]{3,2,1,0:T(8,128)(2,1)S(1)} %collective-permute-done.1.refs_1_, ...), custom_call_target="tpu_custom_call" | custom-call | flops 3000000000 | tf_op jit(solution)/shard_map/project/pallas_call | solution.py:94
  21.6 1.3 %collective-permute-start.9 = (bf16[16,1792]{1,0:T(8,128)(2,1)S(1)}, bf16[16,1792]{1,0:T(8,128)(2,1)S(1)}, u32[]{:S(2)}, u32[]{:S(2)}) collective-permute-start(bf16[16,1792]{1,0:T(8,128)(2,1)S(1)} %get-tuple-element.35), channel_id=1, source_target_pairs={{0,8},{4,12},{8,0},{12,4},{1,9},{5,13},{9,1},{13,5},{2,10},{6,14},... | collective-permute-start | bytes 172040 | tf_op jit(solution)/shard_map/ppermute | solution.py:114
  25.0 2.5 %collective-permute-done.9.refs_1_ = bf16[16,1792]{1,0:T(8,128)(2,1)S(1)} collective-permute-done((bf16[16,1792]{1,0:T(8,128)(2,1)S(1)}, bf16[16,1792]{1,0:T(8,128)(2,1)S(1)}, u32[]{:S(2)}, u32[]{:S(2)}) %collective-permute-start.9) | collective-permute-done | bytes 57376 | tf_op jit(solution)/shard_map/ppermute | solution.py:114
  28.0 2.0 %collective-permute-done.11.refs_3_ = bf16[16,1792]{1,0:T(8,128)(2,1)S(1)} collective-permute-done((bf16[16,1792]{1,0:T(8,128)(2,1)S(1)}, bf16[16,1792]{1,0:T(8,128)(2,1)S(1)}, u32[]{:S(2)}, u32[]{:S(2)}) %collective-permute-start.11) | collective-permute-done | bytes 57376 | tf_op jit(solution)/shard_map/ppermute | solution.py:114
  30.1 1.6 %collective-permute-start.12 = (bf16[16,1920]{1,0:T(8,128)(2,1)S(1)}, bf16[16,1920]{1,0:T(8,128)(2,1)S(1)}, u32[]{:S(2)}, u32[]{:S(2)}) collective-permute-start(bf16[16,1920]{1,0:T(8,128)(2,1)S(1)} %get-tuple-element.39.refs_0_), channel_id=1, source_target_pairs={{0,8},{4,12},{8,0},{12,4},{1,9},{5,13},{9,1},{13,5},{2,10},{6,14},... | collective-permute-start | bytes 184328 | tf_op jit(solution)/shard_map/ppermute | solution.py:114
  32.3 1.4 %collective-permute-start.14 = (bf16[16,1920]{1,0:T(8,128)(2,1)S(1)}, bf16[16,1920]{1,0:T(8,128)(2,1)S(1)}, u32[]{:S(2)}, u32[]{:S(2)}) collective-permute-start(bf16[16,1920]{1,0:T(8,128)(2,1)S(1)} %get-tuple-element.39.refs_0_), channel_id=1, source_target_pairs={{0,4},{4,8},{8,12},{12,0},{1,5},{5,9},{9,13},{13,1},{2,6},{6,10},{... | collective-permute-start | bytes 184328 | tf_op jit(solution)/shard_map/ppermute | solution.py:114
  33.7 2.1 %collective-permute-done.12.refs_1_ = bf16[16,1920]{1,0:T(8,128)(2,1)S(1)} collective-permute-done((bf16[16,1920]{1,0:T(8,128)(2,1)S(1)}, bf16[16,1920]{1,0:T(8,128)(2,1)S(1)}, u32[]{:S(2)}, u32[]{:S(2)}) %collective-permute-start.12) | collective-permute-done | bytes 61472 | tf_op jit(solution)/shard_map/ppermute | solution.py:114
  36.7 1.6 %collective-permute-done.14.refs_3_ = bf16[16,1920]{1,0:T(8,128)(2,1)S(1)} collective-permute-done((bf16[16,1920]{1,0:T(8,128)(2,1)S(1)}, bf16[16,1920]{1,0:T(8,128)(2,1)S(1)}, u32[]{:S(2)}, u32[]{:S(2)}) %collective-permute-start.14) | collective-permute-done | bytes 61472 | tf_op jit(solution)/shard_map/ppermute | solution.py:114
  41.8 1.4 %collective-permute-start.21 = (bf16[64,1408]{1,0:T(8,128)(2,1)S(1)}, bf16[64,1408]{1,0:T(8,128)(2,1)S(1)}, u32[]{:S(2)}, u32[]{:S(2)}) collective-permute-start(bf16[64,1408]{1,0:T(8,128)(2,1)S(1)} %get-tuple-element.40.refs_0_), channel_id=1, source_target_pairs={{0,2},{1,3},{2,0},{3,1},{4,6},{5,7},{6,4},{7,5},{8,10},{9,11},{10,... | collective-permute-start | bytes 540680 | tf_op jit(solution)/shard_map/ppermute | solution.py:108
  44.8 1.6 %hidden_beside.1 = (bf16[64,768]{1,0:T(8,128)(2,1)S(1)}, bf16[64,768]{1,0:T(8,128)(2,1)S(1)}, bf16[64,768]{1,0:T(8,128)(2,1)S(1)}) custom-call(bf16[4,16,1920]{2,1,0:T(8,128)(2,1)S(1)} %gather_rows.1.refs_0_.x, bf16[64,1024]{1,0:T(8,128)(2,1)S(1)} %hidden_across.3.refs_1_, bf16[1792,4608]{1,0:T(8,128)(2,1)S(1)} %bitcast.1, bf16[1792,4608]{1,0:T(8,128)(2,1)S(1)} %bitcast.3), custom_call_target="tpu_custom_call" | custom-call | tf_op jit(solution)/shard_map/hidden_beside/pallas_call | solution.py:94
  47.0 1.6 %hidden_own.1.mine = f32[64,2304]{1,0:T(8,128)S(1)} custom-call(bf16[4,16,1920]{2,1,0:T(8,128)(2,1)S(1)} %gather_rows.1.refs_0_.x, bf16[64,768]{1,0:T(8,128)(2,1)S(1)} %get-tuple-element.42.refs_1_, bf16[1792,4608]{1,0:T(8,128)(2,1)S(1)} %bitcast.1, bf16[1792,4608]{1,0:T(8,128)(2,1)S(1)} %bitcast.3), custom_call_target="tpu_custom_call" | custom-call | flops 550000000 | tf_op jit(solution)/shard_map/hidden_own/pallas_call | solution.py:94
  49.5 1.4 %collective-permute-start.24 = (bf16[64,640]{1,0:T(8,128)(2,1)S(1)}, bf16[64,640]{1,0:T(8,128)(2,1)S(1)}, u32[]{:S(2)}, u32[]{:S(2)}) collective-permute-start(bf16[64,640]{1,0:T(8,128)(2,1)S(1)} %get-tuple-element.46.refs_0_), channel_id=1, source_target_pairs={{0,2},{1,3},{2,0},{3,1},{4,6},{5,7},{6,4},{7,5},{8,10},{9,11},{10,... | collective-permute-start | bytes 245768 | tf_op jit(solution)/shard_map/ppermute | solution.py:108
  51.6 1.3 %collective-permute-start.22 = (bf16[64,512]{1,0:T(8,128)(2,1)S(1)}, bf16[64,512]{1,0:T(8,128)(2,1)S(1)}, u32[]{:S(2)}, u32[]{:S(2)}) collective-permute-start(bf16[64,512]{1,0:T(8,128)(2,1)S(1)} %activate.3.refs_1_), channel_id=1, source_target_pairs={{0,2},{1,3},{2,0},{3,1},{4,6},{5,7},{6,4},{7,5},{8,10},{9,11},{10,... | collective-permute-start | bytes 196616 | tf_op jit(solution)/shard_map/ppermute | solution.py:108
  57.8 1.4 %collective-permute-start.28 = (bf16[16,1792]{1,0:T(8,128)(2,1)S(1)}, bf16[16,1792]{1,0:T(8,128)(2,1)S(1)}, u32[]{:S(2)}, u32[]{:S(2)}) collective-permute-start(bf16[16,1792]{1,0:T(8,128)(2,1)S(1)} %get-tuple-element.52), channel_id=1, source_target_pairs={{0,8},{4,12},{8,0},{12,4},{1,9},{5,13},{9,1},{13,5},{2,10},{6,14},... | collective-permute-start | bytes 172040 | tf_op jit(solution)/shard_map/ppermute | solution.py:114
  61.2 2.3 %collective-permute-done.28.refs_2_ = bf16[16,1792]{1,0:T(8,128)(2,1)S(1)} collective-permute-done((bf16[16,1792]{1,0:T(8,128)(2,1)S(1)}, bf16[16,1792]{1,0:T(8,128)(2,1)S(1)}, u32[]{:S(2)}, u32[]{:S(2)}) %collective-permute-start.28) | collective-permute-done | bytes 57376 | tf_op jit(solution)/shard_map/ppermute | solution.py:114
  64.0 2.0 %collective-permute-done.30.refs_4_ = bf16[16,1792]{1,0:T(8,128)(2,1)S(1)} collective-permute-done((bf16[16,1792]{1,0:T(8,128)(2,1)S(1)}, bf16[16,1792]{1,0:T(8,128)(2,1)S(1)}, u32[]{:S(2)}, u32[]{:S(2)}) %collective-permute-start.30) | collective-permute-done | bytes 57376 | tf_op jit(solution)/shard_map/ppermute | solution.py:114
  (91 shorter events, 20.9 us)
Async XLA Ops:
  3.3 6.4 %collective-permute-start = (bf16[4,16,256]{2,1,0:T(8,128)(2,1)S(1)}, bf16[4,16,256]{2,1,0:T(8,128)(2,1)S(1)}, u32[]{:S(2)}, u32[]{:S(2)}) collective-permute-start(bf16[4,16,256]{2,1,0:T(8,128)(2,1)S(1)} %get-tuple-element.31), channel_id=1, source_target_pairs={{0,8},{4,12},{8,0},{12,4},{1,9},{5,13},{9,1},{13,5},{2,10},{6,14},... | collective-permute-start | bytes 98312 | tf_op jit(solution)/shard_map/ppermute | solution.py:114
  7.4 5.7 %collective-permute-start.4 = (bf16[4,16,256]{2,1,0:T(8,128)(2,1)S(1)}, bf16[4,16,256]{2,1,0:T(8,128)(2,1)S(1)}, u32[]{:S(2)}, u32[]{:S(2)}) collective-permute-start(bf16[4,16,256]{2,1,0:T(8,128)(2,1)S(1)} %get-tuple-element.32), channel_id=1, source_target_pairs={{0,12},{4,8},{8,4},{12,0},{1,13},{5,9},{9,5},{13,1},{2,14},{6,10},... | collective-permute-start | bytes 98312 | tf_op jit(solution)/shard_map/ppermute | solution.py:114
  8.7 4.4 %collective-permute-start.5 = (bf16[4,16,256]{2,1,0:T(8,128)(2,1)S(1)}, bf16[4,16,256]{2,1,0:T(8,128)(2,1)S(1)}, u32[]{:S(2)}, u32[]{:S(2)}) collective-permute-start(bf16[4,16,256]{2,1,0:T(8,128)(2,1)S(1)} %get-tuple-element.33), channel_id=1, source_target_pairs={{0,4},{4,0},{8,12},{12,8},{1,5},{5,1},{9,13},{13,9},{2,6},{6,2},{1... | collective-permute-start | bytes 98312 | tf_op jit(solution)/shard_map/ppermute | solution.py:114
  9.6 5.6 %collective-permute-start.2 = (bf16[2,4,16,256]{3,2,1,0:T(8,128)(2,1)S(1)}, bf16[2,4,16,256]{3,2,1,0:T(8,128)(2,1)S(1)}, u32[]{:S(2)}, u32[]{:S(2)}) collective-permute-start(bf16[2,4,16,256]{3,2,1,0:T(8,128)(2,1)S(1)} %pack_early.1.refs_0_), channel_id=1, source_target_pairs={{0,2},{1,3},{2,0},{3,1},{4,6},{5,7},{6,4},{7,5},{8,10},{9,11},{10,... | collective-permute-start | bytes 196616 | tf_op jit(solution)/shard_map/ppermute | solution.py:108
  13.1 4.3 %collective-permute-start.7 = (bf16[2,4,16,256]{3,2,1,0:T(8,128)(2,1)S(1)}, bf16[2,4,16,256]{3,2,1,0:T(8,128)(2,1)S(1)}, u32[]{:S(2)}, u32[]{:S(2)}) collective-permute-start(bf16[2,4,16,256]{3,2,1,0:T(8,128)(2,1)S(1)} %pack_late.1.refs_4_), channel_id=1, source_target_pairs={{0,2},{1,3},{2,0},{3,1},{4,6},{5,7},{6,4},{7,5},{8,10},{9,11},{10,... | collective-permute-start | bytes 196616 | tf_op jit(solution)/shard_map/ppermute | solution.py:108
  14.7 2.8 %collective-permute-start.1 = (bf16[2,4,16,256]{3,2,1,0:T(8,128)(2,1)S(1)}, bf16[2,4,16,256]{3,2,1,0:T(8,128)(2,1)S(1)}, u32[]{:S(2)}, u32[]{:S(2)}) collective-permute-start(bf16[2,4,16,256]{3,2,1,0:T(8,128)(2,1)S(1)} %pack_early.1.refs_0_), channel_id=1, source_target_pairs={{0,1},{1,0},{2,3},{3,2},{4,5},{5,4},{6,7},{7,6},{8,9},{9,8},{10,11... | collective-permute-start | bytes 196616 | tf_op jit(solution)/shard_map/ppermute | solution.py:108
  14.7 2.8 %collective-permute-start.6 = (bf16[2,4,16,256]{3,2,1,0:T(8,128)(2,1)S(1)}, bf16[2,4,16,256]{3,2,1,0:T(8,128)(2,1)S(1)}, u32[]{:S(2)}, u32[]{:S(2)}) collective-permute-start(bf16[2,4,16,256]{3,2,1,0:T(8,128)(2,1)S(1)} %pack_late.1.refs_4_), channel_id=1, source_target_pairs={{0,1},{1,0},{2,3},{3,2},{4,5},{5,4},{6,7},{7,6},{8,9},{9,8},{10,11... | collective-permute-start | bytes 196616 | tf_op jit(solution)/shard_map/ppermute | solution.py:108
  15.2 2.3 %collective-permute-start.3 = (bf16[2,4,16,256]{3,2,1,0:T(8,128)(2,1)S(1)}, bf16[2,4,16,256]{3,2,1,0:T(8,128)(2,1)S(1)}, u32[]{:S(2)}, u32[]{:S(2)}) collective-permute-start(bf16[2,4,16,256]{3,2,1,0:T(8,128)(2,1)S(1)} %collective-permute-done.2.refs_2_), channel_id=1, source_target_pairs={{0,1},{1,0},{2,3},{3,2},{4,5},{5,4},{6,7},{7,6},{8,9},{9,8},{10,11... | collective-permute-start | bytes 196616 | tf_op jit(solution)/shard_map/ppermute | solution.py:108
  21.6 5.8 %collective-permute-start.9 = (bf16[16,1792]{1,0:T(8,128)(2,1)S(1)}, bf16[16,1792]{1,0:T(8,128)(2,1)S(1)}, u32[]{:S(2)}, u32[]{:S(2)}) collective-permute-start(bf16[16,1792]{1,0:T(8,128)(2,1)S(1)} %get-tuple-element.35), channel_id=1, source_target_pairs={{0,8},{4,12},{8,0},{12,4},{1,9},{5,13},{9,1},{13,5},{2,10},{6,14},... | collective-permute-start | bytes 172040 | tf_op jit(solution)/shard_map/ppermute | solution.py:114
  22.9 5.0 %collective-permute-start.10 = (bf16[16,1792]{1,0:T(8,128)(2,1)S(1)}, bf16[16,1792]{1,0:T(8,128)(2,1)S(1)}, u32[]{:S(2)}, u32[]{:S(2)}) collective-permute-start(bf16[16,1792]{1,0:T(8,128)(2,1)S(1)} %get-tuple-element.36), channel_id=1, source_target_pairs={{0,12},{4,0},{8,4},{12,8},{1,13},{5,1},{9,5},{13,9},{2,14},{6,2},{... | collective-permute-start | bytes 172040 | tf_op jit(solution)/shard_map/ppermute | solution.py:114
  24.0 6.0 %collective-permute-start.11 = (bf16[16,1792]{1,0:T(8,128)(2,1)S(1)}, bf16[16,1792]{1,0:T(8,128)(2,1)S(1)}, u32[]{:S(2)}, u32[]{:S(2)}) collective-permute-start(bf16[16,1792]{1,0:T(8,128)(2,1)S(1)} %get-tuple-element.37), channel_id=1, source_target_pairs={{0,4},{4,8},{8,12},{12,0},{1,5},{5,9},{9,13},{13,1},{2,6},{6,10},{... | collective-permute-start | bytes 172040 | tf_op jit(solution)/shard_map/ppermute | solution.py:114
  30.1 5.7 %collective-permute-start.12 = (bf16[16,1920]{1,0:T(8,128)(2,1)S(1)}, bf16[16,1920]{1,0:T(8,128)(2,1)S(1)}, u32[]{:S(2)}, u32[]{:S(2)}) collective-permute-start(bf16[16,1920]{1,0:T(8,128)(2,1)S(1)} %get-tuple-element.39.refs_0_), channel_id=1, source_target_pairs={{0,8},{4,12},{8,0},{12,4},{1,9},{5,13},{9,1},{13,5},{2,10},{6,14},... | collective-permute-start | bytes 184328 | tf_op jit(solution)/shard_map/ppermute | solution.py:114
  31.7 5.0 %collective-permute-start.13 = (bf16[16,1920]{1,0:T(8,128)(2,1)S(1)}, bf16[16,1920]{1,0:T(8,128)(2,1)S(1)}, u32[]{:S(2)}, u32[]{:S(2)}) collective-permute-start(bf16[16,1920]{1,0:T(8,128)(2,1)S(1)} %get-tuple-element.39.refs_0_), channel_id=1, source_target_pairs={{0,12},{4,0},{8,4},{12,8},{1,13},{5,1},{9,5},{13,9},{2,14},{6,2},{... | collective-permute-start | bytes 184328 | tf_op jit(solution)/shard_map/ppermute | solution.py:114
  32.3 6.0 %collective-permute-start.14 = (bf16[16,1920]{1,0:T(8,128)(2,1)S(1)}, bf16[16,1920]{1,0:T(8,128)(2,1)S(1)}, u32[]{:S(2)}, u32[]{:S(2)}) collective-permute-start(bf16[16,1920]{1,0:T(8,128)(2,1)S(1)} %get-tuple-element.39.refs_0_), channel_id=1, source_target_pairs={{0,4},{4,8},{8,12},{12,0},{1,5},{5,9},{9,13},{13,1},{2,6},{6,10},{... | collective-permute-start | bytes 184328 | tf_op jit(solution)/shard_map/ppermute | solution.py:114
  40.3 2.9 %collective-permute-start.15 = (bf16[64,1024]{1,0:T(8,128)(2,1)S(1)}, bf16[64,1024]{1,0:T(8,128)(2,1)S(1)}, u32[]{:S(2)}, u32[]{:S(2)}) collective-permute-start(bf16[64,1024]{1,0:T(8,128)(2,1)S(1)} %hidden_diagonal.3.refs_0_), channel_id=1, source_target_pairs={{0,1},{1,0},{2,3},{3,2},{4,5},{5,4},{6,7},{7,6},{8,9},{9,8},{10,11... | collective-permute-start | bytes 393224 | tf_op jit(solution)/shard_map/ppermute | solution.py:108
  41.8 7.5 %collective-permute-start.21 = (bf16[64,1408]{1,0:T(8,128)(2,1)S(1)}, bf16[64,1408]{1,0:T(8,128)(2,1)S(1)}, u32[]{:S(2)}, u32[]{:S(2)}) collective-permute-start(bf16[64,1408]{1,0:T(8,128)(2,1)S(1)} %get-tuple-element.40.refs_0_), channel_id=1, source_target_pairs={{0,2},{1,3},{2,0},{3,1},{4,6},{5,7},{6,4},{7,5},{8,10},{9,11},{10,... | collective-permute-start | bytes 540680 | tf_op jit(solution)/shard_map/ppermute | solution.py:108
  44.0 7.3 %collective-permute-start.20 = (bf16[64,1024]{1,0:T(8,128)(2,1)S(1)}, bf16[64,1024]{1,0:T(8,128)(2,1)S(1)}, u32[]{:S(2)}, u32[]{:S(2)}) collective-permute-start(bf16[64,1024]{1,0:T(8,128)(2,1)S(1)} %hidden_across.3.refs_1_), channel_id=1, source_target_pairs={{0,2},{1,3},{2,0},{3,1},{4,6},{5,7},{6,4},{7,5},{8,10},{9,11},{10,... | collective-permute-start | bytes 393224 | tf_op jit(solution)/shard_map/ppermute | solution.py:108
  46.4 2.2 %collective-permute-start.17 = (bf16[64,768]{1,0:T(8,128)(2,1)S(1)}, bf16[64,768]{1,0:T(8,128)(2,1)S(1)}, u32[]{:S(2)}, u32[]{:S(2)}) collective-permute-start(bf16[64,768]{1,0:T(8,128)(2,1)S(1)} %get-tuple-element.42.refs_1_), channel_id=1, source_target_pairs={{0,1},{1,0},{2,3},{3,2},{4,5},{5,4},{6,7},{7,6},{8,9},{9,8},{10,11... | collective-permute-start | bytes 294920 | tf_op jit(solution)/shard_map/ppermute | solution.py:108
  49.5 5.3 %collective-permute-start.24 = (bf16[64,640]{1,0:T(8,128)(2,1)S(1)}, bf16[64,640]{1,0:T(8,128)(2,1)S(1)}, u32[]{:S(2)}, u32[]{:S(2)}) collective-permute-start(bf16[64,640]{1,0:T(8,128)(2,1)S(1)} %get-tuple-element.46.refs_0_), channel_id=1, source_target_pairs={{0,2},{1,3},{2,0},{3,1},{4,6},{5,7},{6,4},{7,5},{8,10},{9,11},{10,... | collective-permute-start | bytes 245768 | tf_op jit(solution)/shard_map/ppermute | solution.py:108
  51.4 3.5 %collective-permute-start.23 = (bf16[64,512]{1,0:T(8,128)(2,1)S(1)}, bf16[64,512]{1,0:T(8,128)(2,1)S(1)}, u32[]{:S(2)}, u32[]{:S(2)}) collective-permute-start(bf16[64,512]{1,0:T(8,128)(2,1)S(1)} %activate.3.refs_1_), channel_id=1, source_target_pairs={{0,1},{1,0},{2,3},{3,2},{4,5},{5,4},{6,7},{7,6},{8,9},{9,8},{10,11... | collective-permute-start | bytes 196616 | tf_op jit(solution)/shard_map/ppermute | solution.py:108
  51.6 4.4 %collective-permute-start.22 = (bf16[64,512]{1,0:T(8,128)(2,1)S(1)}, bf16[64,512]{1,0:T(8,128)(2,1)S(1)}, u32[]{:S(2)}, u32[]{:S(2)}) collective-permute-start(bf16[64,512]{1,0:T(8,128)(2,1)S(1)} %activate.3.refs_1_), channel_id=1, source_target_pairs={{0,2},{1,3},{2,0},{3,1},{4,6},{5,7},{6,4},{7,5},{8,10},{9,11},{10,... | collective-permute-start | bytes 196616 | tf_op jit(solution)/shard_map/ppermute | solution.py:108
  57.8 5.8 %collective-permute-start.28 = (bf16[16,1792]{1,0:T(8,128)(2,1)S(1)}, bf16[16,1792]{1,0:T(8,128)(2,1)S(1)}, u32[]{:S(2)}, u32[]{:S(2)}) collective-permute-start(bf16[16,1792]{1,0:T(8,128)(2,1)S(1)} %get-tuple-element.52), channel_id=1, source_target_pairs={{0,8},{4,12},{8,0},{12,4},{1,9},{5,13},{9,1},{13,5},{2,10},{6,14},... | collective-permute-start | bytes 172040 | tf_op jit(solution)/shard_map/ppermute | solution.py:114
  59.2 4.8 %collective-permute-start.29 = (bf16[16,1792]{1,0:T(8,128)(2,1)S(1)}, bf16[16,1792]{1,0:T(8,128)(2,1)S(1)}, u32[]{:S(2)}, u32[]{:S(2)}) collective-permute-start(bf16[16,1792]{1,0:T(8,128)(2,1)S(1)} %get-tuple-element.53), channel_id=1, source_target_pairs={{0,12},{4,0},{8,4},{12,8},{1,13},{5,1},{9,5},{13,9},{2,14},{6,2},{... | collective-permute-start | bytes 172040 | tf_op jit(solution)/shard_map/ppermute | solution.py:114
  60.0 6.0 %collective-permute-start.30 = (bf16[16,1792]{1,0:T(8,128)(2,1)S(1)}, bf16[16,1792]{1,0:T(8,128)(2,1)S(1)}, u32[]{:S(2)}, u32[]{:S(2)}) collective-permute-start(bf16[16,1792]{1,0:T(8,128)(2,1)S(1)} %get-tuple-element.54), channel_id=1, source_target_pairs={{0,4},{4,8},{8,12},{12,0},{1,5},{5,9},{9,13},{13,1},{2,6},{6,10},{... | collective-permute-start | bytes 172040 | tf_op jit(solution)/shard_map/ppermute | solution.py:114
  (22 other events, 301.6 us)

commit v7 on v6

--- a/solution.py
+++ b/solution.py
@@ -23,8 +23,8 @@
 ROWS_PAIRS = False
 END_PAIRS = False
 ATTEND_US = 20
-SETTLE_US = 3
-GATHER_US = 3
+SETTLE_US = 6
+GATHER_US = 0.05
 ACTIVATE_US = 4
 OWN_US = 0.55
 DOWN_US = 0.05
@@ -234,11 +234,13 @@
     xg[:, width:] = split3(jnp.sum(total * total, axis=1, keepdims=True))
 
 
-def gather_rows(attn, *refs):
-    x = refs[attn]
+def gather_rows(attn, chunk, job, *refs):
+    wg, wu, x, out = refs[attn:]
     a = lax.axis_index("attn")
-    for ref, k in zip(refs, (0, *ROWS_STEPS)):
+    for ref, k in zip(refs[:attn], (0, *ROWS_STEPS)):
         x[source(a, k, attn, ROWS_PAIRS)] = ref[...]
+    j, low, high = job
+    sums(x, wg, wu, (lax.axis_index("ffn") ^ j) * chunk + low, high - low, out)
 
 
 def sums(x, wg, wu, start, cut, out, near=None):
@@ -402,14 +404,6 @@
         flops=int(SETTLE_US * US),
     )
     xs = [xg, *spread([xg] * attn, "attn", ROWS_STEPS, ROWS_PAIRS)]
-    (x,) = call(
-        functools.partial(gather_rows, attn),
-        "gather_rows",
-        [((attn, own_rows, width + 128), BF16)],
-        xs,
-        flops=int(GATHER_US * US),
-    )
-
     middle = (chunk // 128 * 5 + 8) // 9 * 128
     cuts = [(0, middle), (middle, chunk)]
 
@@ -425,10 +419,19 @@
             flops=int(cost * US),
         )
 
-    others, after = [], []
-    for i, cut in enumerate(cuts):
-        after = part([(3, *cut)], "hidden_diagonal", [BF16], after, 128 if i == 0 else 0)
-        others.append(swap(after[0], "ffn", 1))
+    x, first = call(
+        functools.partial(gather_rows, attn, chunk, (3, *cuts[0])),
+        "hidden_diagonal",
+        [
+            ((attn, own_rows, width + 128), BF16),
+            ((total, 2 * middle + 128), BF16),
+        ],
+        xs,
+        weights=[w_gate, w_up],
+        flops=int(GATHER_US * US),
+    )
+    after = part([(3, *cuts[1])], "hidden_diagonal", [BF16], [first])
+    others = [swap(first, "ffn", 1), swap(after[0], "ffn", 1)]
     far = []
     for i, cut in enumerate(cuts):
         more = 128 if i == 0 else 0

time: 66.7 us -> 66.6 us (level)
    pallas_call x19 -> x18, Pallas kernels: 16.9 us -> 16.9 us  [call(): pl.pallas_call(kernel, out_shape=[jax.ShapeDtypeStruct(s, t) for s, t in...]
where the time goes in v7:
time: 66.6 us; the launch traced here: 66.5 us
  starting transfers between devices  26.5 us (40%)
  waiting for transfers between devices  22.2 us (33%)
  Pallas kernels  16.9 us (25%)
  local copies, waits for them, and re-layouts  0.69 us (1%)
    pallas_call x18, Pallas kernels, call(): pl.pallas_call(kernel, out_shape=[jax.ShapeDtypeStruct(s, t) for s, t in...  16.9 us
    ppermute x12, waiting for transfers between devices, spread(): lax.ppermute(blocks[k], axis, [(i, i ^ k if pairs else (i + k) % count) f...  16.8 us
    ppermute x12, starting transfers between devices, spread(): lax.ppermute(blocks[k], axis, [(i, i ^ k if pairs else (i + k) % count) f...  16.1 us
    ppermute x19, starting transfers between devices, swap(): return lax.ppermute(x, axis, [(i, i ^ step) for i in range(count)])  10.4 us
    ppermute x19, waiting for transfers between devices, swap(): return lax.ppermute(x, axis, [(i, i ^ step) for i in range(count)])  5.4 us
  transfers between devices with their start and end apart: 31, of which 18 were waited for; matrix products, arithmetic and copies ran while one was open for 0% of the time, Pallas kernels for 13%

profile of v7, /device:TPU:0, one launch (start us, length us, event | category | flops | bytes accessed | tf_op | source)
XLA Modules:
  0.0 66.5 jit_solution(13022575838655030175)
XLA Ops:
  0.0 3.2 %attend.1 = (bf16[4,16,256]{2,1,0:T(8,128)(2,1)S(1)}, bf16[4,16,256]{2,1,0:T(8,128)(2,1)S(1)}, bf16[4,16,256]{2,1,0:T(8,128)(2,1)S(1)}, bf16[4,16,256]{2,1,0:T(8,128)(2,1)S(1)}) custom-call(s32[4]{0:T(128)} %lens_any.1, bf16[4,16384]{1,0:T(4,128)(2,1)} %q_any.1, bf16[4,1024,512]{2,1,0:T(8,128)(2,1)} %cache.1), custom_call_target="tpu_custom_call" | custom-call | flops 20000000000 | tf_op jit(solution)/shard_map/attend/pallas_call | solution.py:94
  3.3 4.1 %collective-permute-start = (bf16[4,16,256]{2,1,0:T(8,128)(2,1)S(1)}, bf16[4,16,256]{2,1,0:T(8,128)(2,1)S(1)}, u32[]{:S(2)}, u32[]{:S(2)}) collective-permute-start(bf16[4,16,256]{2,1,0:T(8,128)(2,1)S(1)} %get-tuple-element.33), channel_id=1, source_target_pairs={{0,8},{4,12},{8,0},{12,4},{1,9},{5,13},{9,1},{13,5},{2,10},{6,14},... | collective-permute-start | bytes 98312 | tf_op jit(solution)/shard_map/ppermute | solution.py:114
  7.4 1.4 %collective-permute-start.4 = (bf16[4,16,256]{2,1,0:T(8,128)(2,1)S(1)}, bf16[4,16,256]{2,1,0:T(8,128)(2,1)S(1)}, u32[]{:S(2)}, u32[]{:S(2)}) collective-permute-start(bf16[4,16,256]{2,1,0:T(8,128)(2,1)S(1)} %get-tuple-element.34), channel_id=1, source_target_pairs={{0,12},{4,8},{8,4},{12,0},{1,13},{5,9},{9,5},{13,1},{2,14},{6,10},... | collective-permute-start | bytes 98312 | tf_op jit(solution)/shard_map/ppermute | solution.py:114
  9.6 1.7 %collective-permute-start.2 = (bf16[2,4,16,256]{3,2,1,0:T(8,128)(2,1)S(1)}, bf16[2,4,16,256]{3,2,1,0:T(8,128)(2,1)S(1)}, u32[]{:S(2)}, u32[]{:S(2)}) collective-permute-start(bf16[2,4,16,256]{3,2,1,0:T(8,128)(2,1)S(1)} %pack_early.1.refs_0_), channel_id=1, source_target_pairs={{0,2},{1,3},{2,0},{3,1},{4,6},{5,7},{6,4},{7,5},{8,10},{9,11},{10,... | collective-permute-start | bytes 196616 | tf_op jit(solution)/shard_map/ppermute | solution.py:108
  11.3 1.8 %collective-permute-done.4.refs_0_ = bf16[4,16,256]{2,1,0:T(8,128)(2,1)S(1)} collective-permute-done((bf16[4,16,256]{2,1,0:T(8,128)(2,1)S(1)}, bf16[4,16,256]{2,1,0:T(8,128)(2,1)S(1)}, u32[]{:S(2)}, u32[]{:S(2)}) %collective-permute-start.4) | collective-permute-done | bytes 32800 | tf_op jit(solution)/shard_map/ppermute | solution.py:114
  13.1 1.6 %collective-permute-start.7 = (bf16[2,4,16,256]{3,2,1,0:T(8,128)(2,1)S(1)}, bf16[2,4,16,256]{3,2,1,0:T(8,128)(2,1)S(1)}, u32[]{:S(2)}, u32[]{:S(2)}) collective-permute-start(bf16[2,4,16,256]{3,2,1,0:T(8,128)(2,1)S(1)} %pack_late.1.refs_4_), channel_id=1, source_target_pairs={{0,2},{1,3},{2,0},{3,1},{4,6},{5,7},{6,4},{7,5},{8,10},{9,11},{10,... | collective-permute-start | bytes 196616 | tf_op jit(solution)/shard_map/ppermute | solution.py:108
  15.2 2.3 %collective-permute-done.7.refs_6_ = bf16[2,4,16,256]{3,2,1,0:T(8,128)(2,1)S(1)} collective-permute-done((bf16[2,4,16,256]{3,2,1,0:T(8,128)(2,1)S(1)}, bf16[2,4,16,256]{3,2,1,0:T(8,128)(2,1)S(1)}, u32[]{:S(2)}, u32[]{:S(2)}) %collective-permute-start.7) | collective-permute-done | bytes 65568 | tf_op jit(solution)/shard_map/ppermute | solution.py:108
  18.7 2.9 %project.1 = (bf16[16,1792]{1,0:T(8,128)(2,1)S(1)}, bf16[16,1792]{1,0:T(8,128)(2,1)S(1)}, bf16[16,1792]{1,0:T(8,128)(2,1)S(1)}, f32[16,1792]{1,0:T(8,128)S(1)}) custom-call(bf16[2,4,16,256]{3,2,1,0:T(8,128)(2,1)S(1)} %pack_early.1.refs_0_, bf16[2,4,16,256]{3,2,1,0:T(8,128)(2,1)S(1)} %collective-permute-done.1.refs_1_, ...), custom_call_target="tpu_custom_call" | custom-call | flops 3000000000 | tf_op jit(solution)/shard_map/project/pallas_call | solution.py:94
  21.6 1.3 %collective-permute-start.9 = (bf16[16,1792]{1,0:T(8,128)(2,1)S(1)}, bf16[16,1792]{1,0:T(8,128)(2,1)S(1)}, u32[]{:S(2)}, u32[]{:S(2)}) collective-permute-start(bf16[16,1792]{1,0:T(8,128)(2,1)S(1)} %get-tuple-element.37), channel_id=1, source_target_pairs={{0,8},{4,12},{8,0},{12,4},{1,9},{5,13},{9,1},{13,5},{2,10},{6,14},... | collective-permute-start | bytes 172040 | tf_op jit(solution)/shard_map/ppermute | solution.py:114
  25.0 2.5 %collective-permute-done.9.refs_1_ = bf16[16,1792]{1,0:T(8,128)(2,1)S(1)} collective-permute-done((bf16[16,1792]{1,0:T(8,128)(2,1)S(1)}, bf16[16,1792]{1,0:T(8,128)(2,1)S(1)}, u32[]{:S(2)}, u32[]{:S(2)}) %collective-permute-start.9) | collective-permute-done | bytes 57376 | tf_op jit(solution)/shard_map/ppermute | solution.py:114
  28.0 2.0 %collective-permute-done.11.refs_3_ = bf16[16,1792]{1,0:T(8,128)(2,1)S(1)} collective-permute-done((bf16[16,1792]{1,0:T(8,128)(2,1)S(1)}, bf16[16,1792]{1,0:T(8,128)(2,1)S(1)}, u32[]{:S(2)}, u32[]{:S(2)}) %collective-permute-start.11) | collective-permute-done | bytes 57376 | tf_op jit(solution)/shard_map/ppermute | solution.py:114
  30.1 1.6 %collective-permute-start.12 = (bf16[16,1920]{1,0:T(8,128)(2,1)S(1)}, bf16[16,1920]{1,0:T(8,128)(2,1)S(1)}, u32[]{:S(2)}, u32[]{:S(2)}) collective-permute-start(bf16[16,1920]{1,0:T(8,128)(2,1)S(1)} %get-tuple-element.41.refs_0_), channel_id=1, source_target_pairs={{0,8},{4,12},{8,0},{12,4},{1,9},{5,13},{9,1},{13,5},{2,10},{6,14},... | collective-permute-start | bytes 184328 | tf_op jit(solution)/shard_map/ppermute | solution.py:114
  32.3 1.4 %collective-permute-start.14 = (bf16[16,1920]{1,0:T(8,128)(2,1)S(1)}, bf16[16,1920]{1,0:T(8,128)(2,1)S(1)}, u32[]{:S(2)}, u32[]{:S(2)}) collective-permute-start(bf16[16,1920]{1,0:T(8,128)(2,1)S(1)} %get-tuple-element.41.refs_0_), channel_id=1, source_target_pairs={{0,4},{4,8},{8,12},{12,0},{1,5},{5,9},{9,13},{13,1},{2,6},{6,10},{... | collective-permute-start | bytes 184328 | tf_op jit(solution)/shard_map/ppermute | solution.py:114
  33.7 2.1 %collective-permute-done.12.refs_1_ = bf16[16,1920]{1,0:T(8,128)(2,1)S(1)} collective-permute-done((bf16[16,1920]{1,0:T(8,128)(2,1)S(1)}, bf16[16,1920]{1,0:T(8,128)(2,1)S(1)}, u32[]{:S(2)}, u32[]{:S(2)}) %collective-permute-start.12) | collective-permute-done | bytes 61472 | tf_op jit(solution)/shard_map/ppermute | solution.py:114
  36.6 1.6 %collective-permute-done.14.refs_3_ = bf16[16,1920]{1,0:T(8,128)(2,1)S(1)} collective-permute-done((bf16[16,1920]{1,0:T(8,128)(2,1)S(1)}, bf16[16,1920]{1,0:T(8,128)(2,1)S(1)}, u32[]{:S(2)}, u32[]{:S(2)}) %collective-permute-start.14) | collective-permute-done | bytes 61472 | tf_op jit(solution)/shard_map/ppermute | solution.py:114
  41.8 1.4 %collective-permute-start.21 = (bf16[64,1408]{1,0:T(8,128)(2,1)S(1)}, bf16[64,1408]{1,0:T(8,128)(2,1)S(1)}, u32[]{:S(2)}, u32[]{:S(2)}) collective-permute-start(bf16[64,1408]{1,0:T(8,128)(2,1)S(1)} %get-tuple-element.44.refs_0_), channel_id=1, source_target_pairs={{0,2},{1,3},{2,0},{3,1},{4,6},{5,7},{6,4},{7,5},{8,10},{9,11},{10,... | collective-permute-start | bytes 540680 | tf_op jit(solution)/shard_map/ppermute | solution.py:108
  44.7 1.6 %hidden_beside.1 = (bf16[64,768]{1,0:T(8,128)(2,1)S(1)}, bf16[64,768]{1,0:T(8,128)(2,1)S(1)}, bf16[64,768]{1,0:T(8,128)(2,1)S(1)}) custom-call(bf16[4,16,1920]{2,1,0:T(8,128)(2,1)S(1)} %get-tuple-element.42.refs_0_.x, bf16[64,1024]{1,0:T(8,128)(2,1)S(1)} %hidden_across.3.refs_1_, bf16[1792,4608]{1,0:T(8,128)(2,1)S(1)} %bitcast.1, bf16[1792,4608]{1,0:T(8,128)(2,1)S(1)} %bitcast.3), custom_call_target="tpu_custom_call" | custom-call | tf_op jit(solution)/shard_map/hidden_beside/pallas_call | solution.py:94
  46.9 1.6 %hidden_own.1.mine = f32[64,2304]{1,0:T(8,128)S(1)} custom-call(bf16[4,16,1920]{2,1,0:T(8,128)(2,1)S(1)} %get-tuple-element.42.refs_0_.x, bf16[64,768]{1,0:T(8,128)(2,1)S(1)} %get-tuple-element.46.refs_1_, bf16[1792,4608]{1,0:T(8,128)(2,1)S(1)} %bitcast.1, bf16[1792,4608]{1,0:T(8,128)(2,1)S(1)} %bitcast.3), custom_call_target="tpu_custom_call" | custom-call | flops 550000000 | tf_op jit(solution)/shard_map/hidden_own/pallas_call | solution.py:94
  49.5 1.4 %collective-permute-start.24 = (bf16[64,640]{1,0:T(8,128)(2,1)S(1)}, bf16[64,640]{1,0:T(8,128)(2,1)S(1)}, u32[]{:S(2)}, u32[]{:S(2)}) collective-permute-start(bf16[64,640]{1,0:T(8,128)(2,1)S(1)} %get-tuple-element.50.refs_0_), channel_id=1, source_target_pairs={{0,2},{1,3},{2,0},{3,1},{4,6},{5,7},{6,4},{7,5},{8,10},{9,11},{10,... | collective-permute-start | bytes 245768 | tf_op jit(solution)/shard_map/ppermute | solution.py:108
  51.5 1.3 %collective-permute-start.22 = (bf16[64,512]{1,0:T(8,128)(2,1)S(1)}, bf16[64,512]{1,0:T(8,128)(2,1)S(1)}, u32[]{:S(2)}, u32[]{:S(2)}) collective-permute-start(bf16[64,512]{1,0:T(8,128)(2,1)S(1)} %activate.3.refs_1_), channel_id=1, source_target_pairs={{0,2},{1,3},{2,0},{3,1},{4,6},{5,7},{6,4},{7,5},{8,10},{9,11},{10,... | collective-permute-start | bytes 196616 | tf_op jit(solution)/shard_map/ppermute | solution.py:108
  53.5 1.2 %down.4.refs_2_ = f32[64,1792]{1,0:T(8,128)S(1)} custom-call(bf16[64,640]{1,0:T(8,128)(2,1)S(1)} %get-tuple-element.50.refs_0_, bf16[64,512]{1,0:T(8,128)(2,1)S(1)} %activate.3.refs_1_, bf16[64,640]{1,0:T(8,128)(2,1)S(1)} %collective-permute-done.25.refs_2_, bf16[4608,1792]{1,0:T(8,128)(2,1)S(1)} %bitcast.5), custom_call_target="tpu_custom_call" | custom-call | flops 50000000 | tf_op jit(solution)/shard_map/down/pallas_call | solution.py:94
  57.7 1.4 %collective-permute-start.28 = (bf16[16,1792]{1,0:T(8,128)(2,1)S(1)}, bf16[16,1792]{1,0:T(8,128)(2,1)S(1)}, u32[]{:S(2)}, u32[]{:S(2)}) collective-permute-start(bf16[16,1792]{1,0:T(8,128)(2,1)S(1)} %get-tuple-element.56), channel_id=1, source_target_pairs={{0,8},{4,12},{8,0},{12,4},{1,9},{5,13},{9,1},{13,5},{2,10},{6,14},... | collective-permute-start | bytes 172040 | tf_op jit(solution)/shard_map/ppermute | solution.py:114
  61.1 2.3 %collective-permute-done.28.refs_2_ = bf16[16,1792]{1,0:T(8,128)(2,1)S(1)} collective-permute-done((bf16[16,1792]{1,0:T(8,128)(2,1)S(1)}, bf16[16,1792]{1,0:T(8,128)(2,1)S(1)}, u32[]{:S(2)}, u32[]{:S(2)}) %collective-permute-start.28) | collective-permute-done | bytes 57376 | tf_op jit(solution)/shard_map/ppermute | solution.py:114
  63.9 2.0 %collective-permute-done.30.refs_4_ = bf16[16,1792]{1,0:T(8,128)(2,1)S(1)} collective-permute-done((bf16[16,1792]{1,0:T(8,128)(2,1)S(1)}, bf16[16,1792]{1,0:T(8,128)(2,1)S(1)}, u32[]{:S(2)}, u32[]{:S(2)}) %collective-permute-start.30) | collective-permute-done | bytes 57376 | tf_op jit(solution)/shard_map/ppermute | solution.py:114
  (90 shorter events, 20.8 us)
Async XLA Ops:
  3.3 6.4 %collective-permute-start = (bf16[4,16,256]{2,1,0:T(8,128)(2,1)S(1)}, bf16[4,16,256]{2,1,0:T(8,128)(2,1)S(1)}, u32[]{:S(2)}, u32[]{:S(2)}) collective-permute-start(bf16[4,16,256]{2,1,0:T(8,128)(2,1)S(1)} %get-tuple-element.33), channel_id=1, source_target_pairs={{0,8},{4,12},{8,0},{12,4},{1,9},{5,13},{9,1},{13,5},{2,10},{6,14},... | collective-permute-start | bytes 98312 | tf_op jit(solution)/shard_map/ppermute | solution.py:114
  7.4 5.7 %collective-permute-start.4 = (bf16[4,16,256]{2,1,0:T(8,128)(2,1)S(1)}, bf16[4,16,256]{2,1,0:T(8,128)(2,1)S(1)}, u32[]{:S(2)}, u32[]{:S(2)}) collective-permute-start(bf16[4,16,256]{2,1,0:T(8,128)(2,1)S(1)} %get-tuple-element.34), channel_id=1, source_target_pairs={{0,12},{4,8},{8,4},{12,0},{1,13},{5,9},{9,5},{13,1},{2,14},{6,10},... | collective-permute-start | bytes 98312 | tf_op jit(solution)/shard_map/ppermute | solution.py:114
  8.7 4.4 %collective-permute-start.5 = (bf16[4,16,256]{2,1,0:T(8,128)(2,1)S(1)}, bf16[4,16,256]{2,1,0:T(8,128)(2,1)S(1)}, u32[]{:S(2)}, u32[]{:S(2)}) collective-permute-start(bf16[4,16,256]{2,1,0:T(8,128)(2,1)S(1)} %get-tuple-element.35), channel_id=1, source_target_pairs={{0,4},{4,0},{8,12},{12,8},{1,5},{5,1},{9,13},{13,9},{2,6},{6,2},{1... | collective-permute-start | bytes 98312 | tf_op jit(solution)/shard_map/ppermute | solution.py:114
  9.6 5.6 %collective-permute-start.2 = (bf16[2,4,16,256]{3,2,1,0:T(8,128)(2,1)S(1)}, bf16[2,4,16,256]{3,2,1,0:T(8,128)(2,1)S(1)}, u32[]{:S(2)}, u32[]{:S(2)}) collective-permute-start(bf16[2,4,16,256]{3,2,1,0:T(8,128)(2,1)S(1)} %pack_early.1.refs_0_), channel_id=1, source_target_pairs={{0,2},{1,3},{2,0},{3,1},{4,6},{5,7},{6,4},{7,5},{8,10},{9,11},{10,... | collective-permute-start | bytes 196616 | tf_op jit(solution)/shard_map/ppermute | solution.py:108
  13.1 4.3 %collective-permute-start.7 = (bf16[2,4,16,256]{3,2,1,0:T(8,128)(2,1)S(1)}, bf16[2,4,16,256]{3,2,1,0:T(8,128)(2,1)S(1)}, u32[]{:S(2)}, u32[]{:S(2)}) collective-permute-start(bf16[2,4,16,256]{3,2,1,0:T(8,128)(2,1)S(1)} %pack_late.1.refs_4_), channel_id=1, source_target_pairs={{0,2},{1,3},{2,0},{3,1},{4,6},{5,7},{6,4},{7,5},{8,10},{9,11},{10,... | collective-permute-start | bytes 196616 | tf_op jit(solution)/shard_map/ppermute | solution.py:108
  14.7 2.8 %collective-permute-start.1 = (bf16[2,4,16,256]{3,2,1,0:T(8,128)(2,1)S(1)}, bf16[2,4,16,256]{3,2,1,0:T(8,128)(2,1)S(1)}, u32[]{:S(2)}, u32[]{:S(2)}) collective-permute-start(bf16[2,4,16,256]{3,2,1,0:T(8,128)(2,1)S(1)} %pack_early.1.refs_0_), channel_id=1, source_target_pairs={{0,1},{1,0},{2,3},{3,2},{4,5},{5,4},{6,7},{7,6},{8,9},{9,8},{10,11... | collective-permute-start | bytes 196616 | tf_op jit(solution)/shard_map/ppermute | solution.py:108
  14.7 2.8 %collective-permute-start.6 = (bf16[2,4,16,256]{3,2,1,0:T(8,128)(2,1)S(1)}, bf16[2,4,16,256]{3,2,1,0:T(8,128)(2,1)S(1)}, u32[]{:S(2)}, u32[]{:S(2)}) collective-permute-start(bf16[2,4,16,256]{3,2,1,0:T(8,128)(2,1)S(1)} %pack_late.1.refs_4_), channel_id=1, source_target_pairs={{0,1},{1,0},{2,3},{3,2},{4,5},{5,4},{6,7},{7,6},{8,9},{9,8},{10,11... | collective-permute-start | bytes 196616 | tf_op jit(solution)/shard_map/ppermute | solution.py:108
  15.2 2.3 %collective-permute-start.3 = (bf16[2,4,16,256]{3,2,1,0:T(8,128)(2,1)S(1)}, bf16[2,4,16,256]{3,2,1,0:T(8,128)(2,1)S(1)}, u32[]{:S(2)}, u32[]{:S(2)}) collective-permute-start(bf16[2,4,16,256]{3,2,1,0:T(8,128)(2,1)S(1)} %collective-permute-done.2.refs_2_), channel_id=1, source_target_pairs={{0,1},{1,0},{2,3},{3,2},{4,5},{5,4},{6,7},{7,6},{8,9},{9,8},{10,11... | collective-permute-start | bytes 196616 | tf_op jit(solution)/shard_map/ppermute | solution.py:108
  21.6 5.8 %collective-permute-start.9 = (bf16[16,1792]{1,0:T(8,128)(2,1)S(1)}, bf16[16,1792]{1,0:T(8,128)(2,1)S(1)}, u32[]{:S(2)}, u32[]{:S(2)}) collective-permute-start(bf16[16,1792]{1,0:T(8,128)(2,1)S(1)} %get-tuple-element.37), channel_id=1, source_target_pairs={{0,8},{4,12},{8,0},{12,4},{1,9},{5,13},{9,1},{13,5},{2,10},{6,14},... | collective-permute-start | bytes 172040 | tf_op jit(solution)/shard_map/ppermute | solution.py:114
  22.9 5.0 %collective-permute-start.10 = (bf16[16,1792]{1,0:T(8,128)(2,1)S(1)}, bf16[16,1792]{1,0:T(8,128)(2,1)S(1)}, u32[]{:S(2)}, u32[]{:S(2)}) collective-permute-start(bf16[16,1792]{1,0:T(8,128)(2,1)S(1)} %get-tuple-element.38), channel_id=1, source_target_pairs={{0,12},{4,0},{8,4},{12,8},{1,13},{5,1},{9,5},{13,9},{2,14},{6,2},{... | collective-permute-start | bytes 172040 | tf_op jit(solution)/shard_map/ppermute | solution.py:114
  24.0 6.0 %collective-permute-start.11 = (bf16[16,1792]{1,0:T(8,128)(2,1)S(1)}, bf16[16,1792]{1,0:T(8,128)(2,1)S(1)}, u32[]{:S(2)}, u32[]{:S(2)}) collective-permute-start(bf16[16,1792]{1,0:T(8,128)(2,1)S(1)} %get-tuple-element.39), channel_id=1, source_target_pairs={{0,4},{4,8},{8,12},{12,0},{1,5},{5,9},{9,13},{13,1},{2,6},{6,10},{... | collective-permute-start | bytes 172040 | tf_op jit(solution)/shard_map/ppermute | solution.py:114
  30.1 5.7 %collective-permute-start.12 = (bf16[16,1920]{1,0:T(8,128)(2,1)S(1)}, bf16[16,1920]{1,0:T(8,128)(2,1)S(1)}, u32[]{:S(2)}, u32[]{:S(2)}) collective-permute-start(bf16[16,1920]{1,0:T(8,128)(2,1)S(1)} %get-tuple-element.41.refs_0_), channel_id=1, source_target_pairs={{0,8},{4,12},{8,0},{12,4},{1,9},{5,13},{9,1},{13,5},{2,10},{6,14},... | collective-permute-start | bytes 184328 | tf_op jit(solution)/shard_map/ppermute | solution.py:114
  31.6 5.0 %collective-permute-start.13 = (bf16[16,1920]{1,0:T(8,128)(2,1)S(1)}, bf16[16,1920]{1,0:T(8,128)(2,1)S(1)}, u32[]{:S(2)}, u32[]{:S(2)}) collective-permute-start(bf16[16,1920]{1,0:T(8,128)(2,1)S(1)} %get-tuple-element.41.refs_0_), channel_id=1, source_target_pairs={{0,12},{4,0},{8,4},{12,8},{1,13},{5,1},{9,5},{13,9},{2,14},{6,2},{... | collective-permute-start | bytes 184328 | tf_op jit(solution)/shard_map/ppermute | solution.py:114
  32.3 6.0 %collective-permute-start.14 = (bf16[16,1920]{1,0:T(8,128)(2,1)S(1)}, bf16[16,1920]{1,0:T(8,128)(2,1)S(1)}, u32[]{:S(2)}, u32[]{:S(2)}) collective-permute-start(bf16[16,1920]{1,0:T(8,128)(2,1)S(1)} %get-tuple-element.41.refs_0_), channel_id=1, source_target_pairs={{0,4},{4,8},{8,12},{12,0},{1,5},{5,9},{9,13},{13,1},{2,6},{6,10},{... | collective-permute-start | bytes 184328 | tf_op jit(solution)/shard_map/ppermute | solution.py:114
  40.2 2.9 %collective-permute-start.15 = (bf16[64,1024]{1,0:T(8,128)(2,1)S(1)}, bf16[64,1024]{1,0:T(8,128)(2,1)S(1)}, u32[]{:S(2)}, u32[]{:S(2)}) collective-permute-start(bf16[64,1024]{1,0:T(8,128)(2,1)S(1)} %hidden_diagonal.3.refs_0_), channel_id=1, source_target_pairs={{0,1},{1,0},{2,3},{3,2},{4,5},{5,4},{6,7},{7,6},{8,9},{9,8},{10,11... | collective-permute-start | bytes 393224 | tf_op jit(solution)/shard_map/ppermute | solution.py:108
  41.8 7.5 %collective-permute-start.21 = (bf16[64,1408]{1,0:T(8,128)(2,1)S(1)}, bf16[64,1408]{1,0:T(8,128)(2,1)S(1)}, u32[]{:S(2)}, u32[]{:S(2)}) collective-permute-start(bf16[64,1408]{1,0:T(8,128)(2,1)S(1)} %get-tuple-element.44.refs_0_), channel_id=1, source_target_pairs={{0,2},{1,3},{2,0},{3,1},{4,6},{5,7},{6,4},{7,5},{8,10},{9,11},{10,... | collective-permute-start | bytes 540680 | tf_op jit(solution)/shard_map/ppermute | solution.py:108
  43.9 7.3 %collective-permute-start.20 = (bf16[64,1024]{1,0:T(8,128)(2,1)S(1)}, bf16[64,1024]{1,0:T(8,128)(2,1)S(1)}, u32[]{:S(2)}, u32[]{:S(2)}) collective-permute-start(bf16[64,1024]{1,0:T(8,128)(2,1)S(1)} %hidden_across.3.refs_1_), channel_id=1, source_target_pairs={{0,2},{1,3},{2,0},{3,1},{4,6},{5,7},{6,4},{7,5},{8,10},{9,11},{10,... | collective-permute-start | bytes 393224 | tf_op jit(solution)/shard_map/ppermute | solution.py:108
  46.3 2.2 %collective-permute-start.17 = (bf16[64,768]{1,0:T(8,128)(2,1)S(1)}, bf16[64,768]{1,0:T(8,128)(2,1)S(1)}, u32[]{:S(2)}, u32[]{:S(2)}) collective-permute-start(bf16[64,768]{1,0:T(8,128)(2,1)S(1)} %get-tuple-element.46.refs_1_), channel_id=1, source_target_pairs={{0,1},{1,0},{2,3},{3,2},{4,5},{5,4},{6,7},{7,6},{8,9},{9,8},{10,11... | collective-permute-start | bytes 294920 | tf_op jit(solution)/shard_map/ppermute | solution.py:108
  49.5 5.3 %collective-permute-start.24 = (bf16[64,640]{1,0:T(8,128)(2,1)S(1)}, bf16[64,640]{1,0:T(8,128)(2,1)S(1)}, u32[]{:S(2)}, u32[]{:S(2)}) collective-permute-start(bf16[64,640]{1,0:T(8,128)(2,1)S(1)} %get-tuple-element.50.refs_0_), channel_id=1, source_target_pairs={{0,2},{1,3},{2,0},{3,1},{4,6},{5,7},{6,4},{7,5},{8,10},{9,11},{10,... | collective-permute-start | bytes 245768 | tf_op jit(solution)/shard_map/ppermute | solution.py:108
  51.4 3.5 %collective-permute-start.23 = (bf16[64,512]{1,0:T(8,128)(2,1)S(1)}, bf16[64,512]{1,0:T(8,128)(2,1)S(1)}, u32[]{:S(2)}, u32[]{:S(2)}) collective-permute-start(bf16[64,512]{1,0:T(8,128)(2,1)S(1)} %activate.3.refs_1_), channel_id=1, source_target_pairs={{0,1},{1,0},{2,3},{3,2},{4,5},{5,4},{6,7},{7,6},{8,9},{9,8},{10,11... | collective-permute-start | bytes 196616 | tf_op jit(solution)/shard_map/ppermute | solution.py:108
  51.5 4.4 %collective-permute-start.22 = (bf16[64,512]{1,0:T(8,128)(2,1)S(1)}, bf16[64,512]{1,0:T(8,128)(2,1)S(1)}, u32[]{:S(2)}, u32[]{:S(2)}) collective-permute-start(bf16[64,512]{1,0:T(8,128)(2,1)S(1)} %activate.3.refs_1_), channel_id=1, source_target_pairs={{0,2},{1,3},{2,0},{3,1},{4,6},{5,7},{6,4},{7,5},{8,10},{9,11},{10,... | collective-permute-start | bytes 196616 | tf_op jit(solution)/shard_map/ppermute | solution.py:108
  57.7 5.8 %collective-permute-start.28 = (bf16[16,1792]{1,0:T(8,128)(2,1)S(1)}, bf16[16,1792]{1,0:T(8,128)(2,1)S(1)}, u32[]{:S(2)}, u32[]{:S(2)}) collective-permute-start(bf16[16,1792]{1,0:T(8,128)(2,1)S(1)} %get-tuple-element.56), channel_id=1, source_target_pairs={{0,8},{4,12},{8,0},{12,4},{1,9},{5,13},{9,1},{13,5},{2,10},{6,14},... | collective-permute-start | bytes 172040 | tf_op jit(solution)/shard_map/ppermute | solution.py:114
  59.1 4.8 %collective-permute-start.29 = (bf16[16,1792]{1,0:T(8,128)(2,1)S(1)}, bf16[16,1792]{1,0:T(8,128)(2,1)S(1)}, u32[]{:S(2)}, u32[]{:S(2)}) collective-permute-start(bf16[16,1792]{1,0:T(8,128)(2,1)S(1)} %get-tuple-element.57), channel_id=1, source_target_pairs={{0,12},{4,0},{8,4},{12,8},{1,13},{5,1},{9,5},{13,9},{2,14},{6,2},{... | collective-permute-start | bytes 172040 | tf_op jit(solution)/shard_map/ppermute | solution.py:114
  59.9 6.0 %collective-permute-start.30 = (bf16[16,1792]{1,0:T(8,128)(2,1)S(1)}, bf16[16,1792]{1,0:T(8,128)(2,1)S(1)}, u32[]{:S(2)}, u32[]{:S(2)}) collective-permute-start(bf16[16,1792]{1,0:T(8,128)(2,1)S(1)} %get-tuple-element.58), channel_id=1, source_target_pairs={{0,4},{4,8},{8,12},{12,0},{1,5},{5,9},{9,13},{13,1},{2,6},{6,10},{... | collective-permute-start | bytes 172040 | tf_op jit(solution)/shard_map/ppermute | solution.py:114
  (22 other events, 301.1 us)
